TPU v7x, 32 devices: a whole 2x2x4 slice. The times are simulated.
32 devices in a mesh: dp: 4 (over y, x), brick: 8 (over z, core).
Axes of the slice: x: 2, y: 2, z: 4, core: 2. Of those that a mesh axis runs over, the one named last changes fastest.
Arguments:
- features: bfloat16 [4, 64, 512, 64], P('dp', 'brick'), may hold values from -6 to 6
- occupancy: int32 [4, 64, 512], P('dp', 'brick'), may hold values 0 or 1
- neighbours: int32 [4, 64, 27], P('dp', 'brick'), may hold values from -1 to 63, as said below
- owners: int32 [4, 64], P('dp', 'brick'), may hold values from 0 to 63, as said below
- w_conv: bfloat16 [3, 3, 3, 64, 64], replicated, may hold values from -0.15625 to 0.15625
- w_down: bfloat16 [2, 2, 2, 64, 128], replicated, may hold values from -0.25 to 0.25
- w_point: bfloat16 [128, 256], replicated, may hold values from -0.5 to 0.5
- cotangent: bfloat16 [4, 64, 64, 256], P('dp', 'brick'), may hold values from -0.046875 to 0.046875
Outputs:
- grad_w_conv: float32 [3, 3, 3, 64, 64], replicated
- grad_w_down: float32 [2, 2, 2, 64, 128], replicated
- grad_w_point: float32 [128, 256], replicated
Inputs may be any that keep to these rules, and one draw needn't show every extreme that they name: `neighbours`: bricks of a scene form a lattice of 16 x 4 x 1 bricks, 8 consecutive ids a device; an entry names the lattice neighbour at its column's offset or is -1; column 13 is the brick itself. Columns with first offset 0 name bricks of the same device, offset -1 of the same or the previous device, offset +1 of the same or the next. `owners`: within a scene a permutation of the coarse slots; a slot's device is slot // 8. A device hands exactly 1 bricks to each device it hands any to.
All inputs are finite; a program needn't handle non-finite values. No bound on the sum of `occupancy` on one device may be relied on, other than what follows from the above.
Results may differ from a plain program's by a relative error of at most 0.012.
Values may be sent and summed in bfloat16 or wider, within the bound.
No kernel may reach another device: no remote copies, remote signals or barrier semaphores. Data moves between devices by JAX's collectives and lax.ppermute only.
A program may use at most 64 MiB of HBM per device.

v0:
```python
import jax
import jax.numpy as jnp
from jax import lax
from jax.sharding import PartitionSpec as P

SPANS = ((7, 8), (0, 8), (0, 1))


def extended(shard, sides, width):
    for axis, dim in sides:
        peers, length = (lax.axis_size(axis), shard.shape[dim])
        up = [(i, (i + 1) % peers) for i in range(peers - 1)]
        down = [(j, i) for i, j in up]
        last = lax.slice_in_dim(shard, length - width, length, axis=dim)
        initial = lax.slice_in_dim(shard, 0, width, axis=dim)
        before = lax.ppermute(last, axis, up)
        after = lax.ppermute(initial, axis, down)
        shard = jnp.concatenate([before, shard, after], axis=dim)
    return shard


def assemble(pools, indices):
    planes = []
    for a in range(3):
        row_parts = []
        for b in range(3):
            col_parts = []
            for c in range(3):
                window_part = pools[a][
                    :, :, SPANS[b][0] : SPANS[b][1], SPANS[c][0] : SPANS[c][1], :
                ]
                col_parts.append(
                    jnp.take(window_part, indices[a][:, 9 * a + 3 * b + c], axis=0, mode="clip")
                )
            row_parts.append(jnp.concatenate(col_parts, axis=3))
        planes.append(jnp.concatenate(row_parts, axis=2))
    return jnp.concatenate(planes, axis=1)


def silu_slope(signal):
    gate_value = jax.nn.sigmoid(signal)
    return gate_value * (1.0 + signal * (1.0 - gate_value))


def point_layer(rows_in, cot_rows, w_point):
    brick_count = rows_in.shape[0]
    row_block = rows_in.reshape(-1, w_point.shape[0])
    point_act = jnp.dot(row_block, w_point, preferred_element_type=jnp.float32)
    grad_point = (
        cot_rows.reshape(point_act.shape).astype(jnp.float32) * silu_slope(point_act)
    ).astype(jnp.bfloat16)
    grad_weight = lax.dot_general(
        row_block, grad_point, (((0,), (0,)), ((), ())), preferred_element_type=jnp.float32
    )
    grad_rows = lax.dot_general(
        grad_point, w_point, (((1,), (1,)), ((), ())), preferred_element_type=jnp.float32
    )
    return (grad_rows.astype(jnp.bfloat16).reshape(brick_count, -1), grad_weight)


def shards(features, occupancy, neighbours, owners, w_conv, w_down, w_point, cotangent):
    brick_count = features.shape[1]
    in_width = features.shape[3]
    brick_devices = lax.axis_size("brick")
    device_pos = lax.axis_index("brick")
    bricks = features[0].reshape(brick_count, 8, 8, 8, in_width)
    link_table = neighbours[0]
    linked = link_table >= 0
    local_ids = link_table - device_pos * brick_count
    zero_brick = jnp.zeros((1, 8, 8, 8, in_width), bricks.dtype)
    beside_all = extended(bricks, (("brick", 0),), brick_count)
    brick_pool = jnp.concatenate([beside_all, zero_brick], axis=0)
    pool_index = jnp.where(linked, local_ids + brick_count, 3 * brick_count)
    padded = assemble(
        (brick_pool[:, 7:8], brick_pool, brick_pool[:, 0:1]), (pool_index, pool_index, pool_index)
    )
    pre_act = lax.conv_general_dilated(
        padded,
        w_conv,
        (1, 1, 1),
        "VALID",
        dimension_numbers=("NDHWC", "DHWIO", "NDHWC"),
        preferred_element_type=jnp.float32,
    )
    occupied = occupancy[0].reshape(brick_count, 8, 8, 8, 1).astype(jnp.float32)
    hidden = (jax.nn.silu(pre_act) * occupied).astype(jnp.bfloat16)
    grouped = hidden.reshape(brick_count, 4, 2, 4, 2, 4, 2, in_width)
    down_act = jnp.einsum(
        "bpiqjrkc,ijkcd->bpqrd", grouped, w_down, preferred_element_type=jnp.float32
    )
    coarse = jax.nn.silu(down_act).astype(jnp.bfloat16).reshape(brick_count, -1)
    target_dev = owners[0] // brick_count
    recv_slot = owners[0] % brick_count
    capacity = max(1, brick_count // brick_devices)
    dest_hits = (target_dev[:, None] == jnp.arange(brick_devices, dtype=jnp.int32)[None, :]).astype(
        jnp.int32
    )
    earlier_hits = jnp.cumsum(dest_hits, axis=0) - dest_hits
    rank_in = jnp.sum(earlier_hits * dest_hits, axis=1)
    position = target_dev * capacity + rank_in
    slot_out = jnp.full((brick_devices * capacity,), -1, jnp.int32).at[position].set(recv_slot)
    arrived = lax.all_to_all(slot_out, "brick", split_axis=0, concat_axis=0, tiled=True)
    present = arrived >= 0
    safe_slots = jnp.where(present, arrived, 0)
    cot_flat = cotangent[0].reshape(brick_count, -1)
    request = jnp.where(
        present[:, None], jnp.take(cot_flat, safe_slots, axis=0), jnp.zeros((), jnp.bfloat16)
    )
    fetched = lax.all_to_all(request, "brick", split_axis=0, concat_axis=0, tiled=True)
    local_cot = jnp.take(fetched, position, axis=0)
    grad_coarse, grad_w_point = point_layer(coarse, local_cot, w_point)
    grad_down = (
        grad_coarse.reshape(down_act.shape).astype(jnp.float32) * silu_slope(down_act)
    ).astype(jnp.bfloat16)
    grad_w_down = jnp.einsum(
        "bpiqjrkc,bpqrd->ijkcd", grouped, grad_down, preferred_element_type=jnp.float32
    )
    grad_hidden = jnp.einsum(
        "bpqrd,ijkcd->bpiqjrkc", grad_down, w_down, preferred_element_type=jnp.float32
    )
    grad_hidden = grad_hidden.reshape(brick_count, 8, 8, 8, in_width)
    grad_pre = (grad_hidden * occupied * silu_slope(pre_act)).astype(jnp.bfloat16)
    flat_grad = grad_pre.reshape(-1, in_width)
    term_list = []
    for a in range(3):
        for b in range(3):
            for c in range(3):
                window_part = padded[:, a : a + 8, b : b + 8, c : c + 8, :].reshape(-1, in_width)
                term_list.append(
                    lax.dot_general(
                        window_part,
                        flat_grad,
                        (((0,), (0,)), ((), ())),
                        preferred_element_type=jnp.float32,
                    )
                )
    grad_w_conv = jnp.stack(term_list).reshape(3, 3, 3, in_width, in_width)
    summed = lax.psum((grad_w_conv, grad_w_down, grad_w_point), ("dp", "brick"))
    return (summed[0], summed[1], summed[2])


def solution(mesh):
    in_specs = (
        P("dp", "brick", None, None),
        P("dp", "brick", None),
        P("dp", "brick", None),
        P("dp", "brick"),
        P(),
        P(),
        P(),
        P("dp", "brick", None, None),
    )
    out_specs = (P(), P(), P())
    return jax.shard_map(shards, mesh=mesh, in_specs=in_specs, out_specs=out_specs, check_vma=False)
```

profile of v0, /device:TPU:0, one launch (start us, length us, event | category | flops | bytes accessed | tf_op | source)
XLA Modules:
  0.0 303.6 jit_solution(334839375026622639)
XLA Ops:
  7.2 1.9 copy.277
  9.1 3.4 %collective-permute-start = (bf16[8,8,8,8,64]{4,0,3,2,1:T(8,128)(2,1)S(1)}, bf16[8,8,8,8,64]{4,0,3,2,1:T(8,128)(2,1)}, u32[]{:S(2)}, u32[]{:S(2)}) collective-permute-start(bf16[8,8,8,8,64]{4,0,3,2,1:T(8,128)(2,1)S(1)} %bitcast.493), channel_id=1, source_target_pairs={{0,1},{1,2},{2,3},{3,4},{4,5},{5,6},{6,7},{8,9},{9,10},{10,11},{11... | collective-permute-start | bytes 1572872 | tf_op jit(solution)/shard_map/ppermute | solution.py:16
  12.5 1.3 collective-permute-start.1
  16.7 7.2 %all-to-all-start = ((s32[8,1,1]{2,1,0:T(1,128)}), s32[8,1,1]{2,1,0:T(1,128)S(1)}, u32[]{:S(2)}, u32[]{:S(2)}) async-start(s32[8,1,1]{2,1,0:T(1,128)} %copy.306), calls=%async_computation | async-start | bytes 8192 | tf_op jit(solution)/shard_map/all_to_all | solution.py:102
  30.9 1.6 all-to-all-done
  33.3 0.7 gather_fusion.27
  34.7 0.8 reduce.55
  35.5 0.9 reshape.650
  36.4 3.6 %all-to-all-start.1 = ((bf16[8,2,8192]{2,1,0:T(2,128)(2,1)}), bf16[8,2,8192]{2,1,0:T(2,128)(2,1)S(1)}, u32[]{:S(2)}, u32[]{:S(2)}) async-start(bf16[8,2,8192]{2,1,0:T(2,128)(2,1)} %reshape.650), calls=%async_computation.1 | async-start | bytes 524288 | tf_op jit(solution)/shard_map/all_to_all | solution.py:109
  40.0 0.8 copy.365
  43.4 6.3 %all-to-all-done.1 = bf16[8,2,8192]{2,1,0:T(2,128)(2,1)S(1)} async-done(((bf16[8,2,8192]{2,1,0:T(2,128)(2,1)}), bf16[8,2,8192]{2,1,0:T(2,128)(2,1)S(1)}, u32[]{:S(2)}, u32[]{:S(2)}) %all-to-all-start.1) | async-done | bytes 262176 | tf_op jit(solution)/shard_map/all_to_all | solution.py:109
  50.3 0.7 gather_fusion.28
  51.1 0.9 reshape.176
  52.0 2.6 maximum_maximum_fusion
  54.7 0.7 slice_bitcast_fusion.13
  56.8 0.7 slice_bitcast_fusion.8
  57.6 3.0 copy.296
  60.6 0.9 copy.297
  61.5 1.6 gather_fusion.14
  63.2 0.9 copy.294
  64.1 1.6 gather_fusion.12
  65.7 0.9 copy.300
  67.2 0.9 copy.292
  69.3 0.9 copy.288
  71.3 0.9 copy.304
  74.6 0.7 copy.419
  75.3 0.9 copy.316
  77.5 0.9 copy.314
  79.7 0.9 copy.310
  84.0 0.7 copy.415
  84.7 2.8 gather_fusion.13
  87.5 1.2 copy.299
  89.5 2.1 gather_fusion.7
  91.5 1.3 copy.429
  92.9 1.5 copy.284
  94.3 2.1 gather_fusion.5
  96.4 1.3 copy.430
  97.7 1.5 copy.280
  99.2 2.1 gather_fusion.3
  101.3 1.3 copy.431
  103.2 1.5 gather_fusion.1
  105.3 0.9 copy.282
  106.2 2.3 gather_fusion.4
  108.6 1.7 copy.420
  110.3 2.0 gather_fusion.8
  112.3 2.0 gather_fusion.18
  114.2 1.9 gather_fusion.20
  116.2 2.0 gather_fusion.24
  118.1 2.0 gather_fusion.26
  120.1 2.0 gather_fusion.6
  122.1 2.0 gather_fusion.2
  124.0 2.0 gather_fusion
  126.1 5.8 %maximum_maximum_fusion.2 = bf16[8,9,10,10,64]{4,0,3,2,1:T(8,128)(2,1)S(1)} fusion(bf16[8,1,1,1,64]{4,0,3,2,1:T(8,128)(2,1)} %bitcast.594, bf16[8,1,1,8,64]{4,0,3,2,1:T(8,128)(2,1)} %bitcast.564, bf16[8,1,1,1,64]{4,0,3,2,1:T(8,128)(2,1)} %bitcast.592, bf16[8,1,8,1,64]{4,0,3,2,1:T(8,128)(2,1)} %bitcast.566, bf16[8,1,8,8,64]{4,0,3,2,1:T(8,128)(2,1)} %bitcast.534, ...), kind=kLoop, calls=%fused_computation.89 | loop fusion | flops 7833600 | bytes 1843200 | tf_op jit(solution)/shard_map/concatenate | solution.py:37
  132.2 4.4 %multiply_convert_fusion.1 = (bf16[8,8,8,8,64]{4,0,3,2,1:T(8,128)(2,1)S(1)}, f32[8,8,8,8,64]{4,0,3,2,1:T(8,128)S(1)}) fusion(f32[8,8,8,8]{0,3,2,1:T(8,128)S(1)} %bitcast.531, bf16[3,3,3,64,64]{4,3,2,1,0:T(8,128)(2,1)S(1)} %copy-done, bf16[8,1,1,1,64]{4,0,3,2,1:T(8,128)(2,1)S(1)} %bitcast.595, bf16[8,1,1,8,64]{4,0,3,2,1:T(8,128)(2,1)S(1)} %bitcast.565, ...), kind=kOutput, calls=%fused_computation.32 | convolution fusion | flops 920854528 | bytes 2834432 | tf_op jit(solution)/shard_map/conv_general_dilated | solution.py:77
  139.3 2.3 maximum_maximum_fusion.1
  142.0 0.9 fusion.111
  142.9 0.7 copy.414
  143.9 1.2 multiply_convert_fusion
  151.3 0.9 fusion.75
  152.8 1.0 fusion.73
  160.1 0.9 copy-done.3
  161.0 131.2 %all-reduce.3.cloned.1.call-done = (f32[3,3,3,64,64]{4,3,2,1,0:T(8,128)}, f32[2,2,2,64,128]{4,3,0,1,2:T(8,128)}, f32[128,256]{1,0:T(8,128)}) async-done(((f32[3,3,3,64,64]{4,3,2,1,0:T(8,128)}, f32[2,2,2,64,128]{4,3,0,1,2:T(8,128)}, f32[128,256]{1,0:T(8,128)}), (f32[3,3,3,64,64]{4,3,2,1,0:T(8,128)}, f32[2,2,2,64,128]{4,3,0,1,2:T(8,128)}, f32[128,256]{1,0:T(8,128)})) %all-reduce.3.cloned.1.call-update) | async-done | bytes 835600 | tf_op jit(solution)/shard_map/psum | solution.py:138
  292.3 1.7 copy.329
  294.0 2.2 copy.463
  (174 shorter events, 46.6 us)
Async XLA Ops:
  7.2 124.8 %copy-start = (bf16[3,3,3,64,64]{4,3,2,1,0:T(8,128)(2,1)S(1)}, bf16[3,3,3,64,64]{4,3,2,1,0:T(8,128)(2,1)}, u32[]{:S(2)}) copy-start(bf16[3,3,3,64,64]{4,3,2,1,0:T(8,128)(2,1)} %param.14) | copy-start | bytes 663556
  7.2 23.6 %copy-start.7 = (bf16[1,8,64,256]{3,2,1,0:T(8,128)(2,1)S(1)}, bf16[1,8,64,256]{3,2,1,0:T(8,128)(2,1)}, u32[]{:S(2)}) copy-start(bf16[1,8,64,256]{3,2,1,0:T(8,128)(2,1)} %param.17) | copy-start | bytes 786436
  9.1 42.9 %collective-permute-start = (bf16[8,8,8,8,64]{4,0,3,2,1:T(8,128)(2,1)S(1)}, bf16[8,8,8,8,64]{4,0,3,2,1:T(8,128)(2,1)}, u32[]{:S(2)}, u32[]{:S(2)}) collective-permute-start(bf16[8,8,8,8,64]{4,0,3,2,1:T(8,128)(2,1)S(1)} %bitcast.493), channel_id=1, source_target_pairs={{0,1},{1,2},{2,3},{3,4},{4,5},{5,6},{6,7},{8,9},{9,10},{10,11},{11... | collective-permute-start | bytes 1572872 | tf_op jit(solution)/shard_map/ppermute | solution.py:16
  12.5 39.5 %collective-permute-start.1 = (bf16[8,8,8,8,64]{4,0,3,2,1:T(8,128)(2,1)S(1)}, bf16[8,8,8,8,64]{4,0,3,2,1:T(8,128)(2,1)}, u32[]{:S(2)}, u32[]{:S(2)}) collective-permute-start(bf16[8,8,8,8,64]{4,0,3,2,1:T(8,128)(2,1)S(1)} %bitcast.494), channel_id=1, source_target_pairs={{1,0},{2,1},{3,2},{4,3},{5,4},{6,5},{7,6},{9,8},{10,9},{11,10},{12... | collective-permute-start | bytes 1572872 | tf_op jit(solution)/shard_map/ppermute | solution.py:17
  16.7 15.8 %all-to-all-start = ((s32[8,1,1]{2,1,0:T(1,128)}), s32[8,1,1]{2,1,0:T(1,128)S(1)}, u32[]{:S(2)}, u32[]{:S(2)}) async-start(s32[8,1,1]{2,1,0:T(1,128)} %copy.306), calls=%async_computation | async-start | bytes 8192 | tf_op jit(solution)/shard_map/all_to_all | solution.py:102
  33.3 6.7 %copy-start.23 = (s32[1,8,512]{2,1,0:T(8,128)S(1)}, s32[1,8,512]{2,1,0:T(8,128)}, u32[]{:S(2)}) copy-start(s32[1,8,512]{2,1,0:T(8,128)} %param.11) | copy-start | bytes 49156
  36.4 13.3 %all-to-all-start.1 = ((bf16[8,2,8192]{2,1,0:T(2,128)(2,1)}), bf16[8,2,8192]{2,1,0:T(2,128)(2,1)S(1)}, u32[]{:S(2)}, u32[]{:S(2)}) async-start(bf16[8,2,8192]{2,1,0:T(2,128)(2,1)} %reshape.650), calls=%async_computation.1 | async-start | bytes 524288 | tf_op jit(solution)/shard_map/all_to_all | solution.py:109
  39.9 252.3 %all-reduce.3.cloned.1.call-start = ((), (), s32[]{:S(2)}) async-start(), calls=%async_computation.2 | async-start | bytes 2555904 | tf_op jit(solution)/shard_map/psum | solution.py:138
  67.2 14.6 %copy-start.9 = (bf16[25,8,64]{2,0,1:T(8,128)(2,1)S(1)}, bf16[25,8,64]{2,0,1:T(8,128)(2,1)}, u32[]{:S(2)}) copy-start(bf16[25,8,64]{2,0,1:T(8,128)(2,1)} %get-tuple-element.52) | copy-start | bytes 76804
  87.5 1.3 copy-start.8
  108.6 23.4 %copy-start.1 = (bf16[8,8,8,64]{3,0,2,1:T(8,128)(2,1)S(1)}, bf16[8,8,8,64]{3,0,2,1:T(8,128)(2,1)}, u32[]{:S(2)}) copy-start(bf16[8,8,8,64]{3,0,2,1:T(8,128)(2,1)} %copy.419) | copy-start | bytes 196612
  108.6 23.4 %copy-start.2 = (f32[1,8,512]{1,2,0:T(8,128)S(1)}, f32[1,8,512]{1,2,0:T(8,128)}, u32[]{:S(2)}) copy-start(f32[1,8,512]{1,2,0:T(8,128)} %copy.365) | copy-start | bytes 49156
  108.6 23.4 %copy-start.4 = (bf16[8,8,8,64]{3,0,2,1:T(8,128)(2,1)S(1)}, bf16[8,8,8,64]{3,0,2,1:T(8,128)(2,1)}, u32[]{:S(2)}) copy-start(bf16[8,8,8,64]{3,0,2,1:T(8,128)(2,1)} %copy.415) | copy-start | bytes 196612
  108.6 23.4 %copy-start.10 = (bf16[8,8,64]{2,0,1:T(8,128)(2,1)S(1)}, bf16[8,8,64]{2,0,1:T(8,128)(2,1)}, u32[]{:S(2)}) copy-start(bf16[8,8,64]{2,0,1:T(8,128)(2,1)} %copy.427) | copy-start | bytes 24580
  108.6 23.5 %copy-start.11 = (bf16[8,8,64]{2,0,1:T(8,128)(2,1)S(1)}, bf16[8,8,64]{2,0,1:T(8,128)(2,1)}, u32[]{:S(2)}) copy-start(bf16[8,8,64]{2,0,1:T(8,128)(2,1)} %copy.428) | copy-start | bytes 24580
  108.6 23.5 %copy-start.14 = (bf16[8,8,64]{2,0,1:T(8,128)(2,1)S(1)}, bf16[8,8,64]{2,0,1:T(8,128)(2,1)}, u32[]{:S(2)}) copy-start(bf16[8,8,64]{2,0,1:T(8,128)(2,1)} %copy.421) | copy-start | bytes 24580
  108.6 23.5 %copy-start.15 = (bf16[8,8,64]{2,0,1:T(8,128)(2,1)S(1)}, bf16[8,8,64]{2,0,1:T(8,128)(2,1)}, u32[]{:S(2)}) copy-start(bf16[8,8,64]{2,0,1:T(8,128)(2,1)} %copy.422) | copy-start | bytes 24580
  126.0 6.0 %copy-start.5 = (bf16[8,8,8,64]{3,0,2,1:T(8,128)(2,1)S(1)}, bf16[8,8,8,64]{3,0,2,1:T(8,128)(2,1)}, u32[]{:S(2)}) copy-start(bf16[8,8,8,64]{3,0,2,1:T(8,128)(2,1)} %copy.420) | copy-start | bytes 196612
  126.0 6.1 %copy-start.16 = (bf16[8,8,64]{2,0,1:T(8,128)(2,1)S(1)}, bf16[8,8,64]{2,0,1:T(8,128)(2,1)}, u32[]{:S(2)}) copy-start(bf16[8,8,64]{2,0,1:T(8,128)(2,1)} %copy.423) | copy-start | bytes 24580
  126.0 6.1 %copy-start.17 = (bf16[8,8,64]{2,0,1:T(8,128)(2,1)S(1)}, bf16[8,8,64]{2,0,1:T(8,128)(2,1)}, u32[]{:S(2)}) copy-start(bf16[8,8,64]{2,0,1:T(8,128)(2,1)} %copy.424) | copy-start | bytes 24580
  126.0 6.1 %copy-start.18 = (bf16[8,8,64]{2,0,1:T(8,128)(2,1)S(1)}, bf16[8,8,64]{2,0,1:T(8,128)(2,1)}, u32[]{:S(2)}) copy-start(bf16[8,8,64]{2,0,1:T(8,128)(2,1)} %copy.429) | copy-start | bytes 24580
  126.0 6.1 %copy-start.19 = (bf16[8,8,64]{2,0,1:T(8,128)(2,1)S(1)}, bf16[8,8,64]{2,0,1:T(8,128)(2,1)}, u32[]{:S(2)}) copy-start(bf16[8,8,64]{2,0,1:T(8,128)(2,1)} %copy.430) | copy-start | bytes 24580
  126.0 6.1 %copy-start.20 = (bf16[8,8,64]{2,0,1:T(8,128)(2,1)S(1)}, bf16[8,8,64]{2,0,1:T(8,128)(2,1)}, u32[]{:S(2)}) copy-start(bf16[8,8,64]{2,0,1:T(8,128)(2,1)} %copy.431) | copy-start | bytes 24580
  126.0 6.1 %copy-start.21 = (bf16[8,8,64]{2,0,1:T(8,128)(2,1)S(1)}, bf16[8,8,64]{2,0,1:T(8,128)(2,1)}, u32[]{:S(2)}) copy-start(bf16[8,8,64]{2,0,1:T(8,128)(2,1)} %copy.432) | copy-start | bytes 24580
  126.0 6.1 %copy-start.24 = (bf16[8,64]{1,0:T(8,128)(2,1)S(1)}, bf16[8,64]{1,0:T(8,128)(2,1)}, u32[]{:S(2)}) copy-start(bf16[8,64]{1,0:T(8,128)(2,1)} %gather_fusion.8) | copy-start | bytes 3076
  126.1 6.1 %copy-start.25 = (bf16[8,64]{1,0:T(8,128)(2,1)S(1)}, bf16[8,64]{1,0:T(8,128)(2,1)}, u32[]{:S(2)}) copy-start(bf16[8,64]{1,0:T(8,128)(2,1)} %gather_fusion.6) | copy-start | bytes 3076
  126.1 6.1 %copy-start.26 = (bf16[8,64]{1,0:T(8,128)(2,1)S(1)}, bf16[8,64]{1,0:T(8,128)(2,1)}, u32[]{:S(2)}) copy-start(bf16[8,64]{1,0:T(8,128)(2,1)} %gather_fusion.2) | copy-start | bytes 3076
  126.1 6.1 %copy-start.27 = (bf16[8,64]{1,0:T(8,128)(2,1)S(1)}, bf16[8,64]{1,0:T(8,128)(2,1)}, u32[]{:S(2)}) copy-start(bf16[8,64]{1,0:T(8,128)(2,1)} %gather_fusion) | copy-start | bytes 3076
  126.1 6.1 %copy-start.28 = (bf16[8,64]{1,0:T(8,128)(2,1)S(1)}, bf16[8,64]{1,0:T(8,128)(2,1)}, u32[]{:S(2)}) copy-start(bf16[8,64]{1,0:T(8,128)(2,1)} %gather_fusion.18) | copy-start | bytes 3076
  126.1 6.1 %copy-start.29 = (bf16[8,64]{1,0:T(8,128)(2,1)S(1)}, bf16[8,64]{1,0:T(8,128)(2,1)}, u32[]{:S(2)}) copy-start(bf16[8,64]{1,0:T(8,128)(2,1)} %gather_fusion.20) | copy-start | bytes 3076
  126.1 6.1 %copy-start.30 = (bf16[8,64]{1,0:T(8,128)(2,1)S(1)}, bf16[8,64]{1,0:T(8,128)(2,1)}, u32[]{:S(2)}) copy-start(bf16[8,64]{1,0:T(8,128)(2,1)} %gather_fusion.24) | copy-start | bytes 3076
  126.1 6.1 %copy-start.31 = (bf16[8,64]{1,0:T(8,128)(2,1)S(1)}, bf16[8,64]{1,0:T(8,128)(2,1)}, u32[]{:S(2)}) copy-start(bf16[8,64]{1,0:T(8,128)(2,1)} %gather_fusion.26) | copy-start | bytes 3076
  132.2 4.4 %copy-start.13 = (bf16[2,2,2,64,128]{4,3,2,1,0:T(8,128)(2,1)S(1)}, bf16[2,2,2,64,128]{4,3,2,1,0:T(8,128)(2,1)}, u32[]{:S(2)}) copy-start(bf16[2,2,2,64,128]{4,3,2,1,0:T(8,128)(2,1)} %param.15) | copy-start | bytes 393220
  136.6 1.0 copy-start.6
  136.6 1.0 copy-start.22
  160.1 0.9 copy-start.3
  292.2 3.9 %copy-start.12 = (f32[128,256]{1,0:T(8,128)S(1)}, f32[128,256]{1,0:T(8,128)}, u32[]{:S(2)}) copy-start(f32[128,256]{1,0:T(8,128)} %get-tuple-element.103) | copy-start | bytes 393220
Sparse Core Ops, SparseCore 0:
  161.1 131.0 all-reduce.2
where the time goes:
time: 306 us; the launch traced here: 304 us
  waiting for transfers between devices  139 us (45%)
  local copies, waits for them, and re-layouts  88 us (29%)
  other arithmetic  24 us (8%)
  matrix products  22.1 us (7%)
  starting transfers between devices  15.5 us (5%)
  between operations  14.8 us (5%)
    psum x1, waiting for transfers between devices, shards(): summed = lax.psum((grad_w_conv, grad_w_down, grad_w_point), ('dp', 'brick'))  131 us
    gather x48, local copies, waits for them, and re-layouts, assemble(): jnp.take(window_part, indices[a][:, 9 * a + 3 * b + c], axis=0, mode='clip')  52.1 us
    slice x22, local copies, waits for them, and re-layouts, assemble(): pools[a][:, :, SPANS[b][0]:SPANS[b][1], SPANS[c][0]:SPANS[c][1], :]  15.4 us
    dot_general x27, matrix products, shards(): lax.dot_general(window_part, flat_grad, (((0,), (0,)), ((), ())), preferr...  14.9 us
    unnamed x72, local copies, waits for them, and re-layouts  9.55 us
    concatenate x2, other arithmetic, assemble(): return jnp.concatenate(planes, axis=1)  8.14 us
    gather x14, other arithmetic, assemble(): jnp.take(window_part, indices[a][:, 9 * a + 3 * b + c], axis=0, mode='clip')  7.79 us
    all_to_all x1, starting transfers between devices, shards(): lax.all_to_all(slot_out, 'brick', split_axis=0, concat_axis=0, tiled=True)  7.22 us
  transfers between devices with their start and end apart: 5, of which 3 were waited for; matrix products, arithmetic and copies ran while one was open for 6% of the time, Pallas kernels for 0%

commit v1 on v0

v1 whole, which is shorter than its diff:
```python
import jax
import jax.numpy as jnp
from jax import lax
from jax.experimental import pallas as pl
from jax.experimental.pallas import tpu as pltpu
from jax.sharding import PartitionSpec as P

F32 = jnp.float32
BF16 = jnp.bfloat16
LANES = 128
VMEM = pl.BlockSpec(memory_space=pltpu.VMEM)
SMEM = pl.BlockSpec(memory_space=pltpu.SMEM)
CONV_ROWS, DOWN_ROWS, POINT_ROWS = 14 * 64, 512, 256
WIRE_ROWS = CONV_ROWS + DOWN_ROWS + POINT_ROWS
HALF = WIRE_ROWS // 2


def mm(a, b, ca=1, cb=0):
    return lax.dot_general(a, b, (((ca,), (cb,)), ((), ())), preferred_element_type=F32)


def sigmoid(v):
    return 1.0 / (1.0 + jnp.exp(-v))


def forward_kernel(
    feat, occ, valid, before, after, w4, wd, wp,
    shifted, slope_pre, hid, coarse_ref, slope_down, slope_point,
    planes, wide,
):
    lane = lax.broadcasted_iota(jnp.int32, (1, 512), 1)
    jj, kk, bb, qq, rr = lane // 256, lane // 128 % 2, lane % 128 // 16, lane // 4 % 4, lane % 4
    voxel = bb * 128 + 8 * (2 * qq + jj) + 2 * rr + kk
    row = lax.broadcasted_iota(jnp.int32, (1024, 512), 0)
    occ_f = occ[...].astype(F32).astype(BF16)
    rows = []
    for m in range(4):
        rows.append(jnp.concatenate([feat[b, :, 128 * m : 128 * m + 128] for b in range(8)], axis=1))
    occ_rows = [
        jnp.concatenate([occ_f[b : b + 1, 128 * m : 128 * m + 128] for b in range(8)], axis=1)
        for m in range(4)
    ]
    occ_rows = jnp.concatenate(occ_rows + [jnp.zeros((12, 1024), BF16)], axis=0)
    stacked = jnp.concatenate(rows + [occ_rows], axis=0)
    zero4 = jnp.zeros((64, 512), BF16)
    lower = jnp.concatenate([zero4] + [before[b] for b in range(4)], axis=1)
    upper = jnp.concatenate([after[b] for b in range(4)] + [zero4], axis=1)
    occ_x = [None] * 8
    edge = [None, None]
    for e in range(2):
        select = jnp.where(row == voxel + 64 * e, 1.0, 0.0).astype(BF16)
        other = upper if e == 0 else lower
        picked = mm(jnp.concatenate([stacked, other], axis=0), select)
        for m in range(4):
            planes[64 * (2 * m + e + 1) : 64 * (2 * m + e + 2), :] = picked[64 * m : 64 * m + 64]
            occ_x[2 * m + e] = picked[256 + m : 257 + m]
        edge[e] = picked[272:336]
    inner_x = lax.broadcasted_iota(jnp.int32, (64, 128), 1) >= 64
    for g in range(4):
        cut = slice(128 * g, 128 * g + 128)
        low = jnp.where(inner_x, edge[1][:, cut], planes[512:576, cut])
        planes[0:64, cut] = pltpu.roll(low, 64, 1)
        high = jnp.where(inner_x, planes[64:128, cut], edge[0][:, cut])
        planes[576:640, cut] = pltpu.roll(high, 64, 1)
    cell = lax.broadcasted_iota(jnp.int32, (1, 128), 1)
    q_at, r_at = cell // 4 % 4, cell % 4
    source = ((1, -1), (0, 0), (1, 0), (0, 1))
    for t in range(4):
        j, dq = source[t]
        for u in range(4):
            k, dr = source[u]
            g = 2 * j + k
            block = planes[:, 128 * g : 128 * g + 128]
            shift = -(4 * dq + dr) % 128
            if shift:
                block = pltpu.roll(block, shift, 1)
            if dr:
                inside = jnp.where(r_at + dr < 0, 0.0, jnp.where(r_at + dr > 3, 0.0, 1.0))
            else:
                inside = jnp.ones((1, 128), F32)
            cross = None if dq == 0 else (q_at == 0 if dq < 0 else q_at == 3)
            for a, (lo, hi) in enumerate(((0, 64), (64, 576), (576, 640))):
                keep = inside
                near = valid[9 * a + 4 : 9 * a + 5]
                if cross is not None:
                    col = 9 * a + 3 * (dq + 1) + 1
                    keep = keep * jnp.where(cross, valid[col : col + 1], near)
                elif a != 1:
                    keep = keep * near
                part = block[lo:hi]
                if a != 1 or dq or dr:
                    part = part * keep
                shifted[t, lo:hi, 128 * u : 128 * u + 128] = part.astype(BF16)
    zero = jnp.zeros((64, 128), BF16)
    for n in range(9):
        wa, wb, wc, wdd = (w4[n, i] for i in range(4))
        for x, parts in enumerate(((wa, wb, zero), (wc, wdd, zero), (zero, wa, wb), (zero, wc, wdd))):
            for i, part in enumerate(parts):
                wide[64 * x : 64 * x + 64, 384 * n + 128 * i : 384 * n + 128 * i + 128] = part
    for h in range(2):
        for j in range(2):
            taps = [
                shifted[j + b, 256 * h : 256 * h + 384, 128 * c : 128 * c + 256]
                for b in range(3)
                for c in range(3)
            ]
            pre = mm(wide[...], jnp.concatenate(taps, axis=0))
            gate = sigmoid(pre)
            for x in range(4):
                sub = slice(64 * x, 64 * x + 64)
                filled = occ_x[4 * h + x][:, 256 * j : 256 * j + 256]
                act, g = pre[sub], gate[sub]
                r0 = 256 * h + 64 * x
                slope_pre[r0 : r0 + 64, 256 * j : 256 * j + 256] = filled * (g * (1.0 + act * (1.0 - g)))
                out = (act * g * filled).astype(BF16)
                p, i = 2 * h + x // 2, x % 2
                for k in range(2):
                    base = 128 * (2 * j + k) + 64 * i
                    hid[base : base + 64, 128 * p : 128 * p + 128] = out[:, 128 * k : 128 * k + 128]
    down = mm(wd[...], hid[...], 0, 0)
    gate = sigmoid(down)
    coarse = (down * gate).astype(BF16)
    coarse_ref[...] = coarse
    slope_down[...] = gate * (1.0 + down * (1.0 - gate))
    point = mm(coarse, wp[...], 0, 0)
    gate = sigmoid(point)
    slope_point[...] = gate * (1.0 + point * (1.0 - gate))


def backward_kernel(
    where_from, core, shifted, slope_pre, hid, coarse, slope_down, slope_point, cot, wd, wp, wire, grads,
):
    def put(first, value):
        done = 0
        while done < value.shape[0]:
            half, at = divmod(first + done, HALF)
            size = min(value.shape[0] - done, HALF - at)
            wire[core[0] if half == 0 else 1 - core[0], at : at + size] = value[done : done + size].astype(BF16)
            done += size

    parts = []
    for p in range(4):
        for b in range(8):
            parts.append(cot[where_from[b], 16 * p : 16 * p + 16, :])
    cot_rows = jnp.concatenate(parts, axis=0)
    grad_point = (cot_rows.astype(F32) * slope_point[...]).astype(BF16)
    gwp = mm(coarse[...], grad_point)
    put(CONV_ROWS + DOWN_ROWS, jnp.concatenate([gwp[:, :128], gwp[:, 128:]], axis=0))
    grad_coarse = mm(wp[...], grad_point, 1, 1).astype(BF16)
    grad_down = (grad_coarse.astype(F32) * slope_down[...]).astype(BF16)
    put(CONV_ROWS, mm(hid[...], grad_down, 1, 1))
    for jk in range(4):
        grad_hidden = mm(wd[128 * jk : 128 * jk + 128], grad_down)
        for p in range(4):
            cut = slice(128 * jk, 128 * jk + 128)
            value = grad_hidden[:, 128 * p : 128 * p + 128] * slope_pre[128 * p : 128 * p + 128, cut]
            h, base = p // 2, 128 * (p % 2)
            grads[base : base + 128, 512 * h + 128 * jk : 512 * h + 128 * jk + 128] = value.astype(BF16)
    low_lanes = lax.broadcasted_iota(jnp.int32, (64, 128), 1) < 64
    thirds = []
    for n in range(9):
        b, c = divmod(n, 3)
        left = jnp.concatenate(
            [
                shifted[j + b, 256 * h : 256 * h + 384, 128 * c : 128 * c + 256]
                for h in range(2)
                for j in range(2)
            ],
            axis=1,
        )
        band = mm(left, grads[...], 1, 1)
        sums = []
        for a in range(3):
            even = band[64 * a : 64 * a + 64, :128] + band[64 * a + 128 : 64 * a + 192, 128:]
            odd = band[64 * a + 64 : 64 * a + 128, :128] + band[64 * a + 192 : 64 * a + 256, 128:]
            both = jnp.where(low_lanes, even, odd)
            sums.append(both + pltpu.roll(both, 64, 1))
        put(64 * n, jnp.where(low_lanes, sums[0], sums[1]))
        thirds.append(sums[2])
    for n in range(5):
        put(64 * (9 + n), jnp.where(low_lanes, thirds[2 * n], thirds[min(2 * n + 1, 8)]))


def finish_kernel(core, mine, other, gwc, gwd, gwp, total):
    total[core[0]] = mine[...]
    total[1 - core[0]] = other[...]

    def rows(first, count):
        half, at = divmod(first, HALF)
        if at + count <= HALF:
            return total[half, at : at + count]
        cut = HALF - at
        return jnp.concatenate([total[half, at:], total[half + 1, : count - cut]], axis=0)

    for n in range(9):
        pair = rows(64 * n, 64).astype(F32)
        gwc[n] = pair[:, :64]
        gwc[9 + n] = pair[:, 64:]
    for n in range(5):
        pair = rows(64 * (9 + n), 64).astype(F32)
        gwc[18 + 2 * n] = pair[:, :64]
        if n < 4:
            gwc[19 + 2 * n] = pair[:, 64:]
    for i in range(2):
        for jk in range(4):
            gwd[4 * i + jk] = rows(CONV_ROWS + 128 * jk + 64 * i, 64).astype(F32)
    for s in range(2):
        gwp[:, 128 * s : 128 * s + 128] = rows(CONV_ROWS + DOWN_ROWS + 128 * s, 128).astype(F32)


def call(kernel, outs, ins, scratch=(), limit=24 * 2**20, flops=0, specs=None):
    return pl.pallas_call(
        kernel,
        out_shape=outs,
        in_specs=specs or [VMEM] * len(ins),
        out_specs=jax.tree.map(lambda _: VMEM, outs),
        scratch_shapes=scratch,
        compiler_params=pltpu.CompilerParams(vmem_limit_bytes=limit),
        cost_estimate=pl.CostEstimate(flops=flops, bytes_accessed=2**20, transcendentals=0),
    )(*ins)


def swap(value, axis, bit):
    size = lax.axis_size(axis)
    return lax.ppermute(value, axis, [(i, i ^ bit) for i in range(size)])


def powers(size, first):
    bits = []
    while first < size:
        bits.append(first)
        first *= 2
    return bits


def shards(features, occupancy, neighbours, owners, w_conv, w_down, w_point, cotangent):
    dp_size, brick_size = lax.axis_size("dp"), lax.axis_size("brick")
    core = (lax.axis_index("brick") % 2).astype(jnp.int32).reshape(1)
    feat = jnp.swapaxes(features[0], 1, 2)
    slots = owners[0]
    target = slots // 8
    wanted = jnp.arange(brick_size, dtype=jnp.int32)[:, None] == target[None, :]
    request = jnp.max(jnp.where(wanted, (slots % 8)[None, :], 0), axis=1)
    arrived = lax.all_to_all(request, "brick", split_axis=0, concat_axis=0, tiled=True)
    reply = jnp.take(cotangent[0], arrived, axis=0, mode="clip")
    fetched = lax.all_to_all(reply, "brick", split_axis=0, concat_axis=0, tiled=True)
    up = [(i, i + 1) for i in range(brick_size - 1)]
    down = [(j, i) for i, j in up]
    before = lax.ppermute(feat[4:8, :, 384:512], "brick", up)
    after = lax.ppermute(feat[0:4, :, 0:128], "brick", down)
    valid = jnp.repeat((neighbours[0] >= 0).astype(F32).T, 16, axis=1)
    turned = w_conv.transpose(0, 1, 2, 4, 3).reshape(3, 9, 64, 64)
    none = jnp.zeros_like(turned[0])
    w4 = jnp.stack(
        [
            jnp.concatenate([turned[0], turned[1]], axis=-1),
            jnp.concatenate([turned[2], none], axis=-1),
            jnp.concatenate([none, turned[0]], axis=-1),
            jnp.concatenate([turned[1], turned[2]], axis=-1),
        ],
        axis=1,
    )
    wd = w_down.transpose(1, 2, 0, 3, 4).reshape(512, 128)
    shape = jax.ShapeDtypeStruct
    saved = call(
        forward_kernel,
        (
            shape((4, 640, 512), BF16),
            shape((512, 512), F32),
            shape((512, 512), BF16),
            shape((128, 512), BF16),
            shape((128, 512), F32),
            shape((512, 256), F32),
        ),
        (feat, occupancy[0], valid, before, after, w4, wd, w_point),
        scratch=[pltpu.VMEM((640, 512), F32), pltpu.VMEM((256, 3456), BF16)],
        flops=4 * 10**9,
    )
    wire = call(
        backward_kernel,
        shape((2, HALF, LANES), BF16),
        (target, core, *saved, fetched, wd, w_point),
        scratch=[pltpu.VMEM((256, 1024), BF16)],
        flops=4 * 10**9,
        specs=[SMEM, SMEM] + [VMEM] * 9,
    )
    total = wire[0] + swap(wire[1], "brick", 1)
    halves = [total[: HALF // 2], total[HALF // 2 :]]
    bits = powers(dp_size, 1)
    for n in range(len(bits)):
        moved = [swap(part, "dp", bits[(n + s) % len(bits)]) for s, part in enumerate(halves)]
        halves = [a + b for a, b in zip(halves, moved)]
    total = jnp.concatenate(halves, axis=0)
    for bit in powers(brick_size, 2):
        total = total + swap(total, "brick", bit)
    other = swap(total, "brick", 1)
    gwc, gwd, gwp = call(
        finish_kernel,
        (shape((27, 64, 64), F32), shape((8, 64, 128), F32), shape((128, 256), F32)),
        (core, total, other),
        scratch=[pltpu.VMEM((2, HALF, LANES), BF16)],
        specs=[SMEM, VMEM, VMEM],
    )
    return gwc.reshape(3, 3, 3, 64, 64), gwd.reshape(2, 2, 2, 64, 128), gwp


def solution(mesh):
    in_specs = (
        P("dp", "brick", None, None),
        P("dp", "brick", None),
        P("dp", "brick", None),
        P("dp", "brick"),
        P(),
        P(),
        P(),
        P("dp", "brick", None, None),
    )
    out_specs = (P(), P(), P())
    return jax.shard_map(shards, mesh=mesh, in_specs=in_specs, out_specs=out_specs, check_vma=False)
```

time: 306 us -> 75.3 us (0.25)
  waiting for transfers between devices: 139 us -> 28.5 us
  local copies, waits for them, and re-layouts: 88 us -> 12.2 us
  matrix products: 22.1 us -> 0 us
  other arithmetic: 24 us -> 2.96 us
  between operations: 14.8 us -> 0.87 us
  Pallas kernels: 0 us -> 8.41 us
  starting transfers between devices: 15.5 us -> 21.8 us
    psum x1 -> x0, waiting for transfers between devices: 131 us -> none  [shards(): summed = lax.psum((grad_w_conv, grad_w_down, grad_w_point), ('dp', 'brick'))]
    gather x50 -> x1, local copies, waits for them, and re-layouts: 53.5 us -> 1.27 us  [shards(): reply = jnp.take(cotangent[0], arrived, axis=0, mode='clip')]
    ppermute x2 -> x10, waiting for transfers between devices: 0.01 us -> 24.8 us  [the longest x8 24.8 us: swap(): return lax.ppermute(value, axis, [(i, i ^ bit) for i in range(size)])]
    dot_general x33 -> x0, matrix products: 17.7 us -> none  [the longest x27 14.9 us: shards(): lax.dot_general(window_part, flat_grad, (((0,), (0,)), ((), ())), preferr...]
    slice x27 -> x6, local copies, waits for them, and re-layouts: 17.3 us -> 2.57 us  [the longest x2 1.31 us: shards(): turned[0]]
    concatenate x3 -> x1, other arithmetic: 10.7 us -> 0.02 us  [shards(): total = jnp.concatenate(halves, axis=0)]
    pallas_call x0 -> x3, Pallas kernels: none -> 8.41 us  [call(): pl.pallas_call(kernel, out_shape=outs, in_specs=specs or [VMEM] * len(ins...]
    gather x16 -> x1, other arithmetic: 8.41 us -> 0.01 us  [shards(): reply = jnp.take(cotangent[0], arrived, axis=0, mode='clip')]
  transfers between devices with their start and end apart: 5 -> 12, of which waited for: 3 -> 10; matrix products, arithmetic and copies ran while one was open for 6% -> 10% of each run, Pallas kernels for 0% -> 5%
where the time goes in v1:
time: 75.3 us; the launch traced here: 74.8 us
  waiting for transfers between devices  28.5 us (38%)
  starting transfers between devices  21.8 us (29%)
  local copies, waits for them, and re-layouts  12.2 us (16%)
  Pallas kernels  8.41 us (11%)
  other arithmetic  2.96 us (4%)
  between operations  0.87 us (1%)
    ppermute x8, waiting for transfers between devices, swap(): return lax.ppermute(value, axis, [(i, i ^ bit) for i in range(size)])  24.8 us
    pallas_call x3, Pallas kernels, call(): pl.pallas_call(kernel, out_shape=outs, in_specs=specs or [VMEM] * len(ins...  8.41 us
    all_to_all x1, starting transfers between devices, shards(): lax.all_to_all(request, 'brick', split_axis=0, concat_axis=0, tiled=True)  8.24 us
    unnamed x20, local copies, waits for them, and re-layouts  6.46 us
    ppermute x8, starting transfers between devices, swap(): return lax.ppermute(value, axis, [(i, i ^ bit) for i in range(size)])  5.83 us
    all_to_all x1, starting transfers between devices, shards(): lax.all_to_all(reply, 'brick', split_axis=0, concat_axis=0, tiled=True)  4.13 us
    all_to_all x1, waiting for transfers between devices, shards(): lax.all_to_all(reply, 'brick', split_axis=0, concat_axis=0, tiled=True)  2.73 us
    ppermute x1, starting transfers between devices, shards(): before = lax.ppermute(feat[4:8, :, 384:512], 'brick', up)  2.36 us
  transfers between devices with their start and end apart: 12, of which 10 were waited for; matrix products, arithmetic and copies ran while one was open for 10% of the time, Pallas kernels for 5%

profile of v1, /device:TPU:0, one launch (start us, length us, event | category | flops | bytes accessed | tf_op | source)
XLA Modules:
  0.0 74.8 jit_solution(7532011427336514039)
XLA Ops:
  0.6 0.0 copy-start
  0.6 0.9 %fusion.4 = (bf16[4,64,128]{2,1,0:T(8,128)(2,1)S(1)}, bf16[4,64,128]{2,1,0:T(8,128)(2,1)S(1)}) fusion(bf16[8,64,512]{2,1,0:T(8,128)(2,1)} %bitcast.54), kind=kLoop, calls=%fused_computation.29 | loop fusion | bytes 262144 | tf_op jit(solution)/shard_map/slice | solution.py:250
  1.6 2.4 %collective-permute-start = (bf16[4,64,128]{2,1,0:T(8,128)(2,1)S(1)}, bf16[4,64,128]{2,1,0:T(8,128)(2,1)S(1)}, u32[]{:S(2)}, u32[]{:S(2)}) collective-permute-start(bf16[4,64,128]{2,1,0:T(8,128)(2,1)S(1)} %get-tuple-element.22), channel_id=1, source_target_pairs={{0,1},{1,2},{2,3},{3,4},{4,5},{5,6},{6,7},{8,9},{9,10},{10,11},{11... | collective-permute-start | bytes 196616 | tf_op jit(solution)/shard_map/ppermute | solution.py:249
  3.9 1.3 %collective-permute-start.1 = (bf16[4,64,128]{2,1,0:T(8,128)(2,1)S(1)}, bf16[4,64,128]{2,1,0:T(8,128)(2,1)S(1)}, u32[]{:S(2)}, u32[]{:S(2)}) collective-permute-start(bf16[4,64,128]{2,1,0:T(8,128)(2,1)S(1)} %get-tuple-element.21), channel_id=1, source_target_pairs={{1,0},{2,1},{3,2},{4,3},{5,4},{6,5},{7,6},{9,8},{10,9},{11,10},{12... | collective-permute-start | bytes 196616 | tf_op jit(solution)/shard_map/ppermute | solution.py:250
  5.2 0.7 fusion.2
  5.9 0.1 select_reduce_fusion
  6.0 0.7 copy.53
  6.7 8.2 %all-to-all-start = ((s32[8,1,1]{2,1,0:T(1,128)}), s32[8,1,1]{2,1,0:T(1,128)S(1)}, u32[]{:S(2)}, u32[]{:S(2)}) async-start(s32[8,1,1]{2,1,0:T(1,128)} %copy.53), calls=%async_computation | async-start | bytes 8192 | tf_op jit(solution)/shard_map/all_to_all | solution.py:244
  14.9 0.7 and_select_fusion.2.where_from
  15.6 0.0 copy-start.1
  15.6 0.0 copy-start.2
  15.6 0.0 copy-start.3
  15.6 1.1 %fusion.5 = (bf16[1,3,3,64,64]{3,4,2,1,0:T(8,128)(2,1)S(1)}, bf16[1,3,3,64,64]{3,4,2,1,0:T(8,128)(2,1)S(1)}, bf16[1,3,3,64,64]{3,4,2,1,0:T(8,128)(2,1)S(1)}) fusion(bf16[3,3,3,64,64]{3,4,2,1,0:T(8,128)(2,1)} %bitcast.60), kind=kLoop, calls=%fused_computation.30 | loop fusion | bytes 442368 | tf_op jit(solution)/shard_map/slice | solution.py:256
  16.8 0.2 copy.47
  16.9 0.2 copy.48
  17.1 0.2 copy.46
  17.3 0.9 %copy.52 = bf16[2,2,2,64,128]{4,3,2,1,0:T(8,128)(2,1)S(1)} copy(bf16[2,2,2,64,128]{4,3,1,0,2:T(8,128)(2,1)} %bitcast.61) | data formatting | bytes 262144 | tf_op jit(solution)/shard_map/transpose | solution.py:263
  18.2 0.7 convert_bitcast_fusion
  18.9 0.1 copy.45
  19.0 0.1 broadcast_in_dim.25
  19.1 0.1 reshape.36.valid
  19.2 0.3 maximum_bitcast_fusion
  19.4 1.0 %all-to-all-done = s32[8,1,1]{2,1,0:T(1,128)S(1)} async-done(((s32[8,1,1]{2,1,0:T(1,128)}), s32[8,1,1]{2,1,0:T(1,128)S(1)}, u32[]{:S(2)}, u32[]{:S(2)}) %all-to-all-start) | async-done | bytes 64 | tf_op jit(solution)/shard_map/all_to_all | solution.py:244
  20.4 0.2 reduce
  20.7 0.0 copy-done
  20.7 1.3 %gather_fusion = bf16[8,64,256]{2,1,0:T(8,128)(2,1)} fusion(bf16[8,64,256]{2,1,0:T(8,128)(2,1)S(1)} %bitcast.51, s32[1024]{0:T(1024)S(1)} %pad_clamp_fusion), kind=kCustom, calls=%fused_computation | custom fusion | bytes 524320 | tf_op jit(solution)/shard_map/jit(_take)/gather | solution.py:245
  21.9 4.1 %all-to-all-start.1 = ((bf16[8,64,256]{2,1,0:T(8,128)(2,1)}), bf16[8,64,256]{2,1,0:T(8,128)(2,1)S(1)}, u32[]{:S(2)}, u32[]{:S(2)}) async-start(bf16[8,64,256]{2,1,0:T(8,128)(2,1)} %gather_fusion), calls=%async_computation.1 | async-start | bytes 524288 | tf_op jit(solution)/shard_map/all_to_all | solution.py:246
  26.1 0.1 pad_maximum_fusion.w4
  26.2 0.0 collective-permute-done.before
  26.2 0.0 collective-permute-done.1.after
  26.2 0.0 copy-done.1
  26.2 0.0 copy-done.2
  26.2 0.0 copy-done.3
  26.2 4.0 %shard_map.103 = (bf16[4,640,512]{2,1,0:T(8,128)(2,1)S(1)}, f32[512,512]{1,0:T(8,128)S(1)}, bf16[512,512]{1,0:T(8,128)(2,1)S(1)}, bf16[128,512]{1,0:T(8,128)(2,1...) custom-call(bf16[8,64,512]{2,1,0:T(8,128)(2,1)S(1)} %bitcast.55, s32[8,512]{1,0:T(8,128)S(1)} %bitcast.56, ...), custom_call_target="tpu_custom_call" | custom-call | flops 4000000000 | bytes 1048576 | tf_op jit(solution)/shard_map/pallas_call | solution.py:212
  30.2 0.0 copy-start.4
  30.2 1.5 %copy-done.4 = bf16[4,640,512]{2,1,0:T(8,128)(2,1)} copy-done((bf16[4,640,512]{2,1,0:T(8,128)(2,1)}, bf16[4,640,512]{2,1,0:T(8,128)(2,1)S(1)}, u32[]{:S(2)}) %copy-start.4) | copy-done | bytes 2621464
  31.7 0.0 copy-start.6
  31.7 0.7 copy-done.6
  32.4 0.0 copy-start.8
  32.4 0.7 copy-done.8
  33.1 2.7 %all-to-all-done.1.cot = bf16[8,64,256]{2,1,0:T(8,128)(2,1)S(1)} async-done(((bf16[8,64,256]{2,1,0:T(8,128)(2,1)}), bf16[8,64,256]{2,1,0:T(8,128)(2,1)S(1)}, u32[]{:S(2)}, u32[]{:S(2)}) %all-to-all-start.1) | async-done | bytes 262176 | tf_op jit(solution)/shard_map/all_to_all | solution.py:246
  35.8 1.7 %copy-done.5 = bf16[4,640,512]{2,1,0:T(8,128)(2,1)S(1)} copy-done((bf16[4,640,512]{2,1,0:T(8,128)(2,1)S(1)}, bf16[4,640,512]{2,1,0:T(8,128)(2,1)}, u32[]{:S(2)}) %copy-start.5) | copy-done | bytes 2621464
  37.6 0.9 %copy-done.7 = f32[128,512]{1,0:T(8,128)S(1)} copy-done((f32[128,512]{1,0:T(8,128)S(1)}, f32[128,512]{1,0:T(8,128)}, u32[]{:S(2)}) %copy-start.7) | copy-done | bytes 262168
  38.5 0.9 %copy-done.9 = bf16[128,512]{1,0:T(8,128)(2,1)S(1)} copy-done((bf16[128,512]{1,0:T(8,128)(2,1)S(1)}, bf16[128,512]{1,0:T(8,128)(2,1)}, u32[]{:S(2)}) %copy-start.9) | copy-done | bytes 131096
  39.4 3.2 %shard_map.104 = bf16[2,832,128]{2,1,0:T(8,128)(2,1)S(1)} custom-call(s32[8]{0:T(128)S(1)} %and_select_fusion.2.where_from, s32[1]{0:T(128)} %bitcast.core, bf16[4,640,512]{2,1,0:T(8,128)(2,1)S(1)} %copy-done.5, f32[512,512]{1,0:T(8,128)S(1)} %get-tuple-element.13.slope_pre, bf16[512,512]{1,0:T(8,128)(2,1)S(1)} %get-tuple-element.14.hid, ...), custom_call_target="tpu_custom_call" | custom-call | flops 4000000000 | bytes 1048576 | tf_op jit(solution)/shard_map/pallas_call | solution.py:212
  42.7 0.1 collective-permute-start.2
  42.8 1.5 %collective-permute-done.2 = bf16[832,128]{1,0:T(8,128)(2,1)S(1)} collective-permute-done((bf16[832,128]{1,0:T(8,128)(2,1)S(1)}, bf16[832,128]{1,0:T(8,128)(2,1)S(1)}, u32[]{:S(2)}, u32[]{:S(2)}) %collective-permute-start.2) | collective-permute-done | bytes 213024 | tf_op jit(solution)/shard_map/ppermute | solution.py:225
  44.3 1.6 %collective-permute-start.3 = (bf16[416,128]{1,0:T(8,128)(2,1)S(1)}, bf16[416,128]{1,0:T(8,128)(2,1)S(1)}, u32[]{:S(2)}, u32[]{:S(2)}) collective-permute-start(bf16[416,128]{1,0:T(8,128)(2,1)S(1)} %get-tuple-element.28), channel_id=1, source_target_pairs={{0,8},{8,0},{16,24},{24,16},{1,9},{9,1},{17,25},{25,17},{2,10},{10... | collective-permute-start | bytes 319496 | tf_op jit(solution)/shard_map/ppermute | solution.py:225
  45.8 1.5 %collective-permute-start.5 = (bf16[416,128]{1,0:T(8,128)(2,1)S(1)}, bf16[416,128]{1,0:T(8,128)(2,1)S(1)}, u32[]{:S(2)}, u32[]{:S(2)}) collective-permute-start(bf16[416,128]{1,0:T(8,128)(2,1)S(1)} %get-tuple-element.29), channel_id=1, source_target_pairs={{0,16},{8,24},{16,0},{24,8},{1,17},{9,25},{17,1},{25,9},{2,18},{10... | collective-permute-start | bytes 319496 | tf_op jit(solution)/shard_map/ppermute | solution.py:225
  47.3 2.0 %collective-permute-done.3 = bf16[416,128]{1,0:T(8,128)(2,1)S(1)} collective-permute-done((bf16[416,128]{1,0:T(8,128)(2,1)S(1)}, bf16[416,128]{1,0:T(8,128)(2,1)S(1)}, u32[]{:S(2)}, u32[]{:S(2)}) %collective-permute-start.3) | collective-permute-done | bytes 106528 | tf_op jit(solution)/shard_map/ppermute | solution.py:225
  49.4 1.2 %collective-permute-done.5 = bf16[416,128]{1,0:T(8,128)(2,1)S(1)} collective-permute-done((bf16[416,128]{1,0:T(8,128)(2,1)S(1)}, bf16[416,128]{1,0:T(8,128)(2,1)S(1)}, u32[]{:S(2)}, u32[]{:S(2)}) %collective-permute-start.5) | collective-permute-done | bytes 106528 | tf_op jit(solution)/shard_map/ppermute | solution.py:225
  50.6 1.6 %collective-permute-start.4 = (bf16[416,128]{1,0:T(8,128)(2,1)S(1)}, bf16[416,128]{1,0:T(8,128)(2,1)S(1)}, u32[]{:S(2)}, u32[]{:S(2)}) collective-permute-start(bf16[416,128]{1,0:T(8,128)(2,1)S(1)} %get-tuple-element.26), channel_id=1, source_target_pairs={{0,16},{8,24},{16,0},{24,8},{1,17},{9,25},{17,1},{25,9},{2,18},{10... | collective-permute-start | bytes 319496 | tf_op jit(solution)/shard_map/ppermute | solution.py:225
  52.2 0.5 collective-permute-start.6
  52.7 2.6 %collective-permute-done.4 = bf16[416,128]{1,0:T(8,128)(2,1)S(1)} collective-permute-done((bf16[416,128]{1,0:T(8,128)(2,1)S(1)}, bf16[416,128]{1,0:T(8,128)(2,1)S(1)}, u32[]{:S(2)}, u32[]{:S(2)}) %collective-permute-start.4) | collective-permute-done | bytes 106528 | tf_op jit(solution)/shard_map/ppermute | solution.py:225
  55.4 1.5 %collective-permute-done.6 = bf16[416,128]{1,0:T(8,128)(2,1)S(1)} collective-permute-done((bf16[416,128]{1,0:T(8,128)(2,1)S(1)}, bf16[416,128]{1,0:T(8,128)(2,1)S(1)}, u32[]{:S(2)}, u32[]{:S(2)}) %collective-permute-start.6) | collective-permute-done | bytes 106528 | tf_op jit(solution)/shard_map/ppermute | solution.py:225
  56.9 0.2 collective-permute-start.7
  57.2 5.7 %collective-permute-done.7 = bf16[832,128]{1,0:T(8,128)(2,1)S(1)} collective-permute-done((bf16[832,128]{1,0:T(8,128)(2,1)S(1)}, bf16[832,128]{1,0:T(8,128)(2,1)S(1)}, u32[]{:S(2)}, u32[]{:S(2)}) %collective-permute-start.7) | collective-permute-done | bytes 213024 | tf_op jit(solution)/shard_map/ppermute | solution.py:225
  62.9 0.1 fusion.3
  62.9 0.3 collective-permute-start.8
  63.2 8.8 %collective-permute-done.8 = bf16[832,128]{1,0:T(8,128)(2,1)S(1)} collective-permute-done((bf16[832,128]{1,0:T(8,128)(2,1)S(1)}, bf16[832,128]{1,0:T(8,128)(2,1)S(1)}, u32[]{:S(2)}, u32[]{:S(2)}) %collective-permute-start.8) | collective-permute-done | bytes 213024 | tf_op jit(solution)/shard_map/ppermute | solution.py:225
  72.0 0.1 add.46.mine
  72.1 0.1 collective-permute-start.9
  72.2 1.5 %collective-permute-done.9.other = bf16[832,128]{1,0:T(8,128)(2,1)S(1)} collective-permute-done((bf16[832,128]{1,0:T(8,128)(2,1)S(1)}, bf16[832,128]{1,0:T(8,128)(2,1)S(1)}, u32[]{:S(2)}, u32[]{:S(2)}) %collective-permute-start.9) | collective-permute-done | bytes 213024 | tf_op jit(solution)/shard_map/ppermute | solution.py:225
  73.6 1.1 %shard_map.105 = (f32[27,64,64]{2,1,0:T(8,128)}, f32[8,64,128]{2,1,0:T(8,128)}, f32[128,256]{1,0:T(8,128)}) custom-call(s32[1]{0:T(128)} %bitcast.core, bf16[832,128]{1,0:T(8,128)(2,1)S(1)} %add.46.mine, bf16[832,128]{1,0:T(8,128)(2,1)S(1)} %collective-permute-done.9.other), custom_call_target="tpu_custom_call" | custom-call | bytes 1048576 | tf_op jit(solution)/shard_map/pallas_call | solution.py:212
  (11 shorter events, 0.2 us)
Async XLA Ops:
  0.6 20.0 %copy-start = (bf16[1,8,64,256]{3,2,1,0:T(8,128)(2,1)S(1)}, bf16[1,8,64,256]{3,2,1,0:T(8,128)(2,1)}, u32[]{:S(2)}) copy-start(bf16[1,8,64,256]{3,2,1,0:T(8,128)(2,1)} %param.15) | copy-start | bytes 786436
  1.6 24.6 %collective-permute-start = (bf16[4,64,128]{2,1,0:T(8,128)(2,1)S(1)}, bf16[4,64,128]{2,1,0:T(8,128)(2,1)S(1)}, u32[]{:S(2)}, u32[]{:S(2)}) collective-permute-start(bf16[4,64,128]{2,1,0:T(8,128)(2,1)S(1)} %get-tuple-element.22), channel_id=1, source_target_pairs={{0,1},{1,2},{2,3},{3,4},{4,5},{5,6},{6,7},{8,9},{9,10},{10,11},{11... | collective-permute-start | bytes 196616 | tf_op jit(solution)/shard_map/ppermute | solution.py:249
  3.9 22.2 %collective-permute-start.1 = (bf16[4,64,128]{2,1,0:T(8,128)(2,1)S(1)}, bf16[4,64,128]{2,1,0:T(8,128)(2,1)S(1)}, u32[]{:S(2)}, u32[]{:S(2)}) collective-permute-start(bf16[4,64,128]{2,1,0:T(8,128)(2,1)S(1)} %get-tuple-element.21), channel_id=1, source_target_pairs={{1,0},{2,1},{3,2},{4,3},{5,4},{6,5},{7,6},{9,8},{10,9},{11,10},{12... | collective-permute-start | bytes 196616 | tf_op jit(solution)/shard_map/ppermute | solution.py:250
  6.7 13.7 %all-to-all-start = ((s32[8,1,1]{2,1,0:T(1,128)}), s32[8,1,1]{2,1,0:T(1,128)S(1)}, u32[]{:S(2)}, u32[]{:S(2)}) async-start(s32[8,1,1]{2,1,0:T(1,128)} %copy.53), calls=%async_computation | async-start | bytes 8192 | tf_op jit(solution)/shard_map/all_to_all | solution.py:244
  15.6 10.6 %copy-start.1 = (bf16[1,8,512,64]{2,3,1,0:T(8,128)(2,1)S(1)}, bf16[1,8,512,64]{2,3,1,0:T(8,128)(2,1)}, u32[]{:S(2)}) copy-start(bf16[1,8,512,64]{2,3,1,0:T(8,128)(2,1)} %param.8) | copy-start | bytes 1572868
  15.6 10.6 %copy-start.2 = (bf16[128,256]{1,0:T(8,128)(2,1)S(1)}, bf16[128,256]{1,0:T(8,128)(2,1)}, u32[]{:S(2)}) copy-start(bf16[128,256]{1,0:T(8,128)(2,1)} %wp.3) | copy-start | bytes 196612
  15.6 10.6 %copy-start.3 = (s32[1,8,512]{2,1,0:T(8,128)S(1)}, s32[1,8,512]{2,1,0:T(8,128)}, u32[]{:S(2)}) copy-start(s32[1,8,512]{2,1,0:T(8,128)} %param.9) | copy-start | bytes 49156
  21.9 13.9 %all-to-all-start.1 = ((bf16[8,64,256]{2,1,0:T(8,128)(2,1)}), bf16[8,64,256]{2,1,0:T(8,128)(2,1)S(1)}, u32[]{:S(2)}, u32[]{:S(2)}) async-start(bf16[8,64,256]{2,1,0:T(8,128)(2,1)} %gather_fusion), calls=%async_computation.1 | async-start | bytes 524288 | tf_op jit(solution)/shard_map/all_to_all | solution.py:246
  30.2 1.5 %copy-start.4 = (bf16[4,640,512]{2,1,0:T(8,128)(2,1)}, bf16[4,640,512]{2,1,0:T(8,128)(2,1)S(1)}, u32[]{:S(2)}) copy-start(bf16[4,640,512]{2,1,0:T(8,128)(2,1)S(1)} %get-tuple-element.12.shifted) | copy-start | bytes 7864324
  31.7 0.7 copy-start.6
  32.4 0.7 copy-start.8
  35.8 1.7 %copy-start.5 = (bf16[4,640,512]{2,1,0:T(8,128)(2,1)S(1)}, bf16[4,640,512]{2,1,0:T(8,128)(2,1)}, u32[]{:S(2)}) copy-start(bf16[4,640,512]{2,1,0:T(8,128)(2,1)} %copy-done.4) | copy-start | bytes 7864324
  37.6 0.9 %copy-start.7 = (f32[128,512]{1,0:T(8,128)S(1)}, f32[128,512]{1,0:T(8,128)}, u32[]{:S(2)}) copy-start(f32[128,512]{1,0:T(8,128)} %copy-done.6) | copy-start | bytes 786436
  38.5 0.9 %copy-start.9 = (bf16[128,512]{1,0:T(8,128)(2,1)S(1)}, bf16[128,512]{1,0:T(8,128)(2,1)}, u32[]{:S(2)}) copy-start(bf16[128,512]{1,0:T(8,128)(2,1)} %copy-done.8) | copy-start | bytes 393220
  42.7 1.5 %collective-permute-start.2 = (bf16[832,128]{1,0:T(8,128)(2,1)S(1)}, bf16[832,128]{1,0:T(8,128)(2,1)S(1)}, u32[]{:S(2)}, u32[]{:S(2)}) collective-permute-start(bf16[832,128]{1,0:T(8,128)(2,1)S(1)} %slice_bitcast_fusion), channel_id=1, source_target_pairs={{0,1},{1,0},{2,3},{3,2},{4,5},{5,4},{6,7},{7,6},{8,9},{9,8},{10,11... | collective-permute-start | bytes 638984 | tf_op jit(solution)/shard_map/ppermute | solution.py:225
  44.3 5.1 %collective-permute-start.3 = (bf16[416,128]{1,0:T(8,128)(2,1)S(1)}, bf16[416,128]{1,0:T(8,128)(2,1)S(1)}, u32[]{:S(2)}, u32[]{:S(2)}) collective-permute-start(bf16[416,128]{1,0:T(8,128)(2,1)S(1)} %get-tuple-element.28), channel_id=1, source_target_pairs={{0,8},{8,0},{16,24},{24,16},{1,9},{9,1},{17,25},{25,17},{2,10},{10... | collective-permute-start | bytes 319496 | tf_op jit(solution)/shard_map/ppermute | solution.py:225
  45.8 4.7 %collective-permute-start.5 = (bf16[416,128]{1,0:T(8,128)(2,1)S(1)}, bf16[416,128]{1,0:T(8,128)(2,1)S(1)}, u32[]{:S(2)}, u32[]{:S(2)}) collective-permute-start(bf16[416,128]{1,0:T(8,128)(2,1)S(1)} %get-tuple-element.29), channel_id=1, source_target_pairs={{0,16},{8,24},{16,0},{24,8},{1,17},{9,25},{17,1},{25,9},{2,18},{10... | collective-permute-start | bytes 319496 | tf_op jit(solution)/shard_map/ppermute | solution.py:225
  50.6 4.8 %collective-permute-start.4 = (bf16[416,128]{1,0:T(8,128)(2,1)S(1)}, bf16[416,128]{1,0:T(8,128)(2,1)S(1)}, u32[]{:S(2)}, u32[]{:S(2)}) collective-permute-start(bf16[416,128]{1,0:T(8,128)(2,1)S(1)} %get-tuple-element.26), channel_id=1, source_target_pairs={{0,16},{8,24},{16,0},{24,8},{1,17},{9,25},{17,1},{25,9},{2,18},{10... | collective-permute-start | bytes 319496 | tf_op jit(solution)/shard_map/ppermute | solution.py:225
  52.2 4.7 %collective-permute-start.6 = (bf16[416,128]{1,0:T(8,128)(2,1)S(1)}, bf16[416,128]{1,0:T(8,128)(2,1)S(1)}, u32[]{:S(2)}, u32[]{:S(2)}) collective-permute-start(bf16[416,128]{1,0:T(8,128)(2,1)S(1)} %get-tuple-element.27), channel_id=1, source_target_pairs={{0,8},{8,0},{16,24},{24,16},{1,9},{9,1},{17,25},{25,17},{2,10},{10... | collective-permute-start | bytes 319496 | tf_op jit(solution)/shard_map/ppermute | solution.py:225
  56.9 5.9 %collective-permute-start.7 = (bf16[832,128]{1,0:T(8,128)(2,1)S(1)}, bf16[832,128]{1,0:T(8,128)(2,1)S(1)}, u32[]{:S(2)}, u32[]{:S(2)}) collective-permute-start(bf16[832,128]{1,0:T(8,128)(2,1)S(1)} %pad_maximum_fusion.1), channel_id=1, source_target_pairs={{0,2},{1,3},{2,0},{3,1},{4,6},{5,7},{6,4},{7,5},{8,10},{9,11},{10,... | collective-permute-start | bytes 638984 | tf_op jit(solution)/shard_map/ppermute | solution.py:225
  62.9 9.1 %collective-permute-start.8 = (bf16[832,128]{1,0:T(8,128)(2,1)S(1)}, bf16[832,128]{1,0:T(8,128)(2,1)S(1)}, u32[]{:S(2)}, u32[]{:S(2)}) collective-permute-start(bf16[832,128]{1,0:T(8,128)(2,1)S(1)} %fusion.3), channel_id=1, source_target_pairs={{0,4},{1,5},{2,6},{3,7},{4,0},{5,1},{6,2},{7,3},{8,12},{9,13},{10,... | collective-permute-start | bytes 638984 | tf_op jit(solution)/shard_map/ppermute | solution.py:225
  72.1 1.5 %collective-permute-start.9 = (bf16[832,128]{1,0:T(8,128)(2,1)S(1)}, bf16[832,128]{1,0:T(8,128)(2,1)S(1)}, u32[]{:S(2)}, u32[]{:S(2)}) collective-permute-start(bf16[832,128]{1,0:T(8,128)(2,1)S(1)} %add.46.mine), channel_id=1, source_target_pairs={{0,1},{1,0},{2,3},{3,2},{4,5},{5,4},{6,7},{7,6},{8,9},{9,8},{10,11... | collective-permute-start | bytes 638984 | tf_op jit(solution)/shard_map/ppermute | solution.py:225

commit v2 on v1

v2 whole, which is shorter than its diff:
```python
import functools

import jax
import jax.numpy as jnp
from jax import lax
from jax.experimental import pallas as pl
from jax.experimental.pallas import tpu as pltpu
from jax.sharding import PartitionSpec as P

F32 = jnp.float32
BF16 = jnp.bfloat16
LANES = 128
VMEM = pl.BlockSpec(memory_space=pltpu.VMEM)
HBM = pl.BlockSpec(memory_space=pltpu.HBM)
SMEM = pl.BlockSpec(memory_space=pltpu.SMEM)
COARSE_HALF, CONV_HALF = 384, 448


def mm(a, b, ca=1, cb=0):
    return lax.dot_general(a, b, (((ca,), (cb,)), ((), ())), preferred_element_type=F32)


def sigmoid(v):
    return 1.0 / (1.0 + jnp.exp(-v))


def turned_weights(w_conv):
    near = lax.broadcasted_iota(jnp.int32, (64, 64), 0) == lax.broadcasted_iota(jnp.int32, (64, 64), 1)
    eye = jnp.where(near, 1.0, 0.0).astype(BF16)
    zero = jnp.zeros((64, 64), BF16)
    first = jnp.concatenate([w_conv[9 * a + n] if a < 3 else zero for n in range(9) for a in range(4)], axis=0)
    second = jnp.concatenate([w_conv[9 * a + n] if a >= 0 else zero for n in range(9) for a in range(-1, 3)], axis=0)
    return mm(eye, first, 1, 1).astype(BF16), mm(eye, second, 1, 1).astype(BF16)


def near_masks(neighbours):
    brick = lax.broadcasted_iota(jnp.int32, (8, 128), 0)
    lane = lax.broadcasted_iota(jnp.int32, (8, 128), 1)
    spread = jnp.where(lane // 16 == brick, 1.0, 0.0)
    return mm(jnp.where(neighbours >= 0, 1.0, 0.0), spread, 0, 0)


def shift_planes(planes, valid, shifted):
    cell = lax.broadcasted_iota(jnp.int32, (1, 128), 1)
    q_at, r_at = cell // 4 % 4, cell % 4
    source = ((1, -1), (0, 0), (1, 0), (0, 1))
    for t in range(4):
        j, dq = source[t]
        for u in range(4):
            k, dr = source[u]
            g = 2 * j + k
            block = planes[:, 128 * g : 128 * g + 128]
            shift = -(4 * dq + dr) % 128
            if shift:
                block = pltpu.roll(block, shift, 1)
            if dr:
                inside = jnp.where((r_at + dr < 0) | (r_at + dr > 3), 0.0, 1.0)
            else:
                inside = jnp.ones((1, 128), F32)
            cross = None if dq == 0 else (q_at == 0 if dq < 0 else q_at == 3)
            for a, (lo, hi) in enumerate(((0, 64), (64, 576), (576, 640))):
                keep = inside
                near = valid[9 * a + 4 : 9 * a + 5]
                if cross is not None:
                    col = 9 * a + 3 * (dq + 1) + 1
                    keep = keep * jnp.where(cross, valid[col : col + 1], near)
                elif a != 1:
                    keep = keep * near
                part = block[lo:hi]
                if a != 1 or dq or dr:
                    part = part * keep.astype(part.dtype)
                shifted[t, lo:hi, 128 * u : 128 * u + 128] = part.astype(BF16)


def prepare_kernel(
    place, feat_hbm, occ_hbm, neighbours_hbm, w_conv_hbm, wd_hbm, wp_hbm, own_hbm,
    planes, occ_x, valid, wide, wd_rows, wp, own, beside, across,
    feat, occ, neighbours, w_conv, sems,
):
    copies = []
    for n, (source, target) in enumerate(
        ((feat_hbm, feat), (occ_hbm, occ), (w_conv_hbm, w_conv), (neighbours_hbm, neighbours), (wp_hbm, wp), (own_hbm, own))
    ):
        copies.append(pltpu.make_async_copy(source, target, sems.at[n]))
    for jk in range(4):
        for i in range(2):
            n = 2 * jk + i
            target = wd_rows.at[64 * n : 64 * n + 64]
            copies.append(pltpu.make_async_copy(wd_hbm.at[4 * i + jk], target, sems.at[6 + n]))
    for copy in copies:
        copy.start()
    lane = lax.broadcasted_iota(jnp.int32, (1, 512), 1)
    jj, kk, bb, qq, rr = lane // 256, lane // 128 % 2, lane % 128 // 16, lane // 4 % 4, lane % 4
    voxel = bb * 128 + 8 * (2 * qq + jj) + 2 * rr + kk
    row = lax.broadcasted_iota(jnp.int32, (1024, 512), 0)
    copies[0].wait()
    copies[1].wait()
    occ_f = occ[...].astype(F32).astype(BF16)
    rows = []
    for m in range(4):
        rows.append(jnp.concatenate([feat[b, :, 128 * m : 128 * m + 128] for b in range(8)], axis=1))
    occ_rows = [
        jnp.concatenate([occ_f[b : b + 1, 128 * m : 128 * m + 128] for b in range(8)], axis=1)
        for m in range(4)
    ]
    occ_rows = jnp.concatenate(occ_rows + [jnp.zeros((12, 1024), BF16)], axis=0)
    stacked = jnp.concatenate(rows + [occ_rows], axis=0)
    ends = []
    for e in range(2):
        select = jnp.where(row == voxel + 64 * e, 1.0, 0.0).astype(BF16)
        picked = mm(stacked, select)
        moved = picked[:256].astype(BF16)
        for m in range(4):
            planes[64 * (2 * m + e) : 64 * (2 * m + e + 1), :] = moved[64 * m : 64 * m + 64]
            occ_x[2 * m + e : 2 * m + e + 1] = picked[256 + m : 257 + m]
        ends.append(moved[192 * e : 192 * e + 64])
    even = place[0] == 0
    beside[...] = jnp.where(even, ends[1], ends[0])
    across[...] = jnp.where(even, ends[0], ends[1])
    copies[2].wait()
    first, second = turned_weights(w_conv)
    zero = jnp.zeros((64, 128), BF16)
    for n in range(9):
        cut = slice(256 * n, 256 * n + 256)
        for x in range(4):
            band = (first if x % 2 == 0 else second)[:, cut]
            band = [band, zero] if x < 2 else [zero, band]
            wide[64 * x : 64 * x + 64, 384 * n : 384 * n + 384] = jnp.concatenate(band, axis=1)
    copies[3].wait()
    valid[...] = near_masks(neighbours[...])
    for copy in copies[4:]:
        copy.wait()


def forward_kernel(
    place, inner, occ_x, valid, beside, across, wide, wd, wp,
    shifted, slope_pre, hid, coarse_ref, slope_down, slope_point,
    planes,
):
    planes[64:576] = inner[...]
    odd_core = place[0] == 1
    inner_x = lax.broadcasted_iota(jnp.int32, (64, 128), 1) >= 64
    for g in range(4):
        cut = slice(128 * g, 128 * g + 128)
        before = jnp.where(odd_core, beside[:, cut], across[:, cut])
        after = jnp.where(odd_core, across[:, cut], beside[:, cut])
        planes[0:64, cut] = pltpu.roll(jnp.where(inner_x, before, inner[448:512, cut]), 64, 1)
        planes[576:640, cut] = pltpu.roll(jnp.where(inner_x, inner[0:64, cut], after), 64, 1)
    shift_planes(planes, valid, shifted)
    for h in range(2):
        for j in range(2):
            taps = [
                shifted[j + b, 256 * h : 256 * h + 384, 128 * c : 128 * c + 256]
                for b in range(3)
                for c in range(3)
            ]
            pre = mm(wide[...], jnp.concatenate(taps, axis=0))
            gate = sigmoid(pre)
            for x in range(4):
                sub = slice(64 * x, 64 * x + 64)
                filled = occ_x[4 * h + x : 4 * h + x + 1, 256 * j : 256 * j + 256]
                act, g = pre[sub], gate[sub]
                r0 = 256 * h + 64 * x
                slope_pre[r0 : r0 + 64, 256 * j : 256 * j + 256] = filled * (g * (1.0 + act * (1.0 - g)))
                out = (act * g * filled).astype(BF16)
                p, i = 2 * h + x // 2, x % 2
                for k in range(2):
                    base = 128 * (2 * j + k) + 64 * i
                    hid[base : base + 64, 128 * p : 128 * p + 128] = out[:, 128 * k : 128 * k + 128]
    down = mm(wd[...], hid[...], 0, 0)
    gate = sigmoid(down)
    coarse = (down * gate).astype(BF16)
    coarse_ref[...] = coarse
    slope_down[...] = gate * (1.0 + down * (1.0 - gate))
    point = mm(coarse, wp[...], 0, 0)
    gate = sigmoid(point)
    slope_point[...] = gate * (1.0 + point * (1.0 - gate))


def pick_kernel(place, far_owners, own, beside, across, diagonal, near, reply):
    me = place[3]
    owners = [place[4 + b] for b in range(8)]
    tables = (own, beside, across, diagonal)

    def pick(relation, slot):
        value = own[slot]
        for n in range(1, 4):
            value = jnp.where(relation == n, tables[n][slot], value)
        return value

    for b in range(8):
        near[b] = pick(((owners[b] >> 3) ^ me) & 3, owners[b] & 7)
    for i in range(4):
        slot = jnp.int32(0)
        for b in range(8):
            slot = jnp.where((far_owners[b] >> 3) == (me & 4) + i, far_owners[b] & 7, slot)
        reply[i] = pick((me & 3) ^ i, slot)


def backward_kernel(
    split, place, shifted, slope_pre, hid, coarse, slope_down, slope_point, near, far, wd, wp, wire, wire_conv,
    grads,
):
    def put(target, first, value):
        half, at = divmod(first, target.shape[1])
        side = place[0] if half == 0 else 1 - place[0]
        target[side, at : at + value.shape[0]] = value.astype(BF16)

    parts = []
    for p in range(4):
        for b in range(8):
            part = near[b, 16 * p : 16 * p + 16, :]
            if split:
                target = place[4 + b] >> 3
                other = far[target & 3, 16 * p : 16 * p + 16, :]
                part = jnp.where(((target ^ place[3]) & 4) == 0, part, other)
            parts.append(part)
    cot_rows = jnp.concatenate(parts, axis=0)
    grad_point = (cot_rows.astype(F32) * slope_point[...]).astype(BF16)
    gwp = mm(coarse[...], grad_point)
    put(wire, 512, gwp[:, :128])
    put(wire, 640, gwp[:, 128:])
    grad_coarse = mm(wp[...], grad_point, 1, 1).astype(BF16)
    grad_down = (grad_coarse.astype(F32) * slope_down[...]).astype(BF16)
    gwd = mm(hid[...], grad_down, 1, 1)
    put(wire, 0, gwd[:384])
    put(wire, 384, gwd[384:])
    for jk in range(4):
        grad_hidden = mm(wd[128 * jk : 128 * jk + 128], grad_down)
        for p in range(4):
            cut = slice(128 * jk, 128 * jk + 128)
            value = grad_hidden[:, 128 * p : 128 * p + 128] * slope_pre[128 * p : 128 * p + 128, cut]
            h, base = p // 2, 128 * (p % 2)
            grads[base : base + 128, 512 * h + 128 * jk : 512 * h + 128 * jk + 128] = value.astype(BF16)
    low_lanes = lax.broadcasted_iota(jnp.int32, (64, 128), 1) < 64
    thirds = []
    for n in range(9):
        b, c = divmod(n, 3)
        left = jnp.concatenate(
            [
                shifted[j + b, 256 * h : 256 * h + 384, 128 * c : 128 * c + 256]
                for h in range(2)
                for j in range(2)
            ],
            axis=1,
        )
        band = mm(left, grads[...], 1, 1)
        sums = []
        for a in range(3):
            even = band[64 * a : 64 * a + 64, :128] + band[64 * a + 128 : 64 * a + 192, 128:]
            odd = band[64 * a + 64 : 64 * a + 128, :128] + band[64 * a + 192 : 64 * a + 256, 128:]
            both = jnp.where(low_lanes, even, odd)
            sums.append(both + pltpu.roll(both, 64, 1))
        put(wire_conv, 64 * n, jnp.where(low_lanes, sums[0], sums[1]))
        thirds.append(sums[2])
    for n in range(5):
        put(wire_conv, 64 * (9 + n), jnp.where(low_lanes, thirds[2 * n], thirds[min(2 * n + 1, 8)]))


def rows_of(place, mine, other, first, count):
    half, at = divmod(first, mine.shape[0])
    return jnp.where(place[0] == half, mine[at : at + count], other[at : at + count]).astype(F32)


def finish_coarse_kernel(place, mine, other, gwd, gwp):
    for i in range(2):
        for jk in range(4):
            gwd[4 * i + jk] = rows_of(place, mine, other, 128 * jk + 64 * i, 64)
    for s in range(2):
        gwp[:, 128 * s : 128 * s + 128] = rows_of(place, mine, other, 512 + 128 * s, 128)


def finish_conv_kernel(place, mine, other, gwc):
    for n in range(9):
        pair = rows_of(place, mine, other, 64 * n, 64)
        gwc[n] = pair[:, :64]
        gwc[9 + n] = pair[:, 64:]
    for n in range(5):
        pair = rows_of(place, mine, other, 64 * (9 + n), 64)
        gwc[18 + 2 * n] = pair[:, :64]
        if n < 4:
            gwc[19 + 2 * n] = pair[:, 64:]


def call(kernel, outs, ins, scratch=(), limit=24 * 2**20, flops=0, specs=None):
    return pl.pallas_call(
        kernel,
        out_shape=outs,
        in_specs=specs or [VMEM] * len(ins),
        out_specs=jax.tree.map(lambda _: VMEM, outs),
        scratch_shapes=scratch,
        compiler_params=pltpu.CompilerParams(vmem_limit_bytes=limit),
        cost_estimate=pl.CostEstimate(flops=flops, bytes_accessed=2**20, transcendentals=0),
    )(*ins)


def in_hbm(*arrays):
    return [pltpu.with_memory_space_constraint(array, pltpu.HBM) for array in arrays]


def swap(value, axis, bit):
    size = lax.axis_size(axis)
    return lax.ppermute(value, axis, [(i, i ^ bit) for i in range(size)])


def powers(size, first):
    bits = []
    while first < size:
        bits.append(first)
        first *= 2
    return bits


def shards(features, occupancy, neighbours, owners, w_conv, w_down, w_point, cotangent):
    brick_size = lax.axis_size("brick")
    shape = jax.ShapeDtypeStruct
    me = lax.axis_index("brick")
    core = me & 1
    dp_at = lax.axis_index("dp")
    feat = jnp.swapaxes(features[0], 1, 2)
    slots, own = owners[0], cotangent[0]
    split = brick_size == 8
    place = jnp.concatenate([jnp.stack([core, dp_at & 1, dp_at >> 1, me]).astype(jnp.int32), slots])
    prepared = call(
        prepare_kernel,
        (
            shape((512, 512), BF16),
            shape((8, 512), F32),
            shape((27, 128), F32),
            shape((256, 3456), BF16),
            shape((512, 128), BF16),
            shape((128, 256), BF16),
            shape((8, 64, 256), BF16),
            shape((64, 512), BF16),
            shape((64, 512), BF16),
        ),
        (place, *in_hbm(feat, occupancy[0], neighbours[0], w_conv.reshape(27, 64, 64), w_down.reshape(8, 64, 128), w_point, own)),
        scratch=[
            pltpu.VMEM((8, 64, 512), BF16),
            pltpu.VMEM((8, 512), jnp.int32),
            pltpu.VMEM((8, 27), jnp.int32),
            pltpu.VMEM((27, 64, 64), BF16),
            pltpu.SemaphoreType.DMA((14,)),
        ],
        flops=4 * 10**9,
        specs=[SMEM] + [HBM] * 7,
    )
    planes, occ_x, valid, wide, wd, wp, own_copy, beside, across = prepared
    beside = swap(beside, "brick", 1)
    chips = [(i, i + 1) for i in range(1, brick_size - 1, 2)]
    across = lax.ppermute(across, "brick", chips + [(j, i) for i, j in chips])
    if split:
        partner, far_slots, planes = lax.optimization_barrier((swap(own, "brick", 2), swap(slots, "brick", 4), planes))
        tables = (own_copy, swap(own, "brick", 1), partner, swap(partner, "brick", 1))
        near, reply = call(
            pick_kernel,
            (shape((8, 64, 256), BF16), shape((4, 64, 256), BF16)),
            (place, far_slots, *tables),
            specs=[SMEM] * 2 + [VMEM] * 4,
        )
        far = swap(reply, "brick", 4)
    else:
        wanted = jnp.arange(brick_size, dtype=jnp.int32)[:, None] == (slots >> 3)[None, :]
        request = jnp.max(jnp.where(wanted, (slots & 7)[None, :], 0), axis=1)
        arrived = lax.all_to_all(request, "brick", split_axis=0, concat_axis=0, tiled=True)
        reply = jnp.take(own, arrived, axis=0, mode="clip")
        fetched = lax.all_to_all(reply, "brick", split_axis=0, concat_axis=0, tiled=True)
        near = jnp.take(fetched, slots >> 3, axis=0, mode="clip")
        far = near[:4]
    saved = call(
        forward_kernel,
        (
            shape((4, 640, 512), BF16),
            shape((512, 512), F32),
            shape((512, 512), BF16),
            shape((128, 512), BF16),
            shape((128, 512), F32),
            shape((512, 256), F32),
        ),
        (place, planes, occ_x, valid, beside, across, wide, wd, wp),
        scratch=[pltpu.VMEM((640, 512), BF16)],
        flops=4 * 10**9,
        specs=[SMEM] + [VMEM] * 8,
    )
    wires = call(
        functools.partial(backward_kernel, split),
        (shape((2, COARSE_HALF, 128), BF16), shape((2, CONV_HALF, 128), BF16)),
        (place, *saved, near, far, wd, wp),
        scratch=[pltpu.VMEM((256, 1024), BF16)],
        flops=4 * 10**9,
        specs=[SMEM] + [VMEM] * 10,
    )
    bits = powers(brick_size, 4)[::-1]
    far_steps = [("brick", bit) for bit in bits]
    orders = (far_steps + [("dp", 1), ("brick", 2), ("dp", 2)], [("dp", 1)] + far_steps + [("dp", 2), ("brick", 2)])
    sums = [wire[0] + swap(wire[1], "brick", 1) for wire in wires]
    for n in range(len(orders[0])):
        for s in range(2):
            sums[s] = sums[s] + swap(sums[s], *orders[s][n])
    others = [swap(total, "brick", 1) for total in sums]
    specs = [SMEM, VMEM, VMEM]
    gwd, gwp = call(
        finish_coarse_kernel,
        (shape((8, 64, 128), F32), shape((128, 256), F32)),
        (place, sums[0], others[0]),
        specs=specs,
    )
    gwc = call(finish_conv_kernel, shape((27, 64, 64), F32), (place, sums[1], others[1]), specs=specs)
    return gwc.reshape(3, 3, 3, 64, 64), gwd.reshape(2, 2, 2, 64, 128), gwp


def solution(mesh):
    in_specs = (
        P("dp", "brick", None, None),
        P("dp", "brick", None),
        P("dp", "brick", None),
        P("dp", "brick"),
        P(),
        P(),
        P(),
        P("dp", "brick", None, None),
    )
    out_specs = (P(), P(), P())
    return jax.shard_map(shards, mesh=mesh, in_specs=in_specs, out_specs=out_specs, check_vma=False)
```

time: 75.3 us -> 59.1 us (0.78)
  local copies, waits for them, and re-layouts: 12.2 us -> 0.78 us
  Pallas kernels: 8.41 us -> 13.8 us
  waiting for transfers between devices: 28.5 us -> 24.8 us
  starting transfers between devices: 21.8 us -> 18.5 us
  other arithmetic: 2.96 us -> 0.28 us
    all_to_all x2 -> x0, starting transfers between devices: 12.4 us -> none  [the longest x1 8.24 us: shards(): lax.all_to_all(request, 'brick', split_axis=0, concat_axis=0, tiled=True)]
    ppermute x8 -> x18, starting transfers between devices: 5.83 us -> 17.9 us  [swap(): return lax.ppermute(value, axis, [(i, i ^ bit) for i in range(size)])]
    unnamed x20 -> x0, local copies, waits for them, and re-layouts: 6.46 us -> none
    pallas_call x3 -> x6, Pallas kernels: 8.41 us -> 13.8 us  [call(): pl.pallas_call(kernel, out_shape=outs, in_specs=specs or [VMEM] * len(ins...]
    all_to_all x2 -> x0, waiting for transfers between devices: 3.71 us -> none  [the longest x1 2.73 us: shards(): lax.all_to_all(reply, 'brick', split_axis=0, concat_axis=0, tiled=True)]
    ppermute x2 -> x1, starting transfers between devices: 3.65 us -> 0.65 us  [shards(): across = lax.ppermute(across, 'brick', chips + [(j, i) for i, j in chips])]
    slice x6 -> x0, local copies, waits for them, and re-layouts: 2.57 us -> none  [the longest x2 1.31 us: shards(): turned[0]]
    gather x1 -> x0, local copies, waits for them, and re-layouts: 1.27 us -> none  [shards(): reply = jnp.take(cotangent[0], arrived, axis=0, mode='clip')]
  transfers between devices with their start and end apart: 12 -> 19, of which waited for: 10 -> 13; matrix products, arithmetic and copies ran while one was open for 10% -> 2% of each run, Pallas kernels for 5% -> 15%
where the time goes in v2:
time: 59.1 us; the launch traced here: 58.9 us
  waiting for transfers between devices  24.8 us (42%)
  starting transfers between devices  18.5 us (31%)
  Pallas kernels  13.8 us (23%)
  local copies, waits for them, and re-layouts  0.78 us (1%)
  between operations  0.78 us (1%)
    ppermute x18, waiting for transfers between devices, swap(): return lax.ppermute(value, axis, [(i, i ^ bit) for i in range(size)])  24.8 us
    ppermute x18, starting transfers between devices, swap(): return lax.ppermute(value, axis, [(i, i ^ bit) for i in range(size)])  17.9 us
    pallas_call x6, Pallas kernels, call(): pl.pallas_call(kernel, out_shape=outs, in_specs=specs or [VMEM] * len(ins...  13.8 us
  transfers between devices with their start and end apart: 19, of which 13 were waited for; matrix products, arithmetic and copies ran while one was open for 2% of the time, Pallas kernels for 15%

profile of v2, /device:TPU:0, one launch (start us, length us, event | category | flops | bytes accessed | tf_op | source)
XLA Modules:
  0.0 58.9 jit_solution(6264065480867388928)
XLA Ops:
  0.6 0.5 collective-permute-start.4
  1.1 2.7 %collective-permute-start = (bf16[8,64,256]{2,1,0:T(8,128)(2,1)}, bf16[8,64,256]{2,1,0:T(8,128)(2,1)S(1)}, u32[]{:S(2)}, u32[]{:S(2)}) collective-permute-start(bf16[8,64,256]{2,1,0:T(8,128)(2,1)} %bitcast.29), channel_id=1, source_target_pairs={{0,2},{1,3},{2,0},{3,1},{4,6},{5,7},{6,4},{7,5},{8,10},{9,11},{10,... | collective-permute-start | bytes 786440 | tf_op jit(solution)/shard_map/ppermute | solution.py:303
  3.8 2.6 %collective-permute-start.1 = (s32[8]{0:T(128)}, s32[8]{0:T(128)S(1)}, u32[]{:S(2)}, u32[]{:S(2)}) collective-permute-start(s32[8]{0:T(128)} %bitcast.24), channel_id=1, source_target_pairs={{0,4},{1,5},{2,6},{3,7},{4,0},{5,1},{6,2},{7,3},{8,12},{9,13},{10,... | collective-permute-start | bytes 104 | tf_op jit(solution)/shard_map/ppermute | solution.py:303
  6.4 0.8 %concatenate.3.place = s32[12]{0:T(128)S(1)} concatenate(s32[1]{0:T(128)} %bitcast, s32[1]{0:T(128)} %bitcast.1, s32[1]{0:T(128)} %bitcast.2, s32[1]{0:T(128)} %bitcast.3, s32[8]{0:T(128)} %bitcast.25), dimensions={0} | concatenate | bytes 96 | tf_op jit(solution)/shard_map/concatenate | solution.py:323
  7.2 3.2 %shard_map.103 = (bf16[512,512]{1,0:T(8,128)(2,1)S(1)}, f32[8,512]{1,0:T(8,128)S(1)}, f32[27,128]{1,0:T(8,128)S(1)}, bf16[256,3456]{1,0:T(8,128)(2,1)S(1)}, bf16...) custom-call(s32[12]{0:T(128)S(1)} %concatenate.3.place, ...), custom_call_target="tpu_custom_call" | custom-call | flops 4000000000 | bytes 1048576 | tf_op jit(solution)/shard_map/pallas_call | solution.py:286
  10.4 0.0 collective-permute-done.1.far_owners
  10.4 0.5 collective-permute-done.across
  10.9 0.0 collective-permute-start.5
  10.9 0.5 collective-permute-start.2
  11.4 0.7 %collective-permute-start.3 = (bf16[64,512]{1,0:T(8,128)(2,1)S(1)}, bf16[64,512]{1,0:T(8,128)(2,1)S(1)}, u32[]{:S(2)}, u32[]{:S(2)}) collective-permute-start(bf16[64,512]{1,0:T(8,128)(2,1)S(1)} %get-tuple-element.32), channel_id=1, source_target_pairs={{1,2},{3,4},{5,6},{2,1},{4,3},{6,5},{9,10},{11,12},{13,14},{10,9},... | collective-permute-start | bytes 196616 | tf_op jit(solution)/shard_map/ppermute | solution.py:351
  12.1 0.0 collective-permute-done.4.beside
  12.1 0.4 collective-permute-done.5.diagonal
  12.5 0.7 %shard_map.105 = (bf16[8,64,256]{2,1,0:T(8,128)(2,1)S(1)}, bf16[4,64,256]{2,1,0:T(8,128)(2,1)S(1)}) custom-call(s32[12]{0:T(128)S(1)} %concatenate.3.place, s32[8]{0:T(128)S(1)} %collective-permute-done.1.far_owners, bf16[8,64,256]{2,1,0:T(8,128)(2,1)S(1)} %get-tuple-element.43.own, bf16[8,64,256]{2,1,0:T(8,128)(2,1)S(1)} %collective-permute-done.4.beside, ...), custom_call_target="tpu_custom_call" | custom-call | bytes 1048576 | tf_op jit(solution)/shard_map/pallas_call | solution.py:286
  13.1 4.8 %collective-permute-start.6 = (bf16[4,64,256]{2,1,0:T(8,128)(2,1)S(1)}, bf16[4,64,256]{2,1,0:T(8,128)(2,1)S(1)}, u32[]{:S(2)}, u32[]{:S(2)}) collective-permute-start(bf16[4,64,256]{2,1,0:T(8,128)(2,1)S(1)} %get-tuple-element.46), channel_id=1, source_target_pairs={{0,4},{1,5},{2,6},{3,7},{4,0},{5,1},{6,2},{7,3},{8,12},{9,13},{10,... | collective-permute-start | bytes 393224 | tf_op jit(solution)/shard_map/ppermute | solution.py:303
  17.9 0.0 collective-permute-done.2.beside
  17.9 0.0 collective-permute-done.3.across
  17.9 3.7 %shard_map.104 = (bf16[4,640,512]{2,1,0:T(8,128)(2,1)S(1)}, f32[512,512]{1,0:T(8,128)S(1)}, bf16[512,512]{1,0:T(8,128)(2,1)S(1)}, bf16[128,512]{1,0:T(8,128)(2,1...) custom-call(s32[12]{0:T(128)S(1)} %concatenate.3.place, bf16[512,512]{1,0:T(8,128)(2,1)S(1)} %get-tuple-element.28.inner, ...), custom_call_target="tpu_custom_call" | custom-call | flops 4000000000 | bytes 1048576 | tf_op jit(solution)/shard_map/pallas_call | solution.py:286
  21.6 2.4 %collective-permute-done.6.far = bf16[4,64,256]{2,1,0:T(8,128)(2,1)S(1)} collective-permute-done((bf16[4,64,256]{2,1,0:T(8,128)(2,1)S(1)}, bf16[4,64,256]{2,1,0:T(8,128)(2,1)S(1)}, u32[]{:S(2)}, u32[]{:S(2)}) %collective-permute-start.6) | collective-permute-done | bytes 131104 | tf_op jit(solution)/shard_map/ppermute | solution.py:303
  24.1 3.3 %shard_map.106 = (bf16[2,384,128]{2,1,0:T(8,128)(2,1)S(1)}, bf16[2,448,128]{2,1,0:T(8,128)(2,1)S(1)}) custom-call(s32[12]{0:T(128)S(1)} %concatenate.3.place, bf16[4,640,512]{2,1,0:T(8,128)(2,1)S(1)} %get-tuple-element.36.shifted, f32[512,512]{1,0:T(8,128)S(1)} %get-tuple-element.37.slope_pre, bf16[512,512]{1,0:T(8,128)(2,1)S(1)} %get-tuple-element.38.hid, ...), custom_call_target="tpu_custom_call" | custom-call | flops 4000000000 | bytes 1048576 | tf_op jit(solution)/shard_map/pallas_call | solution.py:286
  27.4 0.9 %collective-permute-start.7 = (bf16[448,128]{1,0:T(8,128)(2,1)S(1)}, bf16[448,128]{1,0:T(8,128)(2,1)S(1)}, u32[]{:S(2)}, u32[]{:S(2)}) collective-permute-start(bf16[448,128]{1,0:T(8,128)(2,1)S(1)} %slice_bitcast_fusion), channel_id=1, source_target_pairs={{0,1},{1,0},{2,3},{3,2},{4,5},{5,4},{6,7},{7,6},{8,9},{9,8},{10,11... | collective-permute-start | bytes 344072 | tf_op jit(solution)/shard_map/ppermute | solution.py:303
  28.3 0.1 collective-permute-start.13
  28.4 0.9 %collective-permute-done.7 = bf16[448,128]{1,0:T(8,128)(2,1)S(1)} collective-permute-done((bf16[448,128]{1,0:T(8,128)(2,1)S(1)}, bf16[448,128]{1,0:T(8,128)(2,1)S(1)}, u32[]{:S(2)}, u32[]{:S(2)}) %collective-permute-start.7) | collective-permute-done | bytes 114720 | tf_op jit(solution)/shard_map/ppermute | solution.py:303
  29.2 1.6 %collective-permute-start.8 = (bf16[448,128]{1,0:T(8,128)(2,1)S(1)}, bf16[448,128]{1,0:T(8,128)(2,1)S(1)}, u32[]{:S(2)}, u32[]{:S(2)}) collective-permute-start(bf16[448,128]{1,0:T(8,128)(2,1)S(1)} %bitcast_add_fusion), channel_id=1, source_target_pairs={{0,8},{8,0},{16,24},{24,16},{1,9},{9,1},{17,25},{25,17},{2,10},{10... | collective-permute-start | bytes 344072 | tf_op jit(solution)/shard_map/ppermute | solution.py:303
  30.8 0.0 collective-permute-done.13
  30.8 0.5 collective-permute-start.14
  31.3 3.4 %collective-permute-done.8 = bf16[448,128]{1,0:T(8,128)(2,1)S(1)} collective-permute-done((bf16[448,128]{1,0:T(8,128)(2,1)S(1)}, bf16[448,128]{1,0:T(8,128)(2,1)S(1)}, u32[]{:S(2)}, u32[]{:S(2)}) %collective-permute-start.8) | collective-permute-done | bytes 114720 | tf_op jit(solution)/shard_map/ppermute | solution.py:303
  34.8 0.3 collective-permute-start.9
  35.0 5.4 %collective-permute-done.14 = bf16[384,128]{1,0:T(8,128)(2,1)S(1)} collective-permute-done((bf16[384,128]{1,0:T(8,128)(2,1)S(1)}, bf16[384,128]{1,0:T(8,128)(2,1)S(1)}, u32[]{:S(2)}, u32[]{:S(2)}) %collective-permute-start.14) | collective-permute-done | bytes 98336 | tf_op jit(solution)/shard_map/ppermute | solution.py:303
  40.5 0.1 collective-permute-start.15
  40.5 2.3 %collective-permute-done.9 = bf16[448,128]{1,0:T(8,128)(2,1)S(1)} collective-permute-done((bf16[448,128]{1,0:T(8,128)(2,1)S(1)}, bf16[448,128]{1,0:T(8,128)(2,1)S(1)}, u32[]{:S(2)}, u32[]{:S(2)}) %collective-permute-start.9) | collective-permute-done | bytes 114720 | tf_op jit(solution)/shard_map/ppermute | solution.py:303
  42.8 1.6 %collective-permute-start.10 = (bf16[448,128]{1,0:T(8,128)(2,1)S(1)}, bf16[448,128]{1,0:T(8,128)(2,1)S(1)}, u32[]{:S(2)}, u32[]{:S(2)}) collective-permute-start(bf16[448,128]{1,0:T(8,128)(2,1)S(1)} %add.32), channel_id=1, source_target_pairs={{0,16},{8,24},{16,0},{24,8},{1,17},{9,25},{17,1},{25,9},{2,18},{10... | collective-permute-start | bytes 344072 | tf_op jit(solution)/shard_map/ppermute | solution.py:303
  44.4 0.7 %collective-permute-done.15 = bf16[384,128]{1,0:T(8,128)(2,1)S(1)} collective-permute-done((bf16[384,128]{1,0:T(8,128)(2,1)S(1)}, bf16[384,128]{1,0:T(8,128)(2,1)S(1)}, u32[]{:S(2)}, u32[]{:S(2)}) %collective-permute-start.15) | collective-permute-done | bytes 98336 | tf_op jit(solution)/shard_map/ppermute | solution.py:303
  45.2 0.1 collective-permute-start.16
  45.3 2.7 %collective-permute-done.10 = bf16[448,128]{1,0:T(8,128)(2,1)S(1)} collective-permute-done((bf16[448,128]{1,0:T(8,128)(2,1)S(1)}, bf16[448,128]{1,0:T(8,128)(2,1)S(1)}, u32[]{:S(2)}, u32[]{:S(2)}) %collective-permute-start.10) | collective-permute-done | bytes 114720 | tf_op jit(solution)/shard_map/ppermute | solution.py:303
  48.0 0.1 collective-permute-start.11
  48.1 1.8 %collective-permute-done.16 = bf16[384,128]{1,0:T(8,128)(2,1)S(1)} collective-permute-done((bf16[384,128]{1,0:T(8,128)(2,1)S(1)}, bf16[384,128]{1,0:T(8,128)(2,1)S(1)}, u32[]{:S(2)}, u32[]{:S(2)}) %collective-permute-start.16) | collective-permute-done | bytes 98336 | tf_op jit(solution)/shard_map/ppermute | solution.py:303
  49.9 1.6 %collective-permute-start.17 = (bf16[384,128]{1,0:T(8,128)(2,1)S(1)}, bf16[384,128]{1,0:T(8,128)(2,1)S(1)}, u32[]{:S(2)}, u32[]{:S(2)}) collective-permute-start(bf16[384,128]{1,0:T(8,128)(2,1)S(1)} %add.38), channel_id=1, source_target_pairs={{0,16},{8,24},{16,0},{24,8},{1,17},{9,25},{17,1},{25,9},{2,18},{10... | collective-permute-start | bytes 294920 | tf_op jit(solution)/shard_map/ppermute | solution.py:303
  51.5 1.4 %collective-permute-done.11 = bf16[448,128]{1,0:T(8,128)(2,1)S(1)} collective-permute-done((bf16[448,128]{1,0:T(8,128)(2,1)S(1)}, bf16[448,128]{1,0:T(8,128)(2,1)S(1)}, u32[]{:S(2)}, u32[]{:S(2)}) %collective-permute-start.11) | collective-permute-done | bytes 114720 | tf_op jit(solution)/shard_map/ppermute | solution.py:303
  52.9 0.1 collective-permute-start.12
  53.0 1.6 %collective-permute-done.17 = bf16[384,128]{1,0:T(8,128)(2,1)S(1)} collective-permute-done((bf16[384,128]{1,0:T(8,128)(2,1)S(1)}, bf16[384,128]{1,0:T(8,128)(2,1)S(1)}, u32[]{:S(2)}, u32[]{:S(2)}) %collective-permute-start.17) | collective-permute-done | bytes 98336 | tf_op jit(solution)/shard_map/ppermute | solution.py:303
  54.7 0.1 collective-permute-start.18
  54.7 1.3 %collective-permute-done.18.other = bf16[384,128]{1,0:T(8,128)(2,1)S(1)} collective-permute-done((bf16[384,128]{1,0:T(8,128)(2,1)S(1)}, bf16[384,128]{1,0:T(8,128)(2,1)S(1)}, u32[]{:S(2)}, u32[]{:S(2)}) %collective-permute-start.18) | collective-permute-done | bytes 98336 | tf_op jit(solution)/shard_map/ppermute | solution.py:303
  56.0 1.3 %shard_map.108 = (f32[8,64,128]{2,1,0:T(8,128)}, f32[128,256]{1,0:T(8,128)}) custom-call(s32[12]{0:T(128)S(1)} %concatenate.3.place, bf16[384,128]{1,0:T(8,128)(2,1)S(1)} %add.39.mine, bf16[384,128]{1,0:T(8,128)(2,1)S(1)} %collective-permute-done.18.other), custom_call_target="tpu_custom_call" | custom-call | bytes 1048576 | tf_op jit(solution)/shard_map/pallas_call | solution.py:286
  57.3 0.0 collective-permute-done.12.other
  57.3 1.6 %shard_map.107 = f32[27,64,64]{2,1,0:T(8,128)} custom-call(s32[12]{0:T(128)S(1)} %concatenate.3.place, bf16[448,128]{1,0:T(8,128)(2,1)S(1)} %add.34.mine, bf16[448,128]{1,0:T(8,128)(2,1)S(1)} %collective-permute-done.12.other), custom_call_target="tpu_custom_call" | custom-call | bytes 1048576 | tf_op jit(solution)/shard_map/pallas_call | solution.py:286
  (12 shorter events, 0.3 us)
Async XLA Ops:
  0.6 11.5 %collective-permute-start.4 = (bf16[8,64,256]{2,1,0:T(8,128)(2,1)}, bf16[8,64,256]{2,1,0:T(8,128)(2,1)S(1)}, u32[]{:S(2)}, u32[]{:S(2)}) collective-permute-start(bf16[8,64,256]{2,1,0:T(8,128)(2,1)} %bitcast.28), channel_id=1, source_target_pairs={{0,1},{1,0},{2,3},{3,2},{4,5},{5,4},{6,7},{7,6},{8,9},{9,8},{10,11... | collective-permute-start | bytes 786440 | tf_op jit(solution)/shard_map/ppermute | solution.py:303
  1.1 9.8 %collective-permute-start = (bf16[8,64,256]{2,1,0:T(8,128)(2,1)}, bf16[8,64,256]{2,1,0:T(8,128)(2,1)S(1)}, u32[]{:S(2)}, u32[]{:S(2)}) collective-permute-start(bf16[8,64,256]{2,1,0:T(8,128)(2,1)} %bitcast.29), channel_id=1, source_target_pairs={{0,2},{1,3},{2,0},{3,1},{4,6},{5,7},{6,4},{7,5},{8,10},{9,11},{10,... | collective-permute-start | bytes 786440 | tf_op jit(solution)/shard_map/ppermute | solution.py:303
  3.8 6.6 %collective-permute-start.1 = (s32[8]{0:T(128)}, s32[8]{0:T(128)S(1)}, u32[]{:S(2)}, u32[]{:S(2)}) collective-permute-start(s32[8]{0:T(128)} %bitcast.24), channel_id=1, source_target_pairs={{0,4},{1,5},{2,6},{3,7},{4,0},{5,1},{6,2},{7,3},{8,12},{9,13},{10,... | collective-permute-start | bytes 104 | tf_op jit(solution)/shard_map/ppermute | solution.py:303
  10.9 1.5 %collective-permute-start.5 = (bf16[8,64,256]{2,1,0:T(8,128)(2,1)S(1)}, bf16[8,64,256]{2,1,0:T(8,128)(2,1)S(1)}, u32[]{:S(2)}, u32[]{:S(2)}) collective-permute-start(bf16[8,64,256]{2,1,0:T(8,128)(2,1)S(1)} %collective-permute-done.across), channel_id=1, source_target_pairs={{0,1},{1,0},{2,3},{3,2},{4,5},{5,4},{6,7},{7,6},{8,9},{9,8},{10,11... | collective-permute-start | bytes 786440 | tf_op jit(solution)/shard_map/ppermute | solution.py:303
  10.9 7.0 %collective-permute-start.2 = (bf16[64,512]{1,0:T(8,128)(2,1)S(1)}, bf16[64,512]{1,0:T(8,128)(2,1)S(1)}, u32[]{:S(2)}, u32[]{:S(2)}) collective-permute-start(bf16[64,512]{1,0:T(8,128)(2,1)S(1)} %get-tuple-element.31), channel_id=1, source_target_pairs={{0,1},{1,0},{2,3},{3,2},{4,5},{5,4},{6,7},{7,6},{8,9},{9,8},{10,11... | collective-permute-start | bytes 196616 | tf_op jit(solution)/shard_map/ppermute | solution.py:303
  11.4 6.5 %collective-permute-start.3 = (bf16[64,512]{1,0:T(8,128)(2,1)S(1)}, bf16[64,512]{1,0:T(8,128)(2,1)S(1)}, u32[]{:S(2)}, u32[]{:S(2)}) collective-permute-start(bf16[64,512]{1,0:T(8,128)(2,1)S(1)} %get-tuple-element.32), channel_id=1, source_target_pairs={{1,2},{3,4},{5,6},{2,1},{4,3},{6,5},{9,10},{11,12},{13,14},{10,9},... | collective-permute-start | bytes 196616 | tf_op jit(solution)/shard_map/ppermute | solution.py:351
  13.1 11.0 %collective-permute-start.6 = (bf16[4,64,256]{2,1,0:T(8,128)(2,1)S(1)}, bf16[4,64,256]{2,1,0:T(8,128)(2,1)S(1)}, u32[]{:S(2)}, u32[]{:S(2)}) collective-permute-start(bf16[4,64,256]{2,1,0:T(8,128)(2,1)S(1)} %get-tuple-element.46), channel_id=1, source_target_pairs={{0,4},{1,5},{2,6},{3,7},{4,0},{5,1},{6,2},{7,3},{8,12},{9,13},{10,... | collective-permute-start | bytes 393224 | tf_op jit(solution)/shard_map/ppermute | solution.py:303
  27.4 1.8 %collective-permute-start.7 = (bf16[448,128]{1,0:T(8,128)(2,1)S(1)}, bf16[448,128]{1,0:T(8,128)(2,1)S(1)}, u32[]{:S(2)}, u32[]{:S(2)}) collective-permute-start(bf16[448,128]{1,0:T(8,128)(2,1)S(1)} %slice_bitcast_fusion), channel_id=1, source_target_pairs={{0,1},{1,0},{2,3},{3,2},{4,5},{5,4},{6,7},{7,6},{8,9},{9,8},{10,11... | collective-permute-start | bytes 344072 | tf_op jit(solution)/shard_map/ppermute | solution.py:303
  28.3 2.5 %collective-permute-start.13 = (bf16[384,128]{1,0:T(8,128)(2,1)S(1)}, bf16[384,128]{1,0:T(8,128)(2,1)S(1)}, u32[]{:S(2)}, u32[]{:S(2)}) collective-permute-start(bf16[384,128]{1,0:T(8,128)(2,1)S(1)} %slice_bitcast_fusion.1), channel_id=1, source_target_pairs={{0,1},{1,0},{2,3},{3,2},{4,5},{5,4},{6,7},{7,6},{8,9},{9,8},{10,11... | collective-permute-start | bytes 294920 | tf_op jit(solution)/shard_map/ppermute | solution.py:303
  29.2 5.5 %collective-permute-start.8 = (bf16[448,128]{1,0:T(8,128)(2,1)S(1)}, bf16[448,128]{1,0:T(8,128)(2,1)S(1)}, u32[]{:S(2)}, u32[]{:S(2)}) collective-permute-start(bf16[448,128]{1,0:T(8,128)(2,1)S(1)} %bitcast_add_fusion), channel_id=1, source_target_pairs={{0,8},{8,0},{16,24},{24,16},{1,9},{9,1},{17,25},{25,17},{2,10},{10... | collective-permute-start | bytes 344072 | tf_op jit(solution)/shard_map/ppermute | solution.py:303
  30.8 9.6 %collective-permute-start.14 = (bf16[384,128]{1,0:T(8,128)(2,1)S(1)}, bf16[384,128]{1,0:T(8,128)(2,1)S(1)}, u32[]{:S(2)}, u32[]{:S(2)}) collective-permute-start(bf16[384,128]{1,0:T(8,128)(2,1)S(1)} %bitcast_add_fusion.1), channel_id=1, source_target_pairs={{0,4},{1,5},{2,6},{3,7},{4,0},{5,1},{6,2},{7,3},{8,12},{9,13},{10,... | collective-permute-start | bytes 294920 | tf_op jit(solution)/shard_map/ppermute | solution.py:303
  34.8 8.1 %collective-permute-start.9 = (bf16[448,128]{1,0:T(8,128)(2,1)S(1)}, bf16[448,128]{1,0:T(8,128)(2,1)S(1)}, u32[]{:S(2)}, u32[]{:S(2)}) collective-permute-start(bf16[448,128]{1,0:T(8,128)(2,1)S(1)} %add.31), channel_id=1, source_target_pairs={{0,4},{1,5},{2,6},{3,7},{4,0},{5,1},{6,2},{7,3},{8,12},{9,13},{10,... | collective-permute-start | bytes 344072 | tf_op jit(solution)/shard_map/ppermute | solution.py:303
  40.5 4.7 %collective-permute-start.15 = (bf16[384,128]{1,0:T(8,128)(2,1)S(1)}, bf16[384,128]{1,0:T(8,128)(2,1)S(1)}, u32[]{:S(2)}, u32[]{:S(2)}) collective-permute-start(bf16[384,128]{1,0:T(8,128)(2,1)S(1)} %add.36), channel_id=1, source_target_pairs={{0,8},{8,0},{16,24},{24,16},{1,9},{9,1},{17,25},{25,17},{2,10},{10... | collective-permute-start | bytes 294920 | tf_op jit(solution)/shard_map/ppermute | solution.py:303
  42.8 5.1 %collective-permute-start.10 = (bf16[448,128]{1,0:T(8,128)(2,1)S(1)}, bf16[448,128]{1,0:T(8,128)(2,1)S(1)}, u32[]{:S(2)}, u32[]{:S(2)}) collective-permute-start(bf16[448,128]{1,0:T(8,128)(2,1)S(1)} %add.32), channel_id=1, source_target_pairs={{0,16},{8,24},{16,0},{24,8},{1,17},{9,25},{17,1},{25,9},{2,18},{10... | collective-permute-start | bytes 344072 | tf_op jit(solution)/shard_map/ppermute | solution.py:303
  45.2 4.7 %collective-permute-start.16 = (bf16[384,128]{1,0:T(8,128)(2,1)S(1)}, bf16[384,128]{1,0:T(8,128)(2,1)S(1)}, u32[]{:S(2)}, u32[]{:S(2)}) collective-permute-start(bf16[384,128]{1,0:T(8,128)(2,1)S(1)} %add.37), channel_id=1, source_target_pairs={{0,2},{1,3},{2,0},{3,1},{4,6},{5,7},{6,4},{7,5},{8,10},{9,11},{10,... | collective-permute-start | bytes 294920 | tf_op jit(solution)/shard_map/ppermute | solution.py:303
  48.0 4.9 %collective-permute-start.11 = (bf16[448,128]{1,0:T(8,128)(2,1)S(1)}, bf16[448,128]{1,0:T(8,128)(2,1)S(1)}, u32[]{:S(2)}, u32[]{:S(2)}) collective-permute-start(bf16[448,128]{1,0:T(8,128)(2,1)S(1)} %add.33), channel_id=1, source_target_pairs={{0,2},{1,3},{2,0},{3,1},{4,6},{5,7},{6,4},{7,5},{8,10},{9,11},{10,... | collective-permute-start | bytes 344072 | tf_op jit(solution)/shard_map/ppermute | solution.py:303
  49.9 4.7 %collective-permute-start.17 = (bf16[384,128]{1,0:T(8,128)(2,1)S(1)}, bf16[384,128]{1,0:T(8,128)(2,1)S(1)}, u32[]{:S(2)}, u32[]{:S(2)}) collective-permute-start(bf16[384,128]{1,0:T(8,128)(2,1)S(1)} %add.38), channel_id=1, source_target_pairs={{0,16},{8,24},{16,0},{24,8},{1,17},{9,25},{17,1},{25,9},{2,18},{10... | collective-permute-start | bytes 294920 | tf_op jit(solution)/shard_map/ppermute | solution.py:303
  52.9 4.4 %collective-permute-start.12 = (bf16[448,128]{1,0:T(8,128)(2,1)S(1)}, bf16[448,128]{1,0:T(8,128)(2,1)S(1)}, u32[]{:S(2)}, u32[]{:S(2)}) collective-permute-start(bf16[448,128]{1,0:T(8,128)(2,1)S(1)} %add.34.mine), channel_id=1, source_target_pairs={{0,1},{1,0},{2,3},{3,2},{4,5},{5,4},{6,7},{7,6},{8,9},{9,8},{10,11... | collective-permute-start | bytes 344072 | tf_op jit(solution)/shard_map/ppermute | solution.py:303
  54.7 1.4 %collective-permute-start.18 = (bf16[384,128]{1,0:T(8,128)(2,1)S(1)}, bf16[384,128]{1,0:T(8,128)(2,1)S(1)}, u32[]{:S(2)}, u32[]{:S(2)}) collective-permute-start(bf16[384,128]{1,0:T(8,128)(2,1)S(1)} %add.39.mine), channel_id=1, source_target_pairs={{0,1},{1,0},{2,3},{3,2},{4,5},{5,4},{6,7},{7,6},{8,9},{9,8},{10,11... | collective-permute-start | bytes 294920 | tf_op jit(solution)/shard_map/ppermute | solution.py:303

commit v3 on v2

--- a/solution.py
+++ b/solution.py
@@ -13,7 +13,8 @@
 VMEM = pl.BlockSpec(memory_space=pltpu.VMEM)
 HBM = pl.BlockSpec(memory_space=pltpu.HBM)
 SMEM = pl.BlockSpec(memory_space=pltpu.SMEM)
-COARSE_HALF, CONV_HALF = 384, 448
+POINT_AT, CONV_AT = 512, 768
+PART = 416
 
 
 def mm(a, b, ca=1, cb=0):
@@ -72,6 +73,12 @@
                 shifted[t, lo:hi, 128 * u : 128 * u + 128] = part.astype(BF16)
 
 
+def voxel_at():
+    lane = lax.broadcasted_iota(jnp.int32, (1, 512), 1)
+    jj, kk, bb, qq, rr = lane // 256, lane // 128 % 2, lane % 128 // 16, lane // 4 % 4, lane % 4
+    return bb * 128 + 8 * (2 * qq + jj) + 2 * rr + kk
+
+
 def prepare_kernel(
     place, feat_hbm, occ_hbm, neighbours_hbm, w_conv_hbm, wd_hbm, wp_hbm, own_hbm,
     planes, occ_x, valid, wide, wd_rows, wp, own, beside, across,
@@ -89,9 +96,7 @@
             copies.append(pltpu.make_async_copy(wd_hbm.at[4 * i + jk], target, sems.at[6 + n]))
     for copy in copies:
         copy.start()
-    lane = lax.broadcasted_iota(jnp.int32, (1, 512), 1)
-    jj, kk, bb, qq, rr = lane // 256, lane // 128 % 2, lane % 128 // 16, lane // 4 % 4, lane % 4
-    voxel = bb * 128 + 8 * (2 * qq + jj) + 2 * rr + kk
+    voxel = voxel_at()
     row = lax.broadcasted_iota(jnp.int32, (1024, 512), 0)
     copies[0].wait()
     copies[1].wait()
@@ -198,13 +203,17 @@
 
 
 def backward_kernel(
-    split, place, shifted, slope_pre, hid, coarse, slope_down, slope_point, near, far, wd, wp, wire, wire_conv,
+    split, place, shifted, slope_pre, hid, coarse, slope_down, slope_point, near, far, wd, wp, wire,
     grads,
 ):
-    def put(target, first, value):
-        half, at = divmod(first, target.shape[1])
-        side = place[0] if half == 0 else 1 - place[0]
-        target[side, at : at + value.shape[0]] = value.astype(BF16)
+    def put(first, value):
+        done = 0
+        while done < value.shape[0]:
+            (stream, half), at = divmod((first + done) // PART, 2), (first + done) % PART
+            size = min(value.shape[0] - done, PART - at)
+            side = place[0] if half == 0 else 1 - place[0]
+            wire[side, stream, at : at + size] = value[done : done + size].astype(BF16)
+            done += size
 
     parts = []
     for p in range(4):
@@ -218,13 +227,11 @@
     cot_rows = jnp.concatenate(parts, axis=0)
     grad_point = (cot_rows.astype(F32) * slope_point[...]).astype(BF16)
     gwp = mm(coarse[...], grad_point)
-    put(wire, 512, gwp[:, :128])
-    put(wire, 640, gwp[:, 128:])
+    put(POINT_AT, gwp[:, :128])
+    put(POINT_AT + 128, gwp[:, 128:])
     grad_coarse = mm(wp[...], grad_point, 1, 1).astype(BF16)
     grad_down = (grad_coarse.astype(F32) * slope_down[...]).astype(BF16)
-    gwd = mm(hid[...], grad_down, 1, 1)
-    put(wire, 0, gwd[:384])
-    put(wire, 384, gwd[384:])
+    put(0, mm(hid[...], grad_down, 1, 1))
     for jk in range(4):
         grad_hidden = mm(wd[128 * jk : 128 * jk + 128], grad_down)
         for p in range(4):
@@ -251,35 +258,39 @@
             odd = band[64 * a + 64 : 64 * a + 128, :128] + band[64 * a + 192 : 64 * a + 256, 128:]
             both = jnp.where(low_lanes, even, odd)
             sums.append(both + pltpu.roll(both, 64, 1))
-        put(wire_conv, 64 * n, jnp.where(low_lanes, sums[0], sums[1]))
+        put(CONV_AT + 64 * n, jnp.where(low_lanes, sums[0], sums[1]))
         thirds.append(sums[2])
     for n in range(5):
-        put(wire_conv, 64 * (9 + n), jnp.where(low_lanes, thirds[2 * n], thirds[min(2 * n + 1, 8)]))
-
-
-def rows_of(place, mine, other, first, count):
-    half, at = divmod(first, mine.shape[0])
-    return jnp.where(place[0] == half, mine[at : at + count], other[at : at + count]).astype(F32)
-
-
-def finish_coarse_kernel(place, mine, other, gwd, gwp):
-    for i in range(2):
-        for jk in range(4):
-            gwd[4 * i + jk] = rows_of(place, mine, other, 128 * jk + 64 * i, 64)
-    for s in range(2):
-        gwp[:, 128 * s : 128 * s + 128] = rows_of(place, mine, other, 512 + 128 * s, 128)
-
-
-def finish_conv_kernel(place, mine, other, gwc):
-    for n in range(9):
-        pair = rows_of(place, mine, other, 64 * n, 64)
-        gwc[n] = pair[:, :64]
-        gwc[9 + n] = pair[:, 64:]
-    for n in range(5):
-        pair = rows_of(place, mine, other, 64 * (9 + n), 64)
-        gwc[18 + 2 * n] = pair[:, :64]
-        if n < 4:
-            gwc[19 + 2 * n] = pair[:, 64:]
+        put(CONV_AT + 64 * (9 + n), jnp.where(low_lanes, thirds[2 * n], thirds[min(2 * n + 1, 8)]))
+
+
+def finish_kernel(mine_a, other_a, mine_b, other_b, gwc, gwd, gwp):
+    def emit(halves):
+        def rows(first, count):
+            parts = []
+            while count:
+                (stream, half), at = divmod(first // PART, 2), first % PART
+                size = min(count, PART - at)
+                parts.append(halves[half][stream][at : at + size].astype(F32))
+                first, count = first + size, count - size
+            return jnp.concatenate(parts, axis=0) if len(parts) > 1 else parts[0]
+
+        for i in range(2):
+            for jk in range(4):
+                gwd[4 * i + jk] = rows(128 * jk + 64 * i, 64)
+        for n in range(2):
+            gwp[:, 128 * n : 128 * n + 128] = rows(POINT_AT + 128 * n, 128)
+        for n in range(14):
+            pair = rows(CONV_AT + 64 * n, 64)
+            first, second = (n, 9 + n) if n < 9 else (2 * n, 2 * n + 1)
+            gwc[first] = pair[:, :64]
+            if second < 27:
+                gwc[second] = pair[:, 64:]
+
+    core = lax.axis_index("brick") & 1
+    mine, other = (mine_a, mine_b), (other_a, other_b)
+    pl.when(core == 0)(lambda: emit((mine, other)))
+    pl.when(core == 1)(lambda: emit((other, mine)))
 
 
 def call(kernel, outs, ins, scratch=(), limit=24 * 2**20, flops=0, specs=None):
@@ -382,30 +393,27 @@
         flops=4 * 10**9,
         specs=[SMEM] + [VMEM] * 8,
     )
-    wires = call(
+    wire = call(
         functools.partial(backward_kernel, split),
-        (shape((2, COARSE_HALF, 128), BF16), shape((2, CONV_HALF, 128), BF16)),
+        shape((2, 2, PART, 128), BF16),
         (place, *saved, near, far, wd, wp),
         scratch=[pltpu.VMEM((256, 1024), BF16)],
         flops=4 * 10**9,
         specs=[SMEM] + [VMEM] * 10,
     )
-    bits = powers(brick_size, 4)[::-1]
-    far_steps = [("brick", bit) for bit in bits]
-    orders = (far_steps + [("dp", 1), ("brick", 2), ("dp", 2)], [("dp", 1)] + far_steps + [("dp", 2), ("brick", 2)])
-    sums = [wire[0] + swap(wire[1], "brick", 1) for wire in wires]
+    far_steps = [("brick", bit) for bit in powers(brick_size, 4)]
+    x, y, z = [("dp", 1)], [("dp", 2)], [("brick", 2)]
+    orders = z + x + y + far_steps, x + y + far_steps + z
+    sums = [wire[0, n] + swap(wire[1, n], "brick", 1) for n in range(2)]
     for n in range(len(orders[0])):
-        for s in range(2):
-            sums[s] = sums[s] + swap(sums[s], *orders[s][n])
+        for stream in range(2):
+            sums[stream] = sums[stream] + swap(sums[stream], *orders[stream][n])
     others = [swap(total, "brick", 1) for total in sums]
-    specs = [SMEM, VMEM, VMEM]
-    gwd, gwp = call(
-        finish_coarse_kernel,
-        (shape((8, 64, 128), F32), shape((128, 256), F32)),
-        (place, sums[0], others[0]),
-        specs=specs,
+    gwc, gwd, gwp = call(
+        finish_kernel,
+        (shape((27, 64, 64), F32), shape((8, 64, 128), F32), shape((128, 256), F32)),
+        (sums[0], others[0], sums[1], others[1]),
     )
-    gwc = call(finish_conv_kernel, shape((27, 64, 64), F32), (place, sums[1], others[1]), specs=specs)
     return gwc.reshape(3, 3, 3, 64, 64), gwd.reshape(2, 2, 2, 64, 128), gwp
 
 

time: 59.1 us -> 54.4 us (0.920)
  waiting for transfers between devices: 24.8 us -> 18.6 us
  starting transfers between devices: 18.5 us -> 21.7 us
  Pallas kernels: 13.8 us -> 12.1 us
    ppermute x18, waiting for transfers between devices: 24.8 us -> 18.6 us  [swap(): return lax.ppermute(value, axis, [(i, i ^ bit) for i in range(size)])]
    ppermute x18, starting transfers between devices: 17.9 us -> 21.1 us  [swap(): return lax.ppermute(value, axis, [(i, i ^ bit) for i in range(size)])]
    pallas_call x6 -> x5, Pallas kernels: 13.8 us -> 12.1 us  [call(): pl.pallas_call(kernel, out_shape=outs, in_specs=specs or [VMEM] * len(ins...]
  transfers between devices with their start and end apart: 19 -> 19, of which waited for: 13 -> 13; matrix products, arithmetic and copies ran while one was open for 2% -> 2% of each run, Pallas kernels for 15% -> 14%
where the time goes in v3:
time: 54.4 us; the launch traced here: 54.2 us
  starting transfers between devices  21.7 us (40%)
  waiting for transfers between devices  18.6 us (34%)
  Pallas kernels  12.1 us (22%)
  local copies, waits for them, and re-layouts  0.78 us (1%)
  between operations  0.77 us (1%)
    ppermute x18, starting transfers between devices, swap(): return lax.ppermute(value, axis, [(i, i ^ bit) for i in range(size)])  21.1 us
    ppermute x18, waiting for transfers between devices, swap(): return lax.ppermute(value, axis, [(i, i ^ bit) for i in range(size)])  18.6 us
    pallas_call x5, Pallas kernels, call(): pl.pallas_call(kernel, out_shape=outs, in_specs=specs or [VMEM] * len(ins...  12.1 us
  transfers between devices with their start and end apart: 19, of which 13 were waited for; matrix products, arithmetic and copies ran while one was open for 2% of the time, Pallas kernels for 14%

profile of v3, /device:TPU:0, one launch (start us, length us, event | category | flops | bytes accessed | tf_op | source)
XLA Modules:
  0.0 54.2 jit_solution(13925295738115112523)
XLA Ops:
  0.6 0.5 collective-permute-start.4
  1.1 2.7 %collective-permute-start = (bf16[8,64,256]{2,1,0:T(8,128)(2,1)}, bf16[8,64,256]{2,1,0:T(8,128)(2,1)S(1)}, u32[]{:S(2)}, u32[]{:S(2)}) collective-permute-start(bf16[8,64,256]{2,1,0:T(8,128)(2,1)} %bitcast.33), channel_id=1, source_target_pairs={{0,2},{1,3},{2,0},{3,1},{4,6},{5,7},{6,4},{7,5},{8,10},{9,11},{10,... | collective-permute-start | bytes 786440 | tf_op jit(solution)/shard_map/ppermute | solution.py:314
  3.8 2.6 %collective-permute-start.1 = (s32[8]{0:T(128)}, s32[8]{0:T(128)S(1)}, u32[]{:S(2)}, u32[]{:S(2)}) collective-permute-start(s32[8]{0:T(128)} %bitcast.27), channel_id=1, source_target_pairs={{0,4},{1,5},{2,6},{3,7},{4,0},{5,1},{6,2},{7,3},{8,12},{9,13},{10,... | collective-permute-start | bytes 104 | tf_op jit(solution)/shard_map/ppermute | solution.py:314
  6.4 0.8 %concatenate.3.place = s32[12]{0:T(128)S(1)} concatenate(s32[1]{0:T(128)} %bitcast, s32[1]{0:T(128)} %bitcast.1, s32[1]{0:T(128)} %bitcast.2, s32[1]{0:T(128)} %bitcast.3, s32[8]{0:T(128)} %bitcast.28), dimensions={0} | concatenate | bytes 96 | tf_op jit(solution)/shard_map/concatenate | solution.py:334
  7.2 3.2 %shard_map.103 = (bf16[512,512]{1,0:T(8,128)(2,1)S(1)}, f32[8,512]{1,0:T(8,128)S(1)}, f32[27,128]{1,0:T(8,128)S(1)}, bf16[256,3456]{1,0:T(8,128)(2,1)S(1)}, bf16...) custom-call(s32[12]{0:T(128)S(1)} %concatenate.3.place, ...), custom_call_target="tpu_custom_call" | custom-call | flops 4000000000 | bytes 1048576 | tf_op jit(solution)/shard_map/pallas_call | solution.py:297
  10.4 0.0 collective-permute-done.1.far_owners
  10.4 0.5 collective-permute-done.across
  10.9 0.0 collective-permute-start.5
  10.9 0.5 collective-permute-start.2
  11.4 0.7 %collective-permute-start.3 = (bf16[64,512]{1,0:T(8,128)(2,1)S(1)}, bf16[64,512]{1,0:T(8,128)(2,1)S(1)}, u32[]{:S(2)}, u32[]{:S(2)}) collective-permute-start(bf16[64,512]{1,0:T(8,128)(2,1)S(1)} %get-tuple-element.31), channel_id=1, source_target_pairs={{1,2},{3,4},{5,6},{2,1},{4,3},{6,5},{9,10},{11,12},{13,14},{10,9},... | collective-permute-start | bytes 196616 | tf_op jit(solution)/shard_map/ppermute | solution.py:362
  12.1 0.0 collective-permute-done.4.beside
  12.1 0.4 collective-permute-done.5.diagonal
  12.5 0.7 %shard_map.105 = (bf16[8,64,256]{2,1,0:T(8,128)(2,1)S(1)}, bf16[4,64,256]{2,1,0:T(8,128)(2,1)S(1)}) custom-call(s32[12]{0:T(128)S(1)} %concatenate.3.place, s32[8]{0:T(128)S(1)} %collective-permute-done.1.far_owners, bf16[8,64,256]{2,1,0:T(8,128)(2,1)S(1)} %get-tuple-element.42.own, bf16[8,64,256]{2,1,0:T(8,128)(2,1)S(1)} %collective-permute-done.4.beside, ...), custom_call_target="tpu_custom_call" | custom-call | bytes 1048576 | tf_op jit(solution)/shard_map/pallas_call | solution.py:297
  13.1 4.8 %collective-permute-start.6 = (bf16[4,64,256]{2,1,0:T(8,128)(2,1)S(1)}, bf16[4,64,256]{2,1,0:T(8,128)(2,1)S(1)}, u32[]{:S(2)}, u32[]{:S(2)}) collective-permute-start(bf16[4,64,256]{2,1,0:T(8,128)(2,1)S(1)} %get-tuple-element.45), channel_id=1, source_target_pairs={{0,4},{1,5},{2,6},{3,7},{4,0},{5,1},{6,2},{7,3},{8,12},{9,13},{10,... | collective-permute-start | bytes 393224 | tf_op jit(solution)/shard_map/ppermute | solution.py:314
  17.9 0.0 collective-permute-done.2.beside
  17.9 0.0 collective-permute-done.3.across
  17.9 3.7 %shard_map.104 = (bf16[4,640,512]{2,1,0:T(8,128)(2,1)S(1)}, f32[512,512]{1,0:T(8,128)S(1)}, bf16[512,512]{1,0:T(8,128)(2,1)S(1)}, bf16[128,512]{1,0:T(8,128)(2,1...) custom-call(s32[12]{0:T(128)S(1)} %concatenate.3.place, bf16[512,512]{1,0:T(8,128)(2,1)S(1)} %get-tuple-element.27.inner, ...), custom_call_target="tpu_custom_call" | custom-call | flops 4000000000 | bytes 1048576 | tf_op jit(solution)/shard_map/pallas_call | solution.py:297
  21.6 2.4 %collective-permute-done.6.far = bf16[4,64,256]{2,1,0:T(8,128)(2,1)S(1)} collective-permute-done((bf16[4,64,256]{2,1,0:T(8,128)(2,1)S(1)}, bf16[4,64,256]{2,1,0:T(8,128)(2,1)S(1)}, u32[]{:S(2)}, u32[]{:S(2)}) %collective-permute-start.6) | collective-permute-done | bytes 131104 | tf_op jit(solution)/shard_map/ppermute | solution.py:314
  24.1 3.3 %shard_map.106 = bf16[2,2,416,128]{3,2,1,0:T(8,128)(2,1)S(1)} custom-call(s32[12]{0:T(128)S(1)} %concatenate.3.place, bf16[4,640,512]{2,1,0:T(8,128)(2,1)S(1)} %get-tuple-element.35.shifted, f32[512,512]{1,0:T(8,128)S(1)} %get-tuple-element.36.slope_pre, bf16[512,512]{1,0:T(8,128)(2,1)S(1)} %get-tuple-element.37.hid, ...), custom_call_target="tpu_custom_call" | custom-call | flops 4000000000 | bytes 1048576 | tf_op jit(solution)/shard_map/pallas_call | solution.py:297
  27.4 0.9 %collective-permute-start.13 = (bf16[416,128]{1,0:T(8,128)(2,1)S(1)}, bf16[416,128]{1,0:T(8,128)(2,1)S(1)}, u32[]{:S(2)}, u32[]{:S(2)}) collective-permute-start(bf16[416,128]{1,0:T(8,128)(2,1)S(1)} %get-tuple-element.51), channel_id=1, source_target_pairs={{0,1},{1,0},{2,3},{3,2},{4,5},{5,4},{6,7},{7,6},{8,9},{9,8},{10,11... | collective-permute-start | bytes 319496 | tf_op jit(solution)/shard_map/ppermute | solution.py:314
  28.3 0.1 collective-permute-start.7
  28.3 0.9 %collective-permute-done.13 = bf16[416,128]{1,0:T(8,128)(2,1)S(1)} collective-permute-done((bf16[416,128]{1,0:T(8,128)(2,1)S(1)}, bf16[416,128]{1,0:T(8,128)(2,1)S(1)}, u32[]{:S(2)}, u32[]{:S(2)}) %collective-permute-start.13) | collective-permute-done | bytes 106528 | tf_op jit(solution)/shard_map/ppermute | solution.py:314
  29.2 0.4 collective-permute-done.7
  29.6 1.6 %collective-permute-start.14 = (bf16[416,128]{1,0:T(8,128)(2,1)S(1)}, bf16[416,128]{1,0:T(8,128)(2,1)S(1)}, u32[]{:S(2)}, u32[]{:S(2)}) collective-permute-start(bf16[416,128]{1,0:T(8,128)(2,1)S(1)} %get-tuple-element.49), channel_id=1, source_target_pairs={{0,8},{8,0},{16,24},{24,16},{1,9},{9,1},{17,25},{25,17},{2,10},{10... | collective-permute-start | bytes 319496 | tf_op jit(solution)/shard_map/ppermute | solution.py:314
  31.2 0.0 collective-permute-start.8
  31.2 3.5 %collective-permute-done.14 = bf16[416,128]{1,0:T(8,128)(2,1)S(1)} collective-permute-done((bf16[416,128]{1,0:T(8,128)(2,1)S(1)}, bf16[416,128]{1,0:T(8,128)(2,1)S(1)}, u32[]{:S(2)}, u32[]{:S(2)}) %collective-permute-start.14) | collective-permute-done | bytes 106528 | tf_op jit(solution)/shard_map/ppermute | solution.py:314
  34.7 1.6 %collective-permute-start.15 = (bf16[416,128]{1,0:T(8,128)(2,1)S(1)}, bf16[416,128]{1,0:T(8,128)(2,1)S(1)}, u32[]{:S(2)}, u32[]{:S(2)}) collective-permute-start(bf16[416,128]{1,0:T(8,128)(2,1)S(1)} %add.36), channel_id=1, source_target_pairs={{0,16},{8,24},{16,0},{24,8},{1,17},{9,25},{17,1},{25,9},{2,18},{10... | collective-permute-start | bytes 319496 | tf_op jit(solution)/shard_map/ppermute | solution.py:314
  36.3 0.0 collective-permute-done.8
  36.4 1.6 %collective-permute-start.9 = (bf16[416,128]{1,0:T(8,128)(2,1)S(1)}, bf16[416,128]{1,0:T(8,128)(2,1)S(1)}, u32[]{:S(2)}, u32[]{:S(2)}) collective-permute-start(bf16[416,128]{1,0:T(8,128)(2,1)S(1)} %add.31), channel_id=1, source_target_pairs={{0,8},{8,0},{16,24},{24,16},{1,9},{9,1},{17,25},{25,17},{2,10},{10... | collective-permute-start | bytes 319496 | tf_op jit(solution)/shard_map/ppermute | solution.py:314
  37.9 1.6 %collective-permute-done.15 = bf16[416,128]{1,0:T(8,128)(2,1)S(1)} collective-permute-done((bf16[416,128]{1,0:T(8,128)(2,1)S(1)}, bf16[416,128]{1,0:T(8,128)(2,1)S(1)}, u32[]{:S(2)}, u32[]{:S(2)}) %collective-permute-start.15) | collective-permute-done | bytes 106528 | tf_op jit(solution)/shard_map/ppermute | solution.py:314
  39.5 0.5 collective-permute-start.16
  40.0 1.1 %collective-permute-done.9 = bf16[416,128]{1,0:T(8,128)(2,1)S(1)} collective-permute-done((bf16[416,128]{1,0:T(8,128)(2,1)S(1)}, bf16[416,128]{1,0:T(8,128)(2,1)S(1)}, u32[]{:S(2)}, u32[]{:S(2)}) %collective-permute-start.9) | collective-permute-done | bytes 106528 | tf_op jit(solution)/shard_map/ppermute | solution.py:314
  41.2 1.2 %collective-permute-start.10 = (bf16[416,128]{1,0:T(8,128)(2,1)S(1)}, bf16[416,128]{1,0:T(8,128)(2,1)S(1)}, u32[]{:S(2)}, u32[]{:S(2)}) collective-permute-start(bf16[416,128]{1,0:T(8,128)(2,1)S(1)} %add.32), channel_id=1, source_target_pairs={{0,16},{8,24},{16,0},{24,8},{1,17},{9,25},{17,1},{25,9},{2,18},{10... | collective-permute-start | bytes 319496 | tf_op jit(solution)/shard_map/ppermute | solution.py:314
  42.3 3.2 %collective-permute-done.16 = bf16[416,128]{1,0:T(8,128)(2,1)S(1)} collective-permute-done((bf16[416,128]{1,0:T(8,128)(2,1)S(1)}, bf16[416,128]{1,0:T(8,128)(2,1)S(1)}, u32[]{:S(2)}, u32[]{:S(2)}) %collective-permute-start.16) | collective-permute-done | bytes 106528 | tf_op jit(solution)/shard_map/ppermute | solution.py:314
  45.5 0.1 collective-permute-start.17
  45.6 0.3 collective-permute-done.10
  46.0 2.5 %collective-permute-start.11 = (bf16[416,128]{1,0:T(8,128)(2,1)S(1)}, bf16[416,128]{1,0:T(8,128)(2,1)S(1)}, u32[]{:S(2)}, u32[]{:S(2)}) collective-permute-start(bf16[416,128]{1,0:T(8,128)(2,1)S(1)} %add.33), channel_id=1, source_target_pairs={{0,4},{1,5},{2,6},{3,7},{4,0},{5,1},{6,2},{7,3},{8,12},{9,13},{10,... | collective-permute-start | bytes 319496 | tf_op jit(solution)/shard_map/ppermute | solution.py:314
  48.5 1.9 %collective-permute-done.17 = bf16[416,128]{1,0:T(8,128)(2,1)S(1)} collective-permute-done((bf16[416,128]{1,0:T(8,128)(2,1)S(1)}, bf16[416,128]{1,0:T(8,128)(2,1)S(1)}, u32[]{:S(2)}, u32[]{:S(2)}) %collective-permute-start.17) | collective-permute-done | bytes 106528 | tf_op jit(solution)/shard_map/ppermute | solution.py:314
  50.4 0.1 collective-permute-start.18
  50.4 1.2 %collective-permute-done.11 = bf16[416,128]{1,0:T(8,128)(2,1)S(1)} collective-permute-done((bf16[416,128]{1,0:T(8,128)(2,1)S(1)}, bf16[416,128]{1,0:T(8,128)(2,1)S(1)}, u32[]{:S(2)}, u32[]{:S(2)}) %collective-permute-start.11) | collective-permute-done | bytes 106528 | tf_op jit(solution)/shard_map/ppermute | solution.py:314
  51.7 0.1 collective-permute-start.12
  51.8 0.0 collective-permute-done.18.other_b
  51.8 1.3 %collective-permute-done.12.other_a = bf16[416,128]{1,0:T(8,128)(2,1)S(1)} collective-permute-done((bf16[416,128]{1,0:T(8,128)(2,1)S(1)}, bf16[416,128]{1,0:T(8,128)(2,1)S(1)}, u32[]{:S(2)}, u32[]{:S(2)}) %collective-permute-start.12) | collective-permute-done | bytes 106528 | tf_op jit(solution)/shard_map/ppermute | solution.py:314
  53.1 1.2 %shard_map.107 = (f32[27,64,64]{2,1,0:T(8,128)}, f32[8,64,128]{2,1,0:T(8,128)}, f32[128,256]{1,0:T(8,128)}) custom-call(bf16[416,128]{1,0:T(8,128)(2,1)S(1)} %add.34.mine_a, bf16[416,128]{1,0:T(8,128)(2,1)S(1)} %collective-permute-done.12.other_a, bf16[416,128]{1,0:T(8,128)(2,1)S(1)} %add.39.mine_b, bf16[416,128]{1,0:T(8,128)(2,1)S(1)} %collective-permute-done.18.other_b), custom_call_target="tpu_custom_call" | custom-call | bytes 1048576 | tf_op jit(solution)/shard_map/pallas_call | solution.py:297
  (10 shorter events, 0.3 us)
Async XLA Ops:
  0.6 11.5 %collective-permute-start.4 = (bf16[8,64,256]{2,1,0:T(8,128)(2,1)}, bf16[8,64,256]{2,1,0:T(8,128)(2,1)S(1)}, u32[]{:S(2)}, u32[]{:S(2)}) collective-permute-start(bf16[8,64,256]{2,1,0:T(8,128)(2,1)} %bitcast.32), channel_id=1, source_target_pairs={{0,1},{1,0},{2,3},{3,2},{4,5},{5,4},{6,7},{7,6},{8,9},{9,8},{10,11... | collective-permute-start | bytes 786440 | tf_op jit(solution)/shard_map/ppermute | solution.py:314
  1.1 9.8 %collective-permute-start = (bf16[8,64,256]{2,1,0:T(8,128)(2,1)}, bf16[8,64,256]{2,1,0:T(8,128)(2,1)S(1)}, u32[]{:S(2)}, u32[]{:S(2)}) collective-permute-start(bf16[8,64,256]{2,1,0:T(8,128)(2,1)} %bitcast.33), channel_id=1, source_target_pairs={{0,2},{1,3},{2,0},{3,1},{4,6},{5,7},{6,4},{7,5},{8,10},{9,11},{10,... | collective-permute-start | bytes 786440 | tf_op jit(solution)/shard_map/ppermute | solution.py:314
  3.8 6.6 %collective-permute-start.1 = (s32[8]{0:T(128)}, s32[8]{0:T(128)S(1)}, u32[]{:S(2)}, u32[]{:S(2)}) collective-permute-start(s32[8]{0:T(128)} %bitcast.27), channel_id=1, source_target_pairs={{0,4},{1,5},{2,6},{3,7},{4,0},{5,1},{6,2},{7,3},{8,12},{9,13},{10,... | collective-permute-start | bytes 104 | tf_op jit(solution)/shard_map/ppermute | solution.py:314
  10.9 1.5 %collective-permute-start.5 = (bf16[8,64,256]{2,1,0:T(8,128)(2,1)S(1)}, bf16[8,64,256]{2,1,0:T(8,128)(2,1)S(1)}, u32[]{:S(2)}, u32[]{:S(2)}) collective-permute-start(bf16[8,64,256]{2,1,0:T(8,128)(2,1)S(1)} %collective-permute-done.across), channel_id=1, source_target_pairs={{0,1},{1,0},{2,3},{3,2},{4,5},{5,4},{6,7},{7,6},{8,9},{9,8},{10,11... | collective-permute-start | bytes 786440 | tf_op jit(solution)/shard_map/ppermute | solution.py:314
  10.9 7.0 %collective-permute-start.2 = (bf16[64,512]{1,0:T(8,128)(2,1)S(1)}, bf16[64,512]{1,0:T(8,128)(2,1)S(1)}, u32[]{:S(2)}, u32[]{:S(2)}) collective-permute-start(bf16[64,512]{1,0:T(8,128)(2,1)S(1)} %get-tuple-element.30), channel_id=1, source_target_pairs={{0,1},{1,0},{2,3},{3,2},{4,5},{5,4},{6,7},{7,6},{8,9},{9,8},{10,11... | collective-permute-start | bytes 196616 | tf_op jit(solution)/shard_map/ppermute | solution.py:314
  11.4 6.5 %collective-permute-start.3 = (bf16[64,512]{1,0:T(8,128)(2,1)S(1)}, bf16[64,512]{1,0:T(8,128)(2,1)S(1)}, u32[]{:S(2)}, u32[]{:S(2)}) collective-permute-start(bf16[64,512]{1,0:T(8,128)(2,1)S(1)} %get-tuple-element.31), channel_id=1, source_target_pairs={{1,2},{3,4},{5,6},{2,1},{4,3},{6,5},{9,10},{11,12},{13,14},{10,9},... | collective-permute-start | bytes 196616 | tf_op jit(solution)/shard_map/ppermute | solution.py:362
  13.1 11.0 %collective-permute-start.6 = (bf16[4,64,256]{2,1,0:T(8,128)(2,1)S(1)}, bf16[4,64,256]{2,1,0:T(8,128)(2,1)S(1)}, u32[]{:S(2)}, u32[]{:S(2)}) collective-permute-start(bf16[4,64,256]{2,1,0:T(8,128)(2,1)S(1)} %get-tuple-element.45), channel_id=1, source_target_pairs={{0,4},{1,5},{2,6},{3,7},{4,0},{5,1},{6,2},{7,3},{8,12},{9,13},{10,... | collective-permute-start | bytes 393224 | tf_op jit(solution)/shard_map/ppermute | solution.py:314
  27.4 1.8 %collective-permute-start.13 = (bf16[416,128]{1,0:T(8,128)(2,1)S(1)}, bf16[416,128]{1,0:T(8,128)(2,1)S(1)}, u32[]{:S(2)}, u32[]{:S(2)}) collective-permute-start(bf16[416,128]{1,0:T(8,128)(2,1)S(1)} %get-tuple-element.51), channel_id=1, source_target_pairs={{0,1},{1,0},{2,3},{3,2},{4,5},{5,4},{6,7},{7,6},{8,9},{9,8},{10,11... | collective-permute-start | bytes 319496 | tf_op jit(solution)/shard_map/ppermute | solution.py:314
  28.3 1.3 %collective-permute-start.7 = (bf16[416,128]{1,0:T(8,128)(2,1)S(1)}, bf16[416,128]{1,0:T(8,128)(2,1)S(1)}, u32[]{:S(2)}, u32[]{:S(2)}) collective-permute-start(bf16[416,128]{1,0:T(8,128)(2,1)S(1)} %get-tuple-element.52), channel_id=1, source_target_pairs={{0,1},{1,0},{2,3},{3,2},{4,5},{5,4},{6,7},{7,6},{8,9},{9,8},{10,11... | collective-permute-start | bytes 319496 | tf_op jit(solution)/shard_map/ppermute | solution.py:314
  29.6 5.1 %collective-permute-start.14 = (bf16[416,128]{1,0:T(8,128)(2,1)S(1)}, bf16[416,128]{1,0:T(8,128)(2,1)S(1)}, u32[]{:S(2)}, u32[]{:S(2)}) collective-permute-start(bf16[416,128]{1,0:T(8,128)(2,1)S(1)} %get-tuple-element.49), channel_id=1, source_target_pairs={{0,8},{8,0},{16,24},{24,16},{1,9},{9,1},{17,25},{25,17},{2,10},{10... | collective-permute-start | bytes 319496 | tf_op jit(solution)/shard_map/ppermute | solution.py:314
  31.2 5.2 %collective-permute-start.8 = (bf16[416,128]{1,0:T(8,128)(2,1)S(1)}, bf16[416,128]{1,0:T(8,128)(2,1)S(1)}, u32[]{:S(2)}, u32[]{:S(2)}) collective-permute-start(bf16[416,128]{1,0:T(8,128)(2,1)S(1)} %get-tuple-element.50), channel_id=1, source_target_pairs={{0,2},{1,3},{2,0},{3,1},{4,6},{5,7},{6,4},{7,5},{8,10},{9,11},{10,... | collective-permute-start | bytes 319496 | tf_op jit(solution)/shard_map/ppermute | solution.py:314
  34.7 4.8 %collective-permute-start.15 = (bf16[416,128]{1,0:T(8,128)(2,1)S(1)}, bf16[416,128]{1,0:T(8,128)(2,1)S(1)}, u32[]{:S(2)}, u32[]{:S(2)}) collective-permute-start(bf16[416,128]{1,0:T(8,128)(2,1)S(1)} %add.36), channel_id=1, source_target_pairs={{0,16},{8,24},{16,0},{24,8},{1,17},{9,25},{17,1},{25,9},{2,18},{10... | collective-permute-start | bytes 319496 | tf_op jit(solution)/shard_map/ppermute | solution.py:314
  36.4 4.8 %collective-permute-start.9 = (bf16[416,128]{1,0:T(8,128)(2,1)S(1)}, bf16[416,128]{1,0:T(8,128)(2,1)S(1)}, u32[]{:S(2)}, u32[]{:S(2)}) collective-permute-start(bf16[416,128]{1,0:T(8,128)(2,1)S(1)} %add.31), channel_id=1, source_target_pairs={{0,8},{8,0},{16,24},{24,16},{1,9},{9,1},{17,25},{25,17},{2,10},{10... | collective-permute-start | bytes 319496 | tf_op jit(solution)/shard_map/ppermute | solution.py:314
  39.5 6.0 %collective-permute-start.16 = (bf16[416,128]{1,0:T(8,128)(2,1)S(1)}, bf16[416,128]{1,0:T(8,128)(2,1)S(1)}, u32[]{:S(2)}, u32[]{:S(2)}) collective-permute-start(bf16[416,128]{1,0:T(8,128)(2,1)S(1)} %add.37), channel_id=1, source_target_pairs={{0,4},{1,5},{2,6},{3,7},{4,0},{5,1},{6,2},{7,3},{8,12},{9,13},{10,... | collective-permute-start | bytes 319496 | tf_op jit(solution)/shard_map/ppermute | solution.py:314
  41.2 4.8 %collective-permute-start.10 = (bf16[416,128]{1,0:T(8,128)(2,1)S(1)}, bf16[416,128]{1,0:T(8,128)(2,1)S(1)}, u32[]{:S(2)}, u32[]{:S(2)}) collective-permute-start(bf16[416,128]{1,0:T(8,128)(2,1)S(1)} %add.32), channel_id=1, source_target_pairs={{0,16},{8,24},{16,0},{24,8},{1,17},{9,25},{17,1},{25,9},{2,18},{10... | collective-permute-start | bytes 319496 | tf_op jit(solution)/shard_map/ppermute | solution.py:314
  45.5 4.8 %collective-permute-start.17 = (bf16[416,128]{1,0:T(8,128)(2,1)S(1)}, bf16[416,128]{1,0:T(8,128)(2,1)S(1)}, u32[]{:S(2)}, u32[]{:S(2)}) collective-permute-start(bf16[416,128]{1,0:T(8,128)(2,1)S(1)} %add.38), channel_id=1, source_target_pairs={{0,2},{1,3},{2,0},{3,1},{4,6},{5,7},{6,4},{7,5},{8,10},{9,11},{10,... | collective-permute-start | bytes 319496 | tf_op jit(solution)/shard_map/ppermute | solution.py:314
  46.0 5.7 %collective-permute-start.11 = (bf16[416,128]{1,0:T(8,128)(2,1)S(1)}, bf16[416,128]{1,0:T(8,128)(2,1)S(1)}, u32[]{:S(2)}, u32[]{:S(2)}) collective-permute-start(bf16[416,128]{1,0:T(8,128)(2,1)S(1)} %add.33), channel_id=1, source_target_pairs={{0,4},{1,5},{2,6},{3,7},{4,0},{5,1},{6,2},{7,3},{8,12},{9,13},{10,... | collective-permute-start | bytes 319496 | tf_op jit(solution)/shard_map/ppermute | solution.py:314
  50.4 1.4 %collective-permute-start.18 = (bf16[416,128]{1,0:T(8,128)(2,1)S(1)}, bf16[416,128]{1,0:T(8,128)(2,1)S(1)}, u32[]{:S(2)}, u32[]{:S(2)}) collective-permute-start(bf16[416,128]{1,0:T(8,128)(2,1)S(1)} %add.39.mine_b), channel_id=1, source_target_pairs={{0,1},{1,0},{2,3},{3,2},{4,5},{5,4},{6,7},{7,6},{8,9},{9,8},{10,11... | collective-permute-start | bytes 319496 | tf_op jit(solution)/shard_map/ppermute | solution.py:314
  51.7 1.4 %collective-permute-start.12 = (bf16[416,128]{1,0:T(8,128)(2,1)S(1)}, bf16[416,128]{1,0:T(8,128)(2,1)S(1)}, u32[]{:S(2)}, u32[]{:S(2)}) collective-permute-start(bf16[416,128]{1,0:T(8,128)(2,1)S(1)} %add.34.mine_a), channel_id=1, source_target_pairs={{0,1},{1,0},{2,3},{3,2},{4,5},{5,4},{6,7},{7,6},{8,9},{9,8},{10,11... | collective-permute-start | bytes 319496 | tf_op jit(solution)/shard_map/ppermute | solution.py:314

commit v4 on v3

--- a/solution.py
+++ b/solution.py
@@ -1,5 +1,3 @@
-import functools
-
 import jax
 import jax.numpy as jnp
 from jax import lax
@@ -80,26 +78,32 @@
 
 
 def prepare_kernel(
-    place, feat_hbm, occ_hbm, neighbours_hbm, w_conv_hbm, wd_hbm, wp_hbm, own_hbm,
-    planes, occ_x, valid, wide, wd_rows, wp, own, beside, across,
+    feat_hbm, occ_hbm, neighbours_hbm, w_conv_hbm, wd_hbm, wp_hbm, own_hbm, slots_hbm,
+    planes, occ_x, valid, wide, wd_rows, wp, own, slots,
     feat, occ, neighbours, w_conv, sems,
 ):
-    copies = []
-    for n, (source, target) in enumerate(
-        ((feat_hbm, feat), (occ_hbm, occ), (w_conv_hbm, w_conv), (neighbours_hbm, neighbours), (wp_hbm, wp), (own_hbm, own))
-    ):
-        copies.append(pltpu.make_async_copy(source, target, sems.at[n]))
+    pairs = [(w_conv_hbm, w_conv), (feat_hbm, feat), (occ_hbm, occ), (neighbours_hbm, neighbours)]
+    pairs += [(wp_hbm, wp), (own_hbm, own), (slots_hbm, slots)]
     for jk in range(4):
         for i in range(2):
             n = 2 * jk + i
-            target = wd_rows.at[64 * n : 64 * n + 64]
-            copies.append(pltpu.make_async_copy(wd_hbm.at[4 * i + jk], target, sems.at[6 + n]))
+            pairs.append((wd_hbm.at[4 * i + jk], wd_rows.at[64 * n : 64 * n + 64]))
+    copies = [pltpu.make_async_copy(source, target, sems.at[n]) for n, (source, target) in enumerate(pairs)]
     for copy in copies:
         copy.start()
+    copies[0].wait()
+    first, second = turned_weights(w_conv)
+    zero = jnp.zeros((64, 128), BF16)
+    for n in range(9):
+        cut = slice(256 * n, 256 * n + 256)
+        for x in range(4):
+            band = (first if x % 2 == 0 else second)[:, cut]
+            band = [band, zero] if x < 2 else [zero, band]
+            wide[64 * x : 64 * x + 64, 384 * n : 384 * n + 384] = jnp.concatenate(band, axis=1)
     voxel = voxel_at()
     row = lax.broadcasted_iota(jnp.int32, (1024, 512), 0)
-    copies[0].wait()
     copies[1].wait()
+    copies[2].wait()
     occ_f = occ[...].astype(F32).astype(BF16)
     rows = []
     for m in range(4):
@@ -110,27 +114,12 @@
     ]
     occ_rows = jnp.concatenate(occ_rows + [jnp.zeros((12, 1024), BF16)], axis=0)
     stacked = jnp.concatenate(rows + [occ_rows], axis=0)
-    ends = []
     for e in range(2):
         select = jnp.where(row == voxel + 64 * e, 1.0, 0.0).astype(BF16)
         picked = mm(stacked, select)
-        moved = picked[:256].astype(BF16)
         for m in range(4):
-            planes[64 * (2 * m + e) : 64 * (2 * m + e + 1), :] = moved[64 * m : 64 * m + 64]
+            planes[64 * (2 * m + e) : 64 * (2 * m + e + 1), :] = picked[64 * m : 64 * m + 64].astype(BF16)
             occ_x[2 * m + e : 2 * m + e + 1] = picked[256 + m : 257 + m]
-        ends.append(moved[192 * e : 192 * e + 64])
-    even = place[0] == 0
-    beside[...] = jnp.where(even, ends[1], ends[0])
-    across[...] = jnp.where(even, ends[0], ends[1])
-    copies[2].wait()
-    first, second = turned_weights(w_conv)
-    zero = jnp.zeros((64, 128), BF16)
-    for n in range(9):
-        cut = slice(256 * n, 256 * n + 256)
-        for x in range(4):
-            band = (first if x % 2 == 0 else second)[:, cut]
-            band = [band, zero] if x < 2 else [zero, band]
-            wide[64 * x : 64 * x + 64, 384 * n : 384 * n + 384] = jnp.concatenate(band, axis=1)
     copies[3].wait()
     valid[...] = near_masks(neighbours[...])
     for copy in copies[4:]:
@@ -138,19 +127,22 @@
 
 
 def forward_kernel(
-    place, inner, occ_x, valid, beside, across, wide, wd, wp,
+    inner, occ_x, valid, beside, across, wide, wd, wp,
     shifted, slope_pre, hid, coarse_ref, slope_down, slope_point,
     planes,
 ):
     planes[64:576] = inner[...]
-    odd_core = place[0] == 1
+    odd_core = lax.axis_index("brick") & 1 == 1
     inner_x = lax.broadcasted_iota(jnp.int32, (64, 128), 1) >= 64
+    row = lax.broadcasted_iota(jnp.int32, (512, 512), 0)
+    before = jnp.concatenate([jnp.where(odd_core, beside[b], across[b]) for b in range(4)], axis=1)
+    after = jnp.concatenate([jnp.where(odd_core, across[b], beside[b]) for b in range(4)], axis=1)
+    before = mm(before, jnp.where(row == voxel_at() - 448, 1.0, 0.0).astype(BF16)).astype(BF16)
+    after = mm(after, jnp.where(row == voxel_at(), 1.0, 0.0).astype(BF16)).astype(BF16)
     for g in range(4):
         cut = slice(128 * g, 128 * g + 128)
-        before = jnp.where(odd_core, beside[:, cut], across[:, cut])
-        after = jnp.where(odd_core, across[:, cut], beside[:, cut])
-        planes[0:64, cut] = pltpu.roll(jnp.where(inner_x, before, inner[448:512, cut]), 64, 1)
-        planes[576:640, cut] = pltpu.roll(jnp.where(inner_x, inner[0:64, cut], after), 64, 1)
+        planes[0:64, cut] = pltpu.roll(jnp.where(inner_x, before[:, cut], inner[448:512, cut]), 64, 1)
+        planes[576:640, cut] = pltpu.roll(jnp.where(inner_x, inner[0:64, cut], after[:, cut]), 64, 1)
     shift_planes(planes, valid, shifted)
     for h in range(2):
         for j in range(2):
@@ -182,50 +174,56 @@
     slope_point[...] = gate * (1.0 + point * (1.0 - gate))
 
 
-def pick_kernel(place, far_owners, own, beside, across, diagonal, near, reply):
-    me = place[3]
-    owners = [place[4 + b] for b in range(8)]
-    tables = (own, beside, across, diagonal)
-
-    def pick(relation, slot):
-        value = own[slot]
-        for n in range(1, 4):
-            value = jnp.where(relation == n, tables[n][slot], value)
-        return value
-
+def pick(tables, relation, slot):
+    value = tables[0][slot]
+    for n in range(1, 4):
+        value = jnp.where(relation == n, tables[n][slot], value)
+    return value
+
+
+def reply_kernel(far_slots, own, beside, across, diagonal, reply):
+    me = lax.axis_index("brick")
+    asked = far_slots[...]
+    for i in range(4):
+        mine = (asked >> 3) == (me & 4) + i
+        slot = jnp.sum(jnp.where(mine, (asked & 7).astype(F32), 0.0)).astype(jnp.int32)
+        reply[i] = pick((own, beside, across, diagonal), (me & 3) ^ i, slot)
+
+
+def near_kernel(slots, own, beside, across, diagonal, near, place):
+    me = lax.axis_index("brick")
     for b in range(8):
-        near[b] = pick(((owners[b] >> 3) ^ me) & 3, owners[b] & 7)
-    for i in range(4):
-        slot = jnp.int32(0)
-        for b in range(8):
-            slot = jnp.where((far_owners[b] >> 3) == (me & 4) + i, far_owners[b] & 7, slot)
-        reply[i] = pick((me & 3) ^ i, slot)
+        target = slots[b] >> 3
+        near[b] = pick((own, beside, across, diagonal), (target ^ me) & 3, slots[b] & 7)
+        at = jnp.where(((target ^ me) & 4) == 0, -1, target & 3)
+        place[b : b + 1, :] = jnp.full((1, 256), at, jnp.int32)
 
 
 def backward_kernel(
-    split, place, shifted, slope_pre, hid, coarse, slope_down, slope_point, near, far, wd, wp, wire,
+    shifted, slope_pre, hid, coarse, slope_down, slope_point, near, place, far, wd, wp, wire,
     grads,
 ):
+    me = lax.axis_index("brick")
+    core = me & 1
+
     def put(first, value):
         done = 0
         while done < value.shape[0]:
             (stream, half), at = divmod((first + done) // PART, 2), (first + done) % PART
             size = min(value.shape[0] - done, PART - at)
-            side = place[0] if half == 0 else 1 - place[0]
+            side = core if half == 0 else 1 - core
             wire[side, stream, at : at + size] = value[done : done + size].astype(BF16)
             done += size
 
-    parts = []
-    for p in range(4):
-        for b in range(8):
-            part = near[b, 16 * p : 16 * p + 16, :]
-            if split:
-                target = place[4 + b] >> 3
-                other = far[target & 3, 16 * p : 16 * p + 16, :]
-                part = jnp.where(((target ^ place[3]) & 4) == 0, part, other)
-            parts.append(part)
+    wanted = []
+    for b in range(8):
+        value, at = near[b].astype(F32), place[b : b + 1, :]
+        for i in range(4):
+            value = jnp.where(at == i, far[i].astype(F32), value)
+        wanted.append(value)
+    parts = [wanted[b][16 * p : 16 * p + 16] for p in range(4) for b in range(8)]
     cot_rows = jnp.concatenate(parts, axis=0)
-    grad_point = (cot_rows.astype(F32) * slope_point[...]).astype(BF16)
+    grad_point = (cot_rows * slope_point[...]).astype(BF16)
     gwp = mm(coarse[...], grad_point)
     put(POINT_AT, gwp[:, :128])
     put(POINT_AT + 128, gwp[:, 128:])
@@ -325,14 +323,16 @@
 def shards(features, occupancy, neighbours, owners, w_conv, w_down, w_point, cotangent):
     brick_size = lax.axis_size("brick")
     shape = jax.ShapeDtypeStruct
-    me = lax.axis_index("brick")
-    core = me & 1
-    dp_at = lax.axis_index("dp")
+    core = lax.axis_index("brick") & 1
+    split = brick_size == 8
     feat = jnp.swapaxes(features[0], 1, 2)
     slots, own = owners[0], cotangent[0]
-    split = brick_size == 8
-    place = jnp.concatenate([jnp.stack([core, dp_at & 1, dp_at >> 1, me]).astype(jnp.int32), slots])
-    prepared = call(
+    first, last = feat[0:4, :, 0:128], feat[4:8, :, 384:512]
+    beside = swap(jnp.where(core == 0, last, first), "brick", 1)
+    chips = [(i, i + 1) for i in range(1, brick_size - 1, 2)]
+    across = lax.ppermute(jnp.where(core == 0, first, last), "brick", chips + [(j, i) for i, j in chips])
+    arguments = (feat, occupancy[0], neighbours[0], w_conv.reshape(27, 64, 64), w_down.reshape(8, 64, 128), w_point)
+    planes, occ_x, valid, wide, wd, wp, own_copy, slots_copy = call(
         prepare_kernel,
         (
             shape((512, 512), BF16),
@@ -342,32 +342,30 @@
             shape((512, 128), BF16),
             shape((128, 256), BF16),
             shape((8, 64, 256), BF16),
-            shape((64, 512), BF16),
-            shape((64, 512), BF16),
+            shape((8,), jnp.int32),
         ),
-        (place, *in_hbm(feat, occupancy[0], neighbours[0], w_conv.reshape(27, 64, 64), w_down.reshape(8, 64, 128), w_point, own)),
+        in_hbm(*arguments, own, slots),
         scratch=[
             pltpu.VMEM((8, 64, 512), BF16),
             pltpu.VMEM((8, 512), jnp.int32),
             pltpu.VMEM((8, 27), jnp.int32),
             pltpu.VMEM((27, 64, 64), BF16),
-            pltpu.SemaphoreType.DMA((14,)),
+            pltpu.SemaphoreType.DMA((15,)),
         ],
         flops=4 * 10**9,
-        specs=[SMEM] + [HBM] * 7,
+        specs=[HBM] * 8,
     )
-    planes, occ_x, valid, wide, wd, wp, own_copy, beside, across = prepared
-    beside = swap(beside, "brick", 1)
-    chips = [(i, i + 1) for i in range(1, brick_size - 1, 2)]
-    across = lax.ppermute(across, "brick", chips + [(j, i) for i, j in chips])
     if split:
-        partner, far_slots, planes = lax.optimization_barrier((swap(own, "brick", 2), swap(slots, "brick", 4), planes))
+        partner, far_slots, planes, beside, across = lax.optimization_barrier(
+            (swap(own, "brick", 2), swap(owners, "brick", 4), planes, beside, across)
+        )
         tables = (own_copy, swap(own, "brick", 1), partner, swap(partner, "brick", 1))
-        near, reply = call(
-            pick_kernel,
-            (shape((8, 64, 256), BF16), shape((4, 64, 256), BF16)),
-            (place, far_slots, *tables),
-            specs=[SMEM] * 2 + [VMEM] * 4,
+        reply = call(reply_kernel, shape((4, 64, 256), BF16), (far_slots, *tables))
+        near, place = call(
+            near_kernel,
+            (shape((8, 64, 256), BF16), shape((8, 256), jnp.int32)),
+            (slots_copy, *tables),
+            specs=[SMEM] + [VMEM] * 4,
         )
         far = swap(reply, "brick", 4)
     else:
@@ -377,7 +375,7 @@
         reply = jnp.take(own, arrived, axis=0, mode="clip")
         fetched = lax.all_to_all(reply, "brick", split_axis=0, concat_axis=0, tiled=True)
         near = jnp.take(fetched, slots >> 3, axis=0, mode="clip")
-        far = near[:4]
+        far, place = near[:4], jnp.full((8, 256), -1, jnp.int32)
     saved = call(
         forward_kernel,
         (
@@ -388,18 +386,16 @@
             shape((128, 512), F32),
             shape((512, 256), F32),
         ),
-        (place, planes, occ_x, valid, beside, across, wide, wd, wp),
+        (planes, occ_x, valid, beside, across, wide, wd, wp),
         scratch=[pltpu.VMEM((640, 512), BF16)],
         flops=4 * 10**9,
-        specs=[SMEM] + [VMEM] * 8,
     )
     wire = call(
-        functools.partial(backward_kernel, split),
+        backward_kernel,
         shape((2, 2, PART, 128), BF16),
-        (place, *saved, near, far, wd, wp),
+        (*saved, near, place, far, wd, wp),
         scratch=[pltpu.VMEM((256, 1024), BF16)],
         flops=4 * 10**9,
-        specs=[SMEM] + [VMEM] * 10,
     )
     far_steps = [("brick", bit) for bit in powers(brick_size, 4)]
     x, y, z = [("dp", 1)], [("dp", 2)], [("brick", 2)]

time: 54.4 us -> 53.2 us (0.978)
  starting transfers between devices: 21.7 us -> 18.6 us
  waiting for transfers between devices: 18.6 us -> 21.4 us
  Pallas kernels: 12.1 us -> 11 us
  other arithmetic: 0.28 us -> 1.18 us
  local copies, waits for them, and re-layouts: 0.78 us -> 0.02 us
    ppermute x18, starting transfers between devices: 21.1 us -> 18 us  [swap(): return lax.ppermute(value, axis, [(i, i ^ bit) for i in range(size)])]
    ppermute x18, waiting for transfers between devices: 18.6 us -> 21.4 us  [swap(): return lax.ppermute(value, axis, [(i, i ^ bit) for i in range(size)])]
    pallas_call x5 -> x6, Pallas kernels: 12.1 us -> 11 us  [call(): pl.pallas_call(kernel, out_shape=outs, in_specs=specs or [VMEM] * len(ins...]
    select_n x0 -> x1, other arithmetic: none -> 0.89 us  [shards(): jnp.where(core == 0, first, last)]
    concatenate x1 -> x0, local copies, waits for them, and re-layouts: 0.77 us -> none  [shards(): jnp.concatenate([jnp.stack([core, dp_at & 1, dp_at >> 1, me]).astype(jnp....]
  transfers between devices with their start and end apart: 19 -> 19, of which waited for: 13 -> 13; matrix products, arithmetic and copies ran while one was open for 2% -> 2% of each run, Pallas kernels for 14% -> 13%
where the time goes in v4:
time: 53.2 us; the launch traced here: 53 us
  waiting for transfers between devices  21.4 us (40%)
  starting transfers between devices  18.6 us (35%)
  Pallas kernels  11 us (21%)
  other arithmetic  1.18 us (2%)
  between operations  0.8 us (2%)
    ppermute x18, waiting for transfers between devices, swap(): return lax.ppermute(value, axis, [(i, i ^ bit) for i in range(size)])  21.4 us
    ppermute x18, starting transfers between devices, swap(): return lax.ppermute(value, axis, [(i, i ^ bit) for i in range(size)])  18 us
    pallas_call x6, Pallas kernels, call(): pl.pallas_call(kernel, out_shape=outs, in_specs=specs or [VMEM] * len(ins...  11 us
  transfers between devices with their start and end apart: 19, of which 13 were waited for; matrix products, arithmetic and copies ran while one was open for 2% of the time, Pallas kernels for 13%

profile of v4, /device:TPU:0, one launch (start us, length us, event | category | flops | bytes accessed | tf_op | source)
XLA Modules:
  0.0 53.0 jit_solution(1368235293357745737)
XLA Ops:
  0.6 0.5 collective-permute-start.4
  1.1 2.7 %collective-permute-start = (bf16[8,64,256]{2,1,0:T(8,128)(2,1)}, bf16[8,64,256]{2,1,0:T(8,128)(2,1)S(1)}, u32[]{:S(2)}, u32[]{:S(2)}) collective-permute-start(bf16[8,64,256]{2,1,0:T(8,128)(2,1)} %bitcast.28), channel_id=1, source_target_pairs={{0,2},{1,3},{2,0},{3,1},{4,6},{5,7},{6,4},{7,5},{8,10},{9,11},{10,... | collective-permute-start | bytes 786440 | tf_op jit(solution)/shard_map/ppermute | solution.py:312
  3.8 2.6 %collective-permute-start.1 = (s32[1,8]{1,0:T(1,128)}, s32[1,8]{1,0:T(1,128)S(1)}, u32[]{:S(2)}, u32[]{:S(2)}) collective-permute-start(s32[1,8]{1,0:T(1,128)} %param.11), channel_id=1, source_target_pairs={{0,4},{1,5},{2,6},{3,7},{4,0},{5,1},{6,2},{7,3},{8,12},{9,13},{10,... | collective-permute-start | bytes 104 | tf_op jit(solution)/shard_map/ppermute | solution.py:312
  6.4 0.9 %broadcast_select_fusion = (bf16[4,64,128]{2,1,0:T(8,128)(2,1)S(1)}, bf16[4,64,128]{2,1,0:T(8,128)(2,1)S(1)}) fusion(pred[]{:T(512)S(6)} %eq.4, bf16[8,64,512]{2,1,0:T(8,128)(2,1)} %bitcast.23), kind=kLoop, calls=%fused_computation.6 | loop fusion | flops 65536 | bytes 262145 | tf_op jit(solution)/shard_map/jit(_where)/select_n | solution.py:333
  7.3 0.7 %collective-permute-start.3 = (bf16[4,64,128]{2,1,0:T(8,128)(2,1)S(1)}, bf16[4,64,128]{2,1,0:T(8,128)(2,1)S(1)}, u32[]{:S(2)}, u32[]{:S(2)}) collective-permute-start(bf16[4,64,128]{2,1,0:T(8,128)(2,1)S(1)} %get-tuple-element.51), channel_id=1, source_target_pairs={{1,2},{3,4},{5,6},{2,1},{4,3},{6,5},{9,10},{11,12},{13,14},{10,9},... | collective-permute-start | bytes 196616 | tf_op jit(solution)/shard_map/ppermute | solution.py:333
  8.0 1.9 %collective-permute-start.2 = (bf16[4,64,128]{2,1,0:T(8,128)(2,1)S(1)}, bf16[4,64,128]{2,1,0:T(8,128)(2,1)S(1)}, u32[]{:S(2)}, u32[]{:S(2)}) collective-permute-start(bf16[4,64,128]{2,1,0:T(8,128)(2,1)S(1)} %get-tuple-element.52), channel_id=1, source_target_pairs={{0,1},{1,0},{2,3},{3,2},{4,5},{5,4},{6,7},{7,6},{8,9},{9,8},{10,11... | collective-permute-start | bytes 196616 | tf_op jit(solution)/shard_map/ppermute | solution.py:312
  9.8 2.8 %shard_map.103 = (bf16[512,512]{1,0:T(8,128)(2,1)S(1)}, f32[8,512]{1,0:T(8,128)S(1)}, f32[27,128]{1,0:T(8,128)S(1)}, bf16[256,3456]{1,0:T(8,128)(2,1)S(1)}, bf16...) custom-call(bf16[8,64,512]{2,1,0:T(8,128)(2,1)} %bitcast.24, ...), custom_call_target="tpu_custom_call" | custom-call | flops 4000000000 | bytes 1048576 | tf_op jit(solution)/shard_map/pallas_call | solution.py:295
  12.6 0.0 collective-permute-done.1.far_slots
  12.6 0.0 collective-permute-done.3.across
  12.6 0.0 collective-permute-done.2.beside
  12.6 0.0 collective-permute-done.across
  12.7 0.1 collective-permute-start.5
  12.8 0.0 collective-permute-done.4.beside
  12.8 1.5 %collective-permute-done.5.diagonal = bf16[8,64,256]{2,1,0:T(8,128)(2,1)S(1)} collective-permute-done((bf16[8,64,256]{2,1,0:T(8,128)(2,1)S(1)}, bf16[8,64,256]{2,1,0:T(8,128)(2,1)S(1)}, u32[]{:S(2)}, u32[]{:S(2)}) %collective-permute-start.5) | collective-permute-done | bytes 262176 | tf_op jit(solution)/shard_map/ppermute | solution.py:312
  14.3 0.2 shard_map.106
  14.4 1.2 %collective-permute-start.6 = (bf16[4,64,256]{2,1,0:T(8,128)(2,1)S(1)}, bf16[4,64,256]{2,1,0:T(8,128)(2,1)S(1)}, u32[]{:S(2)}, u32[]{:S(2)}) collective-permute-start(bf16[4,64,256]{2,1,0:T(8,128)(2,1)S(1)} %shard_map.106), channel_id=1, source_target_pairs={{0,4},{1,5},{2,6},{3,7},{4,0},{5,1},{6,2},{7,3},{8,12},{9,13},{10,... | collective-permute-start | bytes 393224 | tf_op jit(solution)/shard_map/ppermute | solution.py:312
  15.6 3.5 %shard_map.104 = (bf16[4,640,512]{2,1,0:T(8,128)(2,1)S(1)}, f32[512,512]{1,0:T(8,128)S(1)}, bf16[512,512]{1,0:T(8,128)(2,1)S(1)}, bf16[128,512]{1,0:T(8,128)(2,1...) custom-call(bf16[512,512]{1,0:T(8,128)(2,1)S(1)} %get-tuple-element.28.inner, ...), custom_call_target="tpu_custom_call" | custom-call | flops 4000000000 | bytes 1048576 | tf_op jit(solution)/shard_map/pallas_call | solution.py:295
  19.1 0.6 %shard_map.105 = (bf16[8,64,256]{2,1,0:T(8,128)(2,1)S(1)}, s32[8,256]{1,0:T(8,128)S(1)}) custom-call(s32[8]{0:T(128)S(1)} %get-tuple-element.42.slots, bf16[8,64,256]{2,1,0:T(8,128)(2,1)S(1)} %get-tuple-element.43.own, bf16[8,64,256]{2,1,0:T(8,128)(2,1)S(1)} %collective-permute-done.4.beside, bf16[8,64,256]{2,1,0:T(8,128)(2,1)S(1)} %collective-permute-done.across, ...), custom_call_target="tpu_custom_call" | custom-call | bytes 1048576 | tf_op jit(solution)/shard_map/pallas_call | solution.py:295
  19.7 4.0 %collective-permute-done.6.far = bf16[4,64,256]{2,1,0:T(8,128)(2,1)S(1)} collective-permute-done((bf16[4,64,256]{2,1,0:T(8,128)(2,1)S(1)}, bf16[4,64,256]{2,1,0:T(8,128)(2,1)S(1)}, u32[]{:S(2)}, u32[]{:S(2)}) %collective-permute-start.6) | collective-permute-done | bytes 131104 | tf_op jit(solution)/shard_map/ppermute | solution.py:312
  23.7 2.8 %shard_map.107 = bf16[2,2,416,128]{3,2,1,0:T(8,128)(2,1)S(1)} custom-call(bf16[4,640,512]{2,1,0:T(8,128)(2,1)S(1)} %get-tuple-element.36.shifted, f32[512,512]{1,0:T(8,128)S(1)} %get-tuple-element.37.slope_pre, bf16[512,512]{1,0:T(8,128)(2,1)S(1)} %get-tuple-element.38.hid, bf16[128,512]{1,0:T(8,128)(2,1)S(1)} %get-tuple-element.39.coarse, ...), custom_call_target="tpu_custom_call" | custom-call | flops 4000000000 | bytes 1048576 | tf_op jit(solution)/shard_map/pallas_call | solution.py:295
  26.6 0.1 collective-permute-start.13
  26.7 0.5 collective-permute-start.7
  27.2 0.8 %collective-permute-done.13 = bf16[416,128]{1,0:T(8,128)(2,1)S(1)} collective-permute-done((bf16[416,128]{1,0:T(8,128)(2,1)S(1)}, bf16[416,128]{1,0:T(8,128)(2,1)S(1)}, u32[]{:S(2)}, u32[]{:S(2)}) %collective-permute-start.13) | collective-permute-done | bytes 106528 | tf_op jit(solution)/shard_map/ppermute | solution.py:312
  28.0 0.2 collective-permute-done.7
  28.2 1.6 %collective-permute-start.14 = (bf16[416,128]{1,0:T(8,128)(2,1)S(1)}, bf16[416,128]{1,0:T(8,128)(2,1)S(1)}, u32[]{:S(2)}, u32[]{:S(2)}) collective-permute-start(bf16[416,128]{1,0:T(8,128)(2,1)S(1)} %get-tuple-element.53), channel_id=1, source_target_pairs={{0,8},{8,0},{16,24},{24,16},{1,9},{9,1},{17,25},{25,17},{2,10},{10... | collective-permute-start | bytes 319496 | tf_op jit(solution)/shard_map/ppermute | solution.py:312
  29.7 0.0 collective-permute-start.8
  29.7 3.7 %collective-permute-done.14 = bf16[416,128]{1,0:T(8,128)(2,1)S(1)} collective-permute-done((bf16[416,128]{1,0:T(8,128)(2,1)S(1)}, bf16[416,128]{1,0:T(8,128)(2,1)S(1)}, u32[]{:S(2)}, u32[]{:S(2)}) %collective-permute-start.14) | collective-permute-done | bytes 106528 | tf_op jit(solution)/shard_map/ppermute | solution.py:312
  33.5 1.6 %collective-permute-start.15 = (bf16[416,128]{1,0:T(8,128)(2,1)S(1)}, bf16[416,128]{1,0:T(8,128)(2,1)S(1)}, u32[]{:S(2)}, u32[]{:S(2)}) collective-permute-start(bf16[416,128]{1,0:T(8,128)(2,1)S(1)} %add.36), channel_id=1, source_target_pairs={{0,16},{8,24},{16,0},{24,8},{1,17},{9,25},{17,1},{25,9},{2,18},{10... | collective-permute-start | bytes 319496 | tf_op jit(solution)/shard_map/ppermute | solution.py:312
  35.1 0.0 collective-permute-done.8
  35.1 1.6 %collective-permute-start.9 = (bf16[416,128]{1,0:T(8,128)(2,1)S(1)}, bf16[416,128]{1,0:T(8,128)(2,1)S(1)}, u32[]{:S(2)}, u32[]{:S(2)}) collective-permute-start(bf16[416,128]{1,0:T(8,128)(2,1)S(1)} %add.31), channel_id=1, source_target_pairs={{0,8},{8,0},{16,24},{24,16},{1,9},{9,1},{17,25},{25,17},{2,10},{10... | collective-permute-start | bytes 319496 | tf_op jit(solution)/shard_map/ppermute | solution.py:312
  36.7 1.6 %collective-permute-done.15 = bf16[416,128]{1,0:T(8,128)(2,1)S(1)} collective-permute-done((bf16[416,128]{1,0:T(8,128)(2,1)S(1)}, bf16[416,128]{1,0:T(8,128)(2,1)S(1)}, u32[]{:S(2)}, u32[]{:S(2)}) %collective-permute-start.15) | collective-permute-done | bytes 106528 | tf_op jit(solution)/shard_map/ppermute | solution.py:312
  38.3 0.1 collective-permute-start.16
  38.4 1.5 %collective-permute-done.9 = bf16[416,128]{1,0:T(8,128)(2,1)S(1)} collective-permute-done((bf16[416,128]{1,0:T(8,128)(2,1)S(1)}, bf16[416,128]{1,0:T(8,128)(2,1)S(1)}, u32[]{:S(2)}, u32[]{:S(2)}) %collective-permute-start.9) | collective-permute-done | bytes 106528 | tf_op jit(solution)/shard_map/ppermute | solution.py:312
  39.9 1.2 %collective-permute-start.10 = (bf16[416,128]{1,0:T(8,128)(2,1)S(1)}, bf16[416,128]{1,0:T(8,128)(2,1)S(1)}, u32[]{:S(2)}, u32[]{:S(2)}) collective-permute-start(bf16[416,128]{1,0:T(8,128)(2,1)S(1)} %add.32), channel_id=1, source_target_pairs={{0,16},{8,24},{16,0},{24,8},{1,17},{9,25},{17,1},{25,9},{2,18},{10... | collective-permute-start | bytes 319496 | tf_op jit(solution)/shard_map/ppermute | solution.py:312
  41.1 3.3 %collective-permute-done.16 = bf16[416,128]{1,0:T(8,128)(2,1)S(1)} collective-permute-done((bf16[416,128]{1,0:T(8,128)(2,1)S(1)}, bf16[416,128]{1,0:T(8,128)(2,1)S(1)}, u32[]{:S(2)}, u32[]{:S(2)}) %collective-permute-start.16) | collective-permute-done | bytes 106528 | tf_op jit(solution)/shard_map/ppermute | solution.py:312
  44.5 0.1 collective-permute-start.17
  44.6 0.1 collective-permute-done.10
  44.7 2.3 %collective-permute-start.11 = (bf16[416,128]{1,0:T(8,128)(2,1)S(1)}, bf16[416,128]{1,0:T(8,128)(2,1)S(1)}, u32[]{:S(2)}, u32[]{:S(2)}) collective-permute-start(bf16[416,128]{1,0:T(8,128)(2,1)S(1)} %add.33), channel_id=1, source_target_pairs={{0,4},{1,5},{2,6},{3,7},{4,0},{5,1},{6,2},{7,3},{8,12},{9,13},{10,... | collective-permute-start | bytes 319496 | tf_op jit(solution)/shard_map/ppermute | solution.py:312
  47.0 2.3 %collective-permute-done.17 = bf16[416,128]{1,0:T(8,128)(2,1)S(1)} collective-permute-done((bf16[416,128]{1,0:T(8,128)(2,1)S(1)}, bf16[416,128]{1,0:T(8,128)(2,1)S(1)}, u32[]{:S(2)}, u32[]{:S(2)}) %collective-permute-start.17) | collective-permute-done | bytes 106528 | tf_op jit(solution)/shard_map/ppermute | solution.py:312
  49.3 0.1 collective-permute-start.18
  49.4 1.0 %collective-permute-done.11 = bf16[416,128]{1,0:T(8,128)(2,1)S(1)} collective-permute-done((bf16[416,128]{1,0:T(8,128)(2,1)S(1)}, bf16[416,128]{1,0:T(8,128)(2,1)S(1)}, u32[]{:S(2)}, u32[]{:S(2)}) %collective-permute-start.11) | collective-permute-done | bytes 106528 | tf_op jit(solution)/shard_map/ppermute | solution.py:312
  50.4 0.1 collective-permute-start.12
  50.5 0.2 collective-permute-done.18.other_b
  50.7 1.1 %collective-permute-done.12.other_a = bf16[416,128]{1,0:T(8,128)(2,1)S(1)} collective-permute-done((bf16[416,128]{1,0:T(8,128)(2,1)S(1)}, bf16[416,128]{1,0:T(8,128)(2,1)S(1)}, u32[]{:S(2)}, u32[]{:S(2)}) %collective-permute-start.12) | collective-permute-done | bytes 106528 | tf_op jit(solution)/shard_map/ppermute | solution.py:312
  51.8 1.2 %shard_map.108 = (f32[27,64,64]{2,1,0:T(8,128)}, f32[8,64,128]{2,1,0:T(8,128)}, f32[128,256]{1,0:T(8,128)}) custom-call(bf16[416,128]{1,0:T(8,128)(2,1)S(1)} %add.34.mine_a, bf16[416,128]{1,0:T(8,128)(2,1)S(1)} %collective-permute-done.12.other_a, bf16[416,128]{1,0:T(8,128)(2,1)S(1)} %add.39.mine_b, bf16[416,128]{1,0:T(8,128)(2,1)S(1)} %collective-permute-done.18.other_b), custom_call_target="tpu_custom_call" | custom-call | bytes 1048576 | tf_op jit(solution)/shard_map/pallas_call | solution.py:295
  (10 shorter events, 0.3 us)
Async XLA Ops:
  0.6 12.2 %collective-permute-start.4 = (bf16[8,64,256]{2,1,0:T(8,128)(2,1)}, bf16[8,64,256]{2,1,0:T(8,128)(2,1)S(1)}, u32[]{:S(2)}, u32[]{:S(2)}) collective-permute-start(bf16[8,64,256]{2,1,0:T(8,128)(2,1)} %bitcast.27), channel_id=1, source_target_pairs={{0,1},{1,0},{2,3},{3,2},{4,5},{5,4},{6,7},{7,6},{8,9},{9,8},{10,11... | collective-permute-start | bytes 786440 | tf_op jit(solution)/shard_map/ppermute | solution.py:312
  1.1 11.5 %collective-permute-start = (bf16[8,64,256]{2,1,0:T(8,128)(2,1)}, bf16[8,64,256]{2,1,0:T(8,128)(2,1)S(1)}, u32[]{:S(2)}, u32[]{:S(2)}) collective-permute-start(bf16[8,64,256]{2,1,0:T(8,128)(2,1)} %bitcast.28), channel_id=1, source_target_pairs={{0,2},{1,3},{2,0},{3,1},{4,6},{5,7},{6,4},{7,5},{8,10},{9,11},{10,... | collective-permute-start | bytes 786440 | tf_op jit(solution)/shard_map/ppermute | solution.py:312
  3.8 8.8 %collective-permute-start.1 = (s32[1,8]{1,0:T(1,128)}, s32[1,8]{1,0:T(1,128)S(1)}, u32[]{:S(2)}, u32[]{:S(2)}) collective-permute-start(s32[1,8]{1,0:T(1,128)} %param.11), channel_id=1, source_target_pairs={{0,4},{1,5},{2,6},{3,7},{4,0},{5,1},{6,2},{7,3},{8,12},{9,13},{10,... | collective-permute-start | bytes 104 | tf_op jit(solution)/shard_map/ppermute | solution.py:312
  7.3 5.3 %collective-permute-start.3 = (bf16[4,64,128]{2,1,0:T(8,128)(2,1)S(1)}, bf16[4,64,128]{2,1,0:T(8,128)(2,1)S(1)}, u32[]{:S(2)}, u32[]{:S(2)}) collective-permute-start(bf16[4,64,128]{2,1,0:T(8,128)(2,1)S(1)} %get-tuple-element.51), channel_id=1, source_target_pairs={{1,2},{3,4},{5,6},{2,1},{4,3},{6,5},{9,10},{11,12},{13,14},{10,9},... | collective-permute-start | bytes 196616 | tf_op jit(solution)/shard_map/ppermute | solution.py:333
  8.0 4.7 %collective-permute-start.2 = (bf16[4,64,128]{2,1,0:T(8,128)(2,1)S(1)}, bf16[4,64,128]{2,1,0:T(8,128)(2,1)S(1)}, u32[]{:S(2)}, u32[]{:S(2)}) collective-permute-start(bf16[4,64,128]{2,1,0:T(8,128)(2,1)S(1)} %get-tuple-element.52), channel_id=1, source_target_pairs={{0,1},{1,0},{2,3},{3,2},{4,5},{5,4},{6,7},{7,6},{8,9},{9,8},{10,11... | collective-permute-start | bytes 196616 | tf_op jit(solution)/shard_map/ppermute | solution.py:312
  12.7 1.6 %collective-permute-start.5 = (bf16[8,64,256]{2,1,0:T(8,128)(2,1)S(1)}, bf16[8,64,256]{2,1,0:T(8,128)(2,1)S(1)}, u32[]{:S(2)}, u32[]{:S(2)}) collective-permute-start(bf16[8,64,256]{2,1,0:T(8,128)(2,1)S(1)} %collective-permute-done.across), channel_id=1, source_target_pairs={{0,1},{1,0},{2,3},{3,2},{4,5},{5,4},{6,7},{7,6},{8,9},{9,8},{10,11... | collective-permute-start | bytes 786440 | tf_op jit(solution)/shard_map/ppermute | solution.py:312
  14.4 9.3 %collective-permute-start.6 = (bf16[4,64,256]{2,1,0:T(8,128)(2,1)S(1)}, bf16[4,64,256]{2,1,0:T(8,128)(2,1)S(1)}, u32[]{:S(2)}, u32[]{:S(2)}) collective-permute-start(bf16[4,64,256]{2,1,0:T(8,128)(2,1)S(1)} %shard_map.106), channel_id=1, source_target_pairs={{0,4},{1,5},{2,6},{3,7},{4,0},{5,1},{6,2},{7,3},{8,12},{9,13},{10,... | collective-permute-start | bytes 393224 | tf_op jit(solution)/shard_map/ppermute | solution.py:312
  26.6 1.4 %collective-permute-start.13 = (bf16[416,128]{1,0:T(8,128)(2,1)S(1)}, bf16[416,128]{1,0:T(8,128)(2,1)S(1)}, u32[]{:S(2)}, u32[]{:S(2)}) collective-permute-start(bf16[416,128]{1,0:T(8,128)(2,1)S(1)} %get-tuple-element.55), channel_id=1, source_target_pairs={{0,1},{1,0},{2,3},{3,2},{4,5},{5,4},{6,7},{7,6},{8,9},{9,8},{10,11... | collective-permute-start | bytes 319496 | tf_op jit(solution)/shard_map/ppermute | solution.py:312
  26.7 1.5 %collective-permute-start.7 = (bf16[416,128]{1,0:T(8,128)(2,1)S(1)}, bf16[416,128]{1,0:T(8,128)(2,1)S(1)}, u32[]{:S(2)}, u32[]{:S(2)}) collective-permute-start(bf16[416,128]{1,0:T(8,128)(2,1)S(1)} %get-tuple-element.56), channel_id=1, source_target_pairs={{0,1},{1,0},{2,3},{3,2},{4,5},{5,4},{6,7},{7,6},{8,9},{9,8},{10,11... | collective-permute-start | bytes 319496 | tf_op jit(solution)/shard_map/ppermute | solution.py:312
  28.2 5.3 %collective-permute-start.14 = (bf16[416,128]{1,0:T(8,128)(2,1)S(1)}, bf16[416,128]{1,0:T(8,128)(2,1)S(1)}, u32[]{:S(2)}, u32[]{:S(2)}) collective-permute-start(bf16[416,128]{1,0:T(8,128)(2,1)S(1)} %get-tuple-element.53), channel_id=1, source_target_pairs={{0,8},{8,0},{16,24},{24,16},{1,9},{9,1},{17,25},{25,17},{2,10},{10... | collective-permute-start | bytes 319496 | tf_op jit(solution)/shard_map/ppermute | solution.py:312
  29.7 5.3 %collective-permute-start.8 = (bf16[416,128]{1,0:T(8,128)(2,1)S(1)}, bf16[416,128]{1,0:T(8,128)(2,1)S(1)}, u32[]{:S(2)}, u32[]{:S(2)}) collective-permute-start(bf16[416,128]{1,0:T(8,128)(2,1)S(1)} %get-tuple-element.54), channel_id=1, source_target_pairs={{0,2},{1,3},{2,0},{3,1},{4,6},{5,7},{6,4},{7,5},{8,10},{9,11},{10,... | collective-permute-start | bytes 319496 | tf_op jit(solution)/shard_map/ppermute | solution.py:312
  33.5 4.8 %collective-permute-start.15 = (bf16[416,128]{1,0:T(8,128)(2,1)S(1)}, bf16[416,128]{1,0:T(8,128)(2,1)S(1)}, u32[]{:S(2)}, u32[]{:S(2)}) collective-permute-start(bf16[416,128]{1,0:T(8,128)(2,1)S(1)} %add.36), channel_id=1, source_target_pairs={{0,16},{8,24},{16,0},{24,8},{1,17},{9,25},{17,1},{25,9},{2,18},{10... | collective-permute-start | bytes 319496 | tf_op jit(solution)/shard_map/ppermute | solution.py:312
  35.1 4.8 %collective-permute-start.9 = (bf16[416,128]{1,0:T(8,128)(2,1)S(1)}, bf16[416,128]{1,0:T(8,128)(2,1)S(1)}, u32[]{:S(2)}, u32[]{:S(2)}) collective-permute-start(bf16[416,128]{1,0:T(8,128)(2,1)S(1)} %add.31), channel_id=1, source_target_pairs={{0,8},{8,0},{16,24},{24,16},{1,9},{9,1},{17,25},{25,17},{2,10},{10... | collective-permute-start | bytes 319496 | tf_op jit(solution)/shard_map/ppermute | solution.py:312
  38.3 6.1 %collective-permute-start.16 = (bf16[416,128]{1,0:T(8,128)(2,1)S(1)}, bf16[416,128]{1,0:T(8,128)(2,1)S(1)}, u32[]{:S(2)}, u32[]{:S(2)}) collective-permute-start(bf16[416,128]{1,0:T(8,128)(2,1)S(1)} %add.37), channel_id=1, source_target_pairs={{0,4},{1,5},{2,6},{3,7},{4,0},{5,1},{6,2},{7,3},{8,12},{9,13},{10,... | collective-permute-start | bytes 319496 | tf_op jit(solution)/shard_map/ppermute | solution.py:312
  39.9 4.8 %collective-permute-start.10 = (bf16[416,128]{1,0:T(8,128)(2,1)S(1)}, bf16[416,128]{1,0:T(8,128)(2,1)S(1)}, u32[]{:S(2)}, u32[]{:S(2)}) collective-permute-start(bf16[416,128]{1,0:T(8,128)(2,1)S(1)} %add.32), channel_id=1, source_target_pairs={{0,16},{8,24},{16,0},{24,8},{1,17},{9,25},{17,1},{25,9},{2,18},{10... | collective-permute-start | bytes 319496 | tf_op jit(solution)/shard_map/ppermute | solution.py:312
  44.5 4.8 %collective-permute-start.17 = (bf16[416,128]{1,0:T(8,128)(2,1)S(1)}, bf16[416,128]{1,0:T(8,128)(2,1)S(1)}, u32[]{:S(2)}, u32[]{:S(2)}) collective-permute-start(bf16[416,128]{1,0:T(8,128)(2,1)S(1)} %add.38), channel_id=1, source_target_pairs={{0,2},{1,3},{2,0},{3,1},{4,6},{5,7},{6,4},{7,5},{8,10},{9,11},{10,... | collective-permute-start | bytes 319496 | tf_op jit(solution)/shard_map/ppermute | solution.py:312
  44.7 5.7 %collective-permute-start.11 = (bf16[416,128]{1,0:T(8,128)(2,1)S(1)}, bf16[416,128]{1,0:T(8,128)(2,1)S(1)}, u32[]{:S(2)}, u32[]{:S(2)}) collective-permute-start(bf16[416,128]{1,0:T(8,128)(2,1)S(1)} %add.33), channel_id=1, source_target_pairs={{0,4},{1,5},{2,6},{3,7},{4,0},{5,1},{6,2},{7,3},{8,12},{9,13},{10,... | collective-permute-start | bytes 319496 | tf_op jit(solution)/shard_map/ppermute | solution.py:312
  49.3 1.4 %collective-permute-start.18 = (bf16[416,128]{1,0:T(8,128)(2,1)S(1)}, bf16[416,128]{1,0:T(8,128)(2,1)S(1)}, u32[]{:S(2)}, u32[]{:S(2)}) collective-permute-start(bf16[416,128]{1,0:T(8,128)(2,1)S(1)} %add.39.mine_b), channel_id=1, source_target_pairs={{0,1},{1,0},{2,3},{3,2},{4,5},{5,4},{6,7},{7,6},{8,9},{9,8},{10,11... | collective-permute-start | bytes 319496 | tf_op jit(solution)/shard_map/ppermute | solution.py:312
  50.4 1.4 %collective-permute-start.12 = (bf16[416,128]{1,0:T(8,128)(2,1)S(1)}, bf16[416,128]{1,0:T(8,128)(2,1)S(1)}, u32[]{:S(2)}, u32[]{:S(2)}) collective-permute-start(bf16[416,128]{1,0:T(8,128)(2,1)S(1)} %add.34.mine_a), channel_id=1, source_target_pairs={{0,1},{1,0},{2,3},{3,2},{4,5},{5,4},{6,7},{7,6},{8,9},{9,8},{10,11... | collective-permute-start | bytes 319496 | tf_op jit(solution)/shard_map/ppermute | solution.py:312

commit v5 on v4

--- a/solution.py
+++ b/solution.py
@@ -1,3 +1,5 @@
+import functools
+
 import jax
 import jax.numpy as jnp
 from jax import lax
@@ -181,13 +183,13 @@
     return value
 
 
-def reply_kernel(far_slots, own, beside, across, diagonal, reply):
+def reply_kernel(chip, far_slots, even, odd, reply):
     me = lax.axis_index("brick")
     asked = far_slots[...]
-    for i in range(4):
-        mine = (asked >> 3) == (me & 4) + i
+    for k in range(2):
+        mine = (asked >> 3) == (me & 4) + ((me & 2) ^ chip) + k
         slot = jnp.sum(jnp.where(mine, (asked & 7).astype(F32), 0.0)).astype(jnp.int32)
-        reply[i] = pick((own, beside, across, diagonal), (me & 3) ^ i, slot)
+        reply[k] = jnp.where((me & 1) == k, even[slot], odd[slot])
 
 
 def near_kernel(slots, own, beside, across, diagonal, near, place):
@@ -195,12 +197,12 @@
     for b in range(8):
         target = slots[b] >> 3
         near[b] = pick((own, beside, across, diagonal), (target ^ me) & 3, slots[b] & 7)
-        at = jnp.where(((target ^ me) & 4) == 0, -1, target & 3)
+        at = jnp.where(((target ^ me) & 4) == 0, -1, (target & 3) ^ (me & 2))
         place[b : b + 1, :] = jnp.full((1, 256), at, jnp.int32)
 
 
 def backward_kernel(
-    shifted, slope_pre, hid, coarse, slope_down, slope_point, near, place, far, wd, wp, wire,
+    shifted, slope_pre, hid, coarse, slope_down, slope_point, near, place, far, far_pair, wd, wp, wire,
     grads,
 ):
     me = lax.axis_index("brick")
@@ -218,8 +220,8 @@
     wanted = []
     for b in range(8):
         value, at = near[b].astype(F32), place[b : b + 1, :]
-        for i in range(4):
-            value = jnp.where(at == i, far[i].astype(F32), value)
+        for i, other in enumerate((far[0], far[1], far_pair[0], far_pair[1])):
+            value = jnp.where(at == i, other.astype(F32), value)
         wanted.append(value)
     parts = [wanted[b][16 * p : 16 * p + 16] for p in range(4) for b in range(8)]
     cot_rows = jnp.concatenate(parts, axis=0)
@@ -360,14 +362,17 @@
             (swap(own, "brick", 2), swap(owners, "brick", 4), planes, beside, across)
         )
         tables = (own_copy, swap(own, "brick", 1), partner, swap(partner, "brick", 1))
-        reply = call(reply_kernel, shape((4, 64, 256), BF16), (far_slots, *tables))
+        fars = []
+        for chip in (0, 2):
+            kernel = functools.partial(reply_kernel, chip)
+            reply = call(kernel, shape((2, 64, 256), BF16), (far_slots, *tables[chip : chip + 2]))
+            fars.append(swap(reply, "brick", 4))
         near, place = call(
             near_kernel,
             (shape((8, 64, 256), BF16), shape((8, 256), jnp.int32)),
             (slots_copy, *tables),
             specs=[SMEM] + [VMEM] * 4,
         )
-        far = swap(reply, "brick", 4)
     else:
         wanted = jnp.arange(brick_size, dtype=jnp.int32)[:, None] == (slots >> 3)[None, :]
         request = jnp.max(jnp.where(wanted, (slots & 7)[None, :], 0), axis=1)
@@ -375,7 +380,7 @@
         reply = jnp.take(own, arrived, axis=0, mode="clip")
         fetched = lax.all_to_all(reply, "brick", split_axis=0, concat_axis=0, tiled=True)
         near = jnp.take(fetched, slots >> 3, axis=0, mode="clip")
-        far, place = near[:4], jnp.full((8, 256), -1, jnp.int32)
+        fars, place = [near[:2], near[2:4]], jnp.full((8, 256), -1, jnp.int32)
     saved = call(
         forward_kernel,
         (
@@ -393,7 +398,7 @@
     wire = call(
         backward_kernel,
         shape((2, 2, PART, 128), BF16),
-        (*saved, near, place, far, wd, wp),
+        (*saved, near, place, *fars, wd, wp),
         scratch=[pltpu.VMEM((256, 1024), BF16)],
         flops=4 * 10**9,
     )

time: 53.2 us -> 52 us (0.977)
  waiting for transfers between devices: 21.4 us -> 18.4 us
  starting transfers between devices: 18.6 us -> 20.3 us
    ppermute x18 -> x19, waiting for transfers between devices: 21.4 us -> 18.4 us  [swap(): return lax.ppermute(value, axis, [(i, i ^ bit) for i in range(size)])]
    ppermute x18 -> x19, starting transfers between devices: 18 us -> 19.6 us  [swap(): return lax.ppermute(value, axis, [(i, i ^ bit) for i in range(size)])]
    pallas_call x6 -> x7, Pallas kernels: 11 us -> 11.1 us  [call(): pl.pallas_call(kernel, out_shape=outs, in_specs=specs or [VMEM] * len(ins...]
  transfers between devices with their start and end apart: 19 -> 20, of which waited for: 13 -> 12; matrix products, arithmetic and copies ran while one was open for 2% -> 2% of each run, Pallas kernels for 13% -> 14%
where the time goes in v5:
time: 52 us; the launch traced here: 51.8 us
  starting transfers between devices  20.3 us (39%)
  waiting for transfers between devices  18.4 us (35%)
  Pallas kernels  11.1 us (21%)
  other arithmetic  1.18 us (2%)
  between operations  0.82 us (2%)
    ppermute x19, starting transfers between devices, swap(): return lax.ppermute(value, axis, [(i, i ^ bit) for i in range(size)])  19.6 us
    ppermute x19, waiting for transfers between devices, swap(): return lax.ppermute(value, axis, [(i, i ^ bit) for i in range(size)])  18.4 us
    pallas_call x7, Pallas kernels, call(): pl.pallas_call(kernel, out_shape=outs, in_specs=specs or [VMEM] * len(ins...  11.1 us
  transfers between devices with their start and end apart: 20, of which 12 were waited for; matrix products, arithmetic and copies ran while one was open for 2% of the time, Pallas kernels for 14%

profile of v5, /device:TPU:0, one launch (start us, length us, event | category | flops | bytes accessed | tf_op | source)
XLA Modules:
  0.0 51.8 jit_solution(9932524052087456725)
XLA Ops:
  0.6 0.5 collective-permute-start.4
  1.1 2.7 %collective-permute-start = (bf16[8,64,256]{2,1,0:T(8,128)(2,1)}, bf16[8,64,256]{2,1,0:T(8,128)(2,1)S(1)}, u32[]{:S(2)}, u32[]{:S(2)}) collective-permute-start(bf16[8,64,256]{2,1,0:T(8,128)(2,1)} %bitcast.28), channel_id=1, source_target_pairs={{0,2},{1,3},{2,0},{3,1},{4,6},{5,7},{6,4},{7,5},{8,10},{9,11},{10,... | collective-permute-start | bytes 786440 | tf_op jit(solution)/shard_map/ppermute | solution.py:314
  3.8 2.6 %collective-permute-start.1 = (s32[1,8]{1,0:T(1,128)}, s32[1,8]{1,0:T(1,128)S(1)}, u32[]{:S(2)}, u32[]{:S(2)}) collective-permute-start(s32[1,8]{1,0:T(1,128)} %param.11), channel_id=1, source_target_pairs={{0,4},{1,5},{2,6},{3,7},{4,0},{5,1},{6,2},{7,3},{8,12},{9,13},{10,... | collective-permute-start | bytes 104 | tf_op jit(solution)/shard_map/ppermute | solution.py:314
  6.4 0.9 %broadcast_select_fusion = (bf16[4,64,128]{2,1,0:T(8,128)(2,1)S(1)}, bf16[4,64,128]{2,1,0:T(8,128)(2,1)S(1)}) fusion(pred[]{:T(512)S(6)} %eq.4, bf16[8,64,512]{2,1,0:T(8,128)(2,1)} %bitcast.23), kind=kLoop, calls=%fused_computation.6 | loop fusion | flops 65536 | bytes 262145 | tf_op jit(solution)/shard_map/jit(_where)/select_n | solution.py:335
  7.3 0.7 %collective-permute-start.3 = (bf16[4,64,128]{2,1,0:T(8,128)(2,1)S(1)}, bf16[4,64,128]{2,1,0:T(8,128)(2,1)S(1)}, u32[]{:S(2)}, u32[]{:S(2)}) collective-permute-start(bf16[4,64,128]{2,1,0:T(8,128)(2,1)S(1)} %get-tuple-element.51), channel_id=1, source_target_pairs={{1,2},{3,4},{5,6},{2,1},{4,3},{6,5},{9,10},{11,12},{13,14},{10,9},... | collective-permute-start | bytes 196616 | tf_op jit(solution)/shard_map/ppermute | solution.py:335
  8.0 1.9 %collective-permute-start.2 = (bf16[4,64,128]{2,1,0:T(8,128)(2,1)S(1)}, bf16[4,64,128]{2,1,0:T(8,128)(2,1)S(1)}, u32[]{:S(2)}, u32[]{:S(2)}) collective-permute-start(bf16[4,64,128]{2,1,0:T(8,128)(2,1)S(1)} %get-tuple-element.52), channel_id=1, source_target_pairs={{0,1},{1,0},{2,3},{3,2},{4,5},{5,4},{6,7},{7,6},{8,9},{9,8},{10,11... | collective-permute-start | bytes 196616 | tf_op jit(solution)/shard_map/ppermute | solution.py:314
  9.8 2.8 %shard_map.103 = (bf16[512,512]{1,0:T(8,128)(2,1)S(1)}, f32[8,512]{1,0:T(8,128)S(1)}, f32[27,128]{1,0:T(8,128)S(1)}, bf16[256,3456]{1,0:T(8,128)(2,1)S(1)}, bf16...) custom-call(bf16[8,64,512]{2,1,0:T(8,128)(2,1)} %bitcast.24, ...), custom_call_target="tpu_custom_call" | custom-call | flops 4000000000 | bytes 1048576 | tf_op jit(solution)/shard_map/pallas_call | solution.py:297
  12.6 0.0 collective-permute-done.1.far_slots
  12.6 0.0 collective-permute-done.3.across
  12.6 0.0 collective-permute-done.2.beside
  12.6 0.0 collective-permute-done.across.even
  12.7 0.1 collective-permute-start.5
  12.8 0.0 collective-permute-done.4.beside.odd
  12.8 0.1 shard_map.106
  12.9 1.5 %collective-permute-start.6 = (bf16[2,64,256]{2,1,0:T(8,128)(2,1)S(1)}, bf16[2,64,256]{2,1,0:T(8,128)(2,1)S(1)}, u32[]{:S(2)}, u32[]{:S(2)}) collective-permute-start(bf16[2,64,256]{2,1,0:T(8,128)(2,1)S(1)} %shard_map.106), channel_id=1, source_target_pairs={{0,4},{1,5},{2,6},{3,7},{4,0},{5,1},{6,2},{7,3},{8,12},{9,13},{10,... | collective-permute-start | bytes 196616 | tf_op jit(solution)/shard_map/ppermute | solution.py:314
  14.4 0.0 collective-permute-done.5.diagonal.odd
  14.4 0.1 shard_map.107
  14.6 1.5 %collective-permute-start.7 = (bf16[2,64,256]{2,1,0:T(8,128)(2,1)S(1)}, bf16[2,64,256]{2,1,0:T(8,128)(2,1)S(1)}, u32[]{:S(2)}, u32[]{:S(2)}) collective-permute-start(bf16[2,64,256]{2,1,0:T(8,128)(2,1)S(1)} %shard_map.107), channel_id=1, source_target_pairs={{0,4},{1,5},{2,6},{3,7},{4,0},{5,1},{6,2},{7,3},{8,12},{9,13},{10,... | collective-permute-start | bytes 196616 | tf_op jit(solution)/shard_map/ppermute | solution.py:314
  16.1 3.5 %shard_map.104 = (bf16[4,640,512]{2,1,0:T(8,128)(2,1)S(1)}, f32[512,512]{1,0:T(8,128)S(1)}, bf16[512,512]{1,0:T(8,128)(2,1)S(1)}, bf16[128,512]{1,0:T(8,128)(2,1...) custom-call(bf16[512,512]{1,0:T(8,128)(2,1)S(1)} %get-tuple-element.28.inner, ...), custom_call_target="tpu_custom_call" | custom-call | flops 4000000000 | bytes 1048576 | tf_op jit(solution)/shard_map/pallas_call | solution.py:297
  19.6 0.6 %shard_map.105 = (bf16[8,64,256]{2,1,0:T(8,128)(2,1)S(1)}, s32[8,256]{1,0:T(8,128)S(1)}) custom-call(s32[8]{0:T(128)S(1)} %get-tuple-element.42.slots, bf16[8,64,256]{2,1,0:T(8,128)(2,1)S(1)} %get-tuple-element.43.own.even, bf16[8,64,256]{2,1,0:T(8,128)(2,1)S(1)} %collective-permute-done.4.beside.odd, ...), custom_call_target="tpu_custom_call" | custom-call | bytes 1048576 | tf_op jit(solution)/shard_map/pallas_call | solution.py:297
  20.2 1.4 %collective-permute-done.6.far = bf16[2,64,256]{2,1,0:T(8,128)(2,1)S(1)} collective-permute-done((bf16[2,64,256]{2,1,0:T(8,128)(2,1)S(1)}, bf16[2,64,256]{2,1,0:T(8,128)(2,1)S(1)}, u32[]{:S(2)}, u32[]{:S(2)}) %collective-permute-start.6) | collective-permute-done | bytes 65568 | tf_op jit(solution)/shard_map/ppermute | solution.py:314
  21.6 1.0 %collective-permute-done.7.far_pair = bf16[2,64,256]{2,1,0:T(8,128)(2,1)S(1)} collective-permute-done((bf16[2,64,256]{2,1,0:T(8,128)(2,1)S(1)}, bf16[2,64,256]{2,1,0:T(8,128)(2,1)S(1)}, u32[]{:S(2)}, u32[]{:S(2)}) %collective-permute-start.7) | collective-permute-done | bytes 65568 | tf_op jit(solution)/shard_map/ppermute | solution.py:314
  22.6 2.8 %shard_map.108 = bf16[2,2,416,128]{3,2,1,0:T(8,128)(2,1)S(1)} custom-call(bf16[4,640,512]{2,1,0:T(8,128)(2,1)S(1)} %get-tuple-element.36.shifted, f32[512,512]{1,0:T(8,128)S(1)} %get-tuple-element.37.slope_pre, bf16[512,512]{1,0:T(8,128)(2,1)S(1)} %get-tuple-element.38.hid, bf16[128,512]{1,0:T(8,128)(2,1)S(1)} %get-tuple-element.39.coarse, ...), custom_call_target="tpu_custom_call" | custom-call | flops 4000000000 | bytes 1048576 | tf_op jit(solution)/shard_map/pallas_call | solution.py:297
  25.4 0.1 collective-permute-start.14
  25.5 0.5 collective-permute-start.8
  26.0 0.8 %collective-permute-done.14 = bf16[416,128]{1,0:T(8,128)(2,1)S(1)} collective-permute-done((bf16[416,128]{1,0:T(8,128)(2,1)S(1)}, bf16[416,128]{1,0:T(8,128)(2,1)S(1)}, u32[]{:S(2)}, u32[]{:S(2)}) %collective-permute-start.14) | collective-permute-done | bytes 106528 | tf_op jit(solution)/shard_map/ppermute | solution.py:314
  26.8 0.2 collective-permute-done.8
  27.0 1.6 %collective-permute-start.15 = (bf16[416,128]{1,0:T(8,128)(2,1)S(1)}, bf16[416,128]{1,0:T(8,128)(2,1)S(1)}, u32[]{:S(2)}, u32[]{:S(2)}) collective-permute-start(bf16[416,128]{1,0:T(8,128)(2,1)S(1)} %get-tuple-element.53), channel_id=1, source_target_pairs={{0,8},{8,0},{16,24},{24,16},{1,9},{9,1},{17,25},{25,17},{2,10},{10... | collective-permute-start | bytes 319496 | tf_op jit(solution)/shard_map/ppermute | solution.py:314
  28.6 0.0 collective-permute-start.9
  28.6 3.7 %collective-permute-done.15 = bf16[416,128]{1,0:T(8,128)(2,1)S(1)} collective-permute-done((bf16[416,128]{1,0:T(8,128)(2,1)S(1)}, bf16[416,128]{1,0:T(8,128)(2,1)S(1)}, u32[]{:S(2)}, u32[]{:S(2)}) %collective-permute-start.15) | collective-permute-done | bytes 106528 | tf_op jit(solution)/shard_map/ppermute | solution.py:314
  32.3 1.6 %collective-permute-start.16 = (bf16[416,128]{1,0:T(8,128)(2,1)S(1)}, bf16[416,128]{1,0:T(8,128)(2,1)S(1)}, u32[]{:S(2)}, u32[]{:S(2)}) collective-permute-start(bf16[416,128]{1,0:T(8,128)(2,1)S(1)} %add.36), channel_id=1, source_target_pairs={{0,16},{8,24},{16,0},{24,8},{1,17},{9,25},{17,1},{25,9},{2,18},{10... | collective-permute-start | bytes 319496 | tf_op jit(solution)/shard_map/ppermute | solution.py:314
  33.9 0.0 collective-permute-done.9
  33.9 1.6 %collective-permute-start.10 = (bf16[416,128]{1,0:T(8,128)(2,1)S(1)}, bf16[416,128]{1,0:T(8,128)(2,1)S(1)}, u32[]{:S(2)}, u32[]{:S(2)}) collective-permute-start(bf16[416,128]{1,0:T(8,128)(2,1)S(1)} %add.31), channel_id=1, source_target_pairs={{0,8},{8,0},{16,24},{24,16},{1,9},{9,1},{17,25},{25,17},{2,10},{10... | collective-permute-start | bytes 319496 | tf_op jit(solution)/shard_map/ppermute | solution.py:314
  35.5 1.6 %collective-permute-done.16 = bf16[416,128]{1,0:T(8,128)(2,1)S(1)} collective-permute-done((bf16[416,128]{1,0:T(8,128)(2,1)S(1)}, bf16[416,128]{1,0:T(8,128)(2,1)S(1)}, u32[]{:S(2)}, u32[]{:S(2)}) %collective-permute-start.16) | collective-permute-done | bytes 106528 | tf_op jit(solution)/shard_map/ppermute | solution.py:314
  37.1 0.1 collective-permute-start.17
  37.2 1.5 %collective-permute-done.10 = bf16[416,128]{1,0:T(8,128)(2,1)S(1)} collective-permute-done((bf16[416,128]{1,0:T(8,128)(2,1)S(1)}, bf16[416,128]{1,0:T(8,128)(2,1)S(1)}, u32[]{:S(2)}, u32[]{:S(2)}) %collective-permute-start.10) | collective-permute-done | bytes 106528 | tf_op jit(solution)/shard_map/ppermute | solution.py:314
  38.8 1.2 %collective-permute-start.11 = (bf16[416,128]{1,0:T(8,128)(2,1)S(1)}, bf16[416,128]{1,0:T(8,128)(2,1)S(1)}, u32[]{:S(2)}, u32[]{:S(2)}) collective-permute-start(bf16[416,128]{1,0:T(8,128)(2,1)S(1)} %add.32), channel_id=1, source_target_pairs={{0,16},{8,24},{16,0},{24,8},{1,17},{9,25},{17,1},{25,9},{2,18},{10... | collective-permute-start | bytes 319496 | tf_op jit(solution)/shard_map/ppermute | solution.py:314
  39.9 3.1 %collective-permute-done.17 = bf16[416,128]{1,0:T(8,128)(2,1)S(1)} collective-permute-done((bf16[416,128]{1,0:T(8,128)(2,1)S(1)}, bf16[416,128]{1,0:T(8,128)(2,1)S(1)}, u32[]{:S(2)}, u32[]{:S(2)}) %collective-permute-start.17) | collective-permute-done | bytes 106528 | tf_op jit(solution)/shard_map/ppermute | solution.py:314
  43.0 0.1 collective-permute-start.18
  43.1 0.4 collective-permute-done.11
  43.6 2.1 %collective-permute-start.12 = (bf16[416,128]{1,0:T(8,128)(2,1)S(1)}, bf16[416,128]{1,0:T(8,128)(2,1)S(1)}, u32[]{:S(2)}, u32[]{:S(2)}) collective-permute-start(bf16[416,128]{1,0:T(8,128)(2,1)S(1)} %add.33), channel_id=1, source_target_pairs={{0,4},{1,5},{2,6},{3,7},{4,0},{5,1},{6,2},{7,3},{8,12},{9,13},{10,... | collective-permute-start | bytes 319496 | tf_op jit(solution)/shard_map/ppermute | solution.py:314
  45.6 2.2 %collective-permute-done.18 = bf16[416,128]{1,0:T(8,128)(2,1)S(1)} collective-permute-done((bf16[416,128]{1,0:T(8,128)(2,1)S(1)}, bf16[416,128]{1,0:T(8,128)(2,1)S(1)}, u32[]{:S(2)}, u32[]{:S(2)}) %collective-permute-start.18) | collective-permute-done | bytes 106528 | tf_op jit(solution)/shard_map/ppermute | solution.py:314
  47.8 0.1 collective-permute-start.19
  47.9 1.3 %collective-permute-done.12 = bf16[416,128]{1,0:T(8,128)(2,1)S(1)} collective-permute-done((bf16[416,128]{1,0:T(8,128)(2,1)S(1)}, bf16[416,128]{1,0:T(8,128)(2,1)S(1)}, u32[]{:S(2)}, u32[]{:S(2)}) %collective-permute-start.12) | collective-permute-done | bytes 106528 | tf_op jit(solution)/shard_map/ppermute | solution.py:314
  49.3 0.1 collective-permute-start.13
  49.4 0.0 collective-permute-done.19.other_b
  49.4 1.3 %collective-permute-done.13.other_a = bf16[416,128]{1,0:T(8,128)(2,1)S(1)} collective-permute-done((bf16[416,128]{1,0:T(8,128)(2,1)S(1)}, bf16[416,128]{1,0:T(8,128)(2,1)S(1)}, u32[]{:S(2)}, u32[]{:S(2)}) %collective-permute-start.13) | collective-permute-done | bytes 106528 | tf_op jit(solution)/shard_map/ppermute | solution.py:314
  50.7 1.2 %shard_map.109 = (f32[27,64,64]{2,1,0:T(8,128)}, f32[8,64,128]{2,1,0:T(8,128)}, f32[128,256]{1,0:T(8,128)}) custom-call(bf16[416,128]{1,0:T(8,128)(2,1)S(1)} %add.34.mine_a, bf16[416,128]{1,0:T(8,128)(2,1)S(1)} %collective-permute-done.13.other_a, bf16[416,128]{1,0:T(8,128)(2,1)S(1)} %add.39.mine_b, bf16[416,128]{1,0:T(8,128)(2,1)S(1)} %collective-permute-done.19.other_b), custom_call_target="tpu_custom_call" | custom-call | bytes 1048576 | tf_op jit(solution)/shard_map/pallas_call | solution.py:297
  (10 shorter events, 0.3 us)
Async XLA Ops:
  0.6 12.2 %collective-permute-start.4 = (bf16[8,64,256]{2,1,0:T(8,128)(2,1)}, bf16[8,64,256]{2,1,0:T(8,128)(2,1)S(1)}, u32[]{:S(2)}, u32[]{:S(2)}) collective-permute-start(bf16[8,64,256]{2,1,0:T(8,128)(2,1)} %bitcast.27), channel_id=1, source_target_pairs={{0,1},{1,0},{2,3},{3,2},{4,5},{5,4},{6,7},{7,6},{8,9},{9,8},{10,11... | collective-permute-start | bytes 786440 | tf_op jit(solution)/shard_map/ppermute | solution.py:314
  1.1 11.5 %collective-permute-start = (bf16[8,64,256]{2,1,0:T(8,128)(2,1)}, bf16[8,64,256]{2,1,0:T(8,128)(2,1)S(1)}, u32[]{:S(2)}, u32[]{:S(2)}) collective-permute-start(bf16[8,64,256]{2,1,0:T(8,128)(2,1)} %bitcast.28), channel_id=1, source_target_pairs={{0,2},{1,3},{2,0},{3,1},{4,6},{5,7},{6,4},{7,5},{8,10},{9,11},{10,... | collective-permute-start | bytes 786440 | tf_op jit(solution)/shard_map/ppermute | solution.py:314
  3.8 8.8 %collective-permute-start.1 = (s32[1,8]{1,0:T(1,128)}, s32[1,8]{1,0:T(1,128)S(1)}, u32[]{:S(2)}, u32[]{:S(2)}) collective-permute-start(s32[1,8]{1,0:T(1,128)} %param.11), channel_id=1, source_target_pairs={{0,4},{1,5},{2,6},{3,7},{4,0},{5,1},{6,2},{7,3},{8,12},{9,13},{10,... | collective-permute-start | bytes 104 | tf_op jit(solution)/shard_map/ppermute | solution.py:314
  7.3 5.3 %collective-permute-start.3 = (bf16[4,64,128]{2,1,0:T(8,128)(2,1)S(1)}, bf16[4,64,128]{2,1,0:T(8,128)(2,1)S(1)}, u32[]{:S(2)}, u32[]{:S(2)}) collective-permute-start(bf16[4,64,128]{2,1,0:T(8,128)(2,1)S(1)} %get-tuple-element.51), channel_id=1, source_target_pairs={{1,2},{3,4},{5,6},{2,1},{4,3},{6,5},{9,10},{11,12},{13,14},{10,9},... | collective-permute-start | bytes 196616 | tf_op jit(solution)/shard_map/ppermute | solution.py:335
  8.0 4.7 %collective-permute-start.2 = (bf16[4,64,128]{2,1,0:T(8,128)(2,1)S(1)}, bf16[4,64,128]{2,1,0:T(8,128)(2,1)S(1)}, u32[]{:S(2)}, u32[]{:S(2)}) collective-permute-start(bf16[4,64,128]{2,1,0:T(8,128)(2,1)S(1)} %get-tuple-element.52), channel_id=1, source_target_pairs={{0,1},{1,0},{2,3},{3,2},{4,5},{5,4},{6,7},{7,6},{8,9},{9,8},{10,11... | collective-permute-start | bytes 196616 | tf_op jit(solution)/shard_map/ppermute | solution.py:314
  12.7 1.8 %collective-permute-start.5 = (bf16[8,64,256]{2,1,0:T(8,128)(2,1)S(1)}, bf16[8,64,256]{2,1,0:T(8,128)(2,1)S(1)}, u32[]{:S(2)}, u32[]{:S(2)}) collective-permute-start(bf16[8,64,256]{2,1,0:T(8,128)(2,1)S(1)} %collective-permute-done.across.even), channel_id=1, source_target_pairs={{0,1},{1,0},{2,3},{3,2},{4,5},{5,4},{6,7},{7,6},{8,9},{9,8},{10,11... | collective-permute-start | bytes 786440 | tf_op jit(solution)/shard_map/ppermute | solution.py:314
  12.9 8.7 %collective-permute-start.6 = (bf16[2,64,256]{2,1,0:T(8,128)(2,1)S(1)}, bf16[2,64,256]{2,1,0:T(8,128)(2,1)S(1)}, u32[]{:S(2)}, u32[]{:S(2)}) collective-permute-start(bf16[2,64,256]{2,1,0:T(8,128)(2,1)S(1)} %shard_map.106), channel_id=1, source_target_pairs={{0,4},{1,5},{2,6},{3,7},{4,0},{5,1},{6,2},{7,3},{8,12},{9,13},{10,... | collective-permute-start | bytes 196616 | tf_op jit(solution)/shard_map/ppermute | solution.py:314
  14.6 8.0 %collective-permute-start.7 = (bf16[2,64,256]{2,1,0:T(8,128)(2,1)S(1)}, bf16[2,64,256]{2,1,0:T(8,128)(2,1)S(1)}, u32[]{:S(2)}, u32[]{:S(2)}) collective-permute-start(bf16[2,64,256]{2,1,0:T(8,128)(2,1)S(1)} %shard_map.107), channel_id=1, source_target_pairs={{0,4},{1,5},{2,6},{3,7},{4,0},{5,1},{6,2},{7,3},{8,12},{9,13},{10,... | collective-permute-start | bytes 196616 | tf_op jit(solution)/shard_map/ppermute | solution.py:314
  25.4 1.4 %collective-permute-start.14 = (bf16[416,128]{1,0:T(8,128)(2,1)S(1)}, bf16[416,128]{1,0:T(8,128)(2,1)S(1)}, u32[]{:S(2)}, u32[]{:S(2)}) collective-permute-start(bf16[416,128]{1,0:T(8,128)(2,1)S(1)} %get-tuple-element.55), channel_id=1, source_target_pairs={{0,1},{1,0},{2,3},{3,2},{4,5},{5,4},{6,7},{7,6},{8,9},{9,8},{10,11... | collective-permute-start | bytes 319496 | tf_op jit(solution)/shard_map/ppermute | solution.py:314
  25.5 1.5 %collective-permute-start.8 = (bf16[416,128]{1,0:T(8,128)(2,1)S(1)}, bf16[416,128]{1,0:T(8,128)(2,1)S(1)}, u32[]{:S(2)}, u32[]{:S(2)}) collective-permute-start(bf16[416,128]{1,0:T(8,128)(2,1)S(1)} %get-tuple-element.56), channel_id=1, source_target_pairs={{0,1},{1,0},{2,3},{3,2},{4,5},{5,4},{6,7},{7,6},{8,9},{9,8},{10,11... | collective-permute-start | bytes 319496 | tf_op jit(solution)/shard_map/ppermute | solution.py:314
  27.0 5.3 %collective-permute-start.15 = (bf16[416,128]{1,0:T(8,128)(2,1)S(1)}, bf16[416,128]{1,0:T(8,128)(2,1)S(1)}, u32[]{:S(2)}, u32[]{:S(2)}) collective-permute-start(bf16[416,128]{1,0:T(8,128)(2,1)S(1)} %get-tuple-element.53), channel_id=1, source_target_pairs={{0,8},{8,0},{16,24},{24,16},{1,9},{9,1},{17,25},{25,17},{2,10},{10... | collective-permute-start | bytes 319496 | tf_op jit(solution)/shard_map/ppermute | solution.py:314
  28.6 5.3 %collective-permute-start.9 = (bf16[416,128]{1,0:T(8,128)(2,1)S(1)}, bf16[416,128]{1,0:T(8,128)(2,1)S(1)}, u32[]{:S(2)}, u32[]{:S(2)}) collective-permute-start(bf16[416,128]{1,0:T(8,128)(2,1)S(1)} %get-tuple-element.54), channel_id=1, source_target_pairs={{0,2},{1,3},{2,0},{3,1},{4,6},{5,7},{6,4},{7,5},{8,10},{9,11},{10,... | collective-permute-start | bytes 319496 | tf_op jit(solution)/shard_map/ppermute | solution.py:314
  32.3 4.8 %collective-permute-start.16 = (bf16[416,128]{1,0:T(8,128)(2,1)S(1)}, bf16[416,128]{1,0:T(8,128)(2,1)S(1)}, u32[]{:S(2)}, u32[]{:S(2)}) collective-permute-start(bf16[416,128]{1,0:T(8,128)(2,1)S(1)} %add.36), channel_id=1, source_target_pairs={{0,16},{8,24},{16,0},{24,8},{1,17},{9,25},{17,1},{25,9},{2,18},{10... | collective-permute-start | bytes 319496 | tf_op jit(solution)/shard_map/ppermute | solution.py:314
  33.9 4.8 %collective-permute-start.10 = (bf16[416,128]{1,0:T(8,128)(2,1)S(1)}, bf16[416,128]{1,0:T(8,128)(2,1)S(1)}, u32[]{:S(2)}, u32[]{:S(2)}) collective-permute-start(bf16[416,128]{1,0:T(8,128)(2,1)S(1)} %add.31), channel_id=1, source_target_pairs={{0,8},{8,0},{16,24},{24,16},{1,9},{9,1},{17,25},{25,17},{2,10},{10... | collective-permute-start | bytes 319496 | tf_op jit(solution)/shard_map/ppermute | solution.py:314
  37.1 5.9 %collective-permute-start.17 = (bf16[416,128]{1,0:T(8,128)(2,1)S(1)}, bf16[416,128]{1,0:T(8,128)(2,1)S(1)}, u32[]{:S(2)}, u32[]{:S(2)}) collective-permute-start(bf16[416,128]{1,0:T(8,128)(2,1)S(1)} %add.37), channel_id=1, source_target_pairs={{0,4},{1,5},{2,6},{3,7},{4,0},{5,1},{6,2},{7,3},{8,12},{9,13},{10,... | collective-permute-start | bytes 319496 | tf_op jit(solution)/shard_map/ppermute | solution.py:314
  38.8 4.8 %collective-permute-start.11 = (bf16[416,128]{1,0:T(8,128)(2,1)S(1)}, bf16[416,128]{1,0:T(8,128)(2,1)S(1)}, u32[]{:S(2)}, u32[]{:S(2)}) collective-permute-start(bf16[416,128]{1,0:T(8,128)(2,1)S(1)} %add.32), channel_id=1, source_target_pairs={{0,16},{8,24},{16,0},{24,8},{1,17},{9,25},{17,1},{25,9},{2,18},{10... | collective-permute-start | bytes 319496 | tf_op jit(solution)/shard_map/ppermute | solution.py:314
  43.0 4.8 %collective-permute-start.18 = (bf16[416,128]{1,0:T(8,128)(2,1)S(1)}, bf16[416,128]{1,0:T(8,128)(2,1)S(1)}, u32[]{:S(2)}, u32[]{:S(2)}) collective-permute-start(bf16[416,128]{1,0:T(8,128)(2,1)S(1)} %add.38), channel_id=1, source_target_pairs={{0,2},{1,3},{2,0},{3,1},{4,6},{5,7},{6,4},{7,5},{8,10},{9,11},{10,... | collective-permute-start | bytes 319496 | tf_op jit(solution)/shard_map/ppermute | solution.py:314
  43.6 5.7 %collective-permute-start.12 = (bf16[416,128]{1,0:T(8,128)(2,1)S(1)}, bf16[416,128]{1,0:T(8,128)(2,1)S(1)}, u32[]{:S(2)}, u32[]{:S(2)}) collective-permute-start(bf16[416,128]{1,0:T(8,128)(2,1)S(1)} %add.33), channel_id=1, source_target_pairs={{0,4},{1,5},{2,6},{3,7},{4,0},{5,1},{6,2},{7,3},{8,12},{9,13},{10,... | collective-permute-start | bytes 319496 | tf_op jit(solution)/shard_map/ppermute | solution.py:314
  47.8 1.5 %collective-permute-start.19 = (bf16[416,128]{1,0:T(8,128)(2,1)S(1)}, bf16[416,128]{1,0:T(8,128)(2,1)S(1)}, u32[]{:S(2)}, u32[]{:S(2)}) collective-permute-start(bf16[416,128]{1,0:T(8,128)(2,1)S(1)} %add.39.mine_b), channel_id=1, source_target_pairs={{0,1},{1,0},{2,3},{3,2},{4,5},{5,4},{6,7},{7,6},{8,9},{9,8},{10,11... | collective-permute-start | bytes 319496 | tf_op jit(solution)/shard_map/ppermute | solution.py:314
  49.3 1.4 %collective-permute-start.13 = (bf16[416,128]{1,0:T(8,128)(2,1)S(1)}, bf16[416,128]{1,0:T(8,128)(2,1)S(1)}, u32[]{:S(2)}, u32[]{:S(2)}) collective-permute-start(bf16[416,128]{1,0:T(8,128)(2,1)S(1)} %add.34.mine_a), channel_id=1, source_target_pairs={{0,1},{1,0},{2,3},{3,2},{4,5},{5,4},{6,7},{7,6},{8,9},{9,8},{10,11... | collective-permute-start | bytes 319496 | tf_op jit(solution)/shard_map/ppermute | solution.py:314

commit v6 on v5

--- a/solution.py
+++ b/solution.py
@@ -136,11 +136,13 @@
     planes[64:576] = inner[...]
     odd_core = lax.axis_index("brick") & 1 == 1
     inner_x = lax.broadcasted_iota(jnp.int32, (64, 128), 1) >= 64
-    row = lax.broadcasted_iota(jnp.int32, (512, 512), 0)
-    before = jnp.concatenate([jnp.where(odd_core, beside[b], across[b]) for b in range(4)], axis=1)
-    after = jnp.concatenate([jnp.where(odd_core, across[b], beside[b]) for b in range(4)], axis=1)
-    before = mm(before, jnp.where(row == voxel_at() - 448, 1.0, 0.0).astype(BF16)).astype(BF16)
-    after = mm(after, jnp.where(row == voxel_at(), 1.0, 0.0).astype(BF16)).astype(BF16)
+    row = lax.broadcasted_iota(jnp.int32, (256, 512), 0)
+    voxel = voxel_at()
+    voxel = voxel - 64 * (voxel // 128)
+    before = jnp.where(odd_core, beside[...], across[...])
+    after = jnp.where(odd_core, across[...], beside[...])
+    before = mm(before, jnp.where(row == voxel - 256, 1.0, 0.0).astype(BF16)).astype(BF16)
+    after = mm(after, jnp.where(row == voxel, 1.0, 0.0).astype(BF16)).astype(BF16)
     for g in range(4):
         cut = slice(128 * g, 128 * g + 128)
         planes[0:64, cut] = pltpu.roll(jnp.where(inner_x, before[:, cut], inner[448:512, cut]), 64, 1)
@@ -329,7 +331,8 @@
     split = brick_size == 8
     feat = jnp.swapaxes(features[0], 1, 2)
     slots, own = owners[0], cotangent[0]
-    first, last = feat[0:4, :, 0:128], feat[4:8, :, 384:512]
+    first = jnp.concatenate([feat[b, :, 0:64] for b in range(4)], axis=1)
+    last = jnp.concatenate([feat[b, :, 448:512] for b in range(4, 8)], axis=1)
     beside = swap(jnp.where(core == 0, last, first), "brick", 1)
     chips = [(i, i + 1) for i in range(1, brick_size - 1, 2)]
     across = lax.ppermute(jnp.where(core == 0, first, last), "brick", chips + [(j, i) for i, j in chips])

time: 52 us -> 53.3 us (1.025)
  waiting for transfers between devices: 18.4 us -> 19.7 us
  local copies, waits for them, and re-layouts: 0.02 us -> 0.94 us
  other arithmetic: 1.18 us -> 0.4 us
    ppermute x19, waiting for transfers between devices: 18.4 us -> 19.7 us  [swap(): return lax.ppermute(value, axis, [(i, i ^ bit) for i in range(size)])]
    squeeze x0 -> x1, local copies, waits for them, and re-layouts: none -> 0.92 us  [shards(): last = jnp.concatenate([feat[b, :, 448:512] for b in range(4, 8)], axis=1)]
    select_n x1, other arithmetic: 0.89 us -> 0.11 us  [shards(): jnp.where(core == 0, first, last)]
  transfers between devices with their start and end apart: 20 -> 20, of which waited for: 12 -> 12; matrix products, arithmetic and copies ran while one was open for 2% -> 2% of each run, Pallas kernels for 14% -> 13%
where the time goes in v6:
time: 53.3 us; the launch traced here: 53.1 us
  starting transfers between devices  20.2 us (38%)
  waiting for transfers between devices  19.7 us (37%)
  Pallas kernels  11.1 us (21%)
  local copies, waits for them, and re-layouts  0.94 us (2%)
  between operations  0.83 us (2%)
    ppermute x19, waiting for transfers between devices, swap(): return lax.ppermute(value, axis, [(i, i ^ bit) for i in range(size)])  19.7 us
    ppermute x19, starting transfers between devices, swap(): return lax.ppermute(value, axis, [(i, i ^ bit) for i in range(size)])  19.6 us
    pallas_call x7, Pallas kernels, call(): pl.pallas_call(kernel, out_shape=outs, in_specs=specs or [VMEM] * len(ins...  11.1 us
  transfers between devices with their start and end apart: 20, of which 12 were waited for; matrix products, arithmetic and copies ran while one was open for 2% of the time, Pallas kernels for 13%

profile of v6, /device:TPU:0, one launch (start us, length us, event | category | flops | bytes accessed | tf_op | source)
XLA Modules:
  0.0 53.1 jit_solution(1483749964859565692)
XLA Ops:
  0.6 0.5 collective-permute-start.4
  1.1 2.7 %collective-permute-start = (bf16[8,64,256]{2,1,0:T(8,128)(2,1)}, bf16[8,64,256]{2,1,0:T(8,128)(2,1)S(1)}, u32[]{:S(2)}, u32[]{:S(2)}) collective-permute-start(bf16[8,64,256]{2,1,0:T(8,128)(2,1)} %bitcast.44), channel_id=1, source_target_pairs={{0,2},{1,3},{2,0},{3,1},{4,6},{5,7},{6,4},{7,5},{8,10},{9,11},{10,... | collective-permute-start | bytes 786440 | tf_op jit(solution)/shard_map/ppermute | solution.py:316
  3.8 2.6 %collective-permute-start.1 = (s32[1,8]{1,0:T(1,128)}, s32[1,8]{1,0:T(1,128)S(1)}, u32[]{:S(2)}, u32[]{:S(2)}) collective-permute-start(s32[1,8]{1,0:T(1,128)} %param.11), channel_id=1, source_target_pairs={{0,4},{1,5},{2,6},{3,7},{4,0},{5,1},{6,2},{7,3},{8,12},{9,13},{10,... | collective-permute-start | bytes 104 | tf_op jit(solution)/shard_map/ppermute | solution.py:316
  6.4 0.9 %slice_bitcast_fusion.11 = (bf16[64,64]{1,0:T(8,128)(2,1)S(1)}, bf16[64,64]{1,0:T(8,128)(2,1)S(1)}, bf16[64,64]{1,0:T(8,128)(2,1)S(1)}, bf16[64,64]{1,0:T(8,128)...) fusion(bf16[8,64,512]{2,1,0:T(8,128)(2,1)} %bitcast.39), kind=kLoop, calls=%fused_computation.17 | loop fusion | bytes 131072 | tf_op jit(solution)/shard_map/squeeze | solution.py:335
  7.3 0.1 broadcast_select_fusion
  7.4 0.7 %collective-permute-start.3 = (bf16[64,256]{1,0:T(8,128)(2,1)S(1)}, bf16[64,256]{1,0:T(8,128)(2,1)S(1)}, u32[]{:S(2)}, u32[]{:S(2)}) collective-permute-start(bf16[64,256]{1,0:T(8,128)(2,1)S(1)} %get-tuple-element.63), channel_id=1, source_target_pairs={{1,2},{3,4},{5,6},{2,1},{4,3},{6,5},{9,10},{11,12},{13,14},{10,9},... | collective-permute-start | bytes 98312 | tf_op jit(solution)/shard_map/ppermute | solution.py:338
  8.1 1.9 %collective-permute-start.2 = (bf16[64,256]{1,0:T(8,128)(2,1)S(1)}, bf16[64,256]{1,0:T(8,128)(2,1)S(1)}, u32[]{:S(2)}, u32[]{:S(2)}) collective-permute-start(bf16[64,256]{1,0:T(8,128)(2,1)S(1)} %get-tuple-element.64), channel_id=1, source_target_pairs={{0,1},{1,0},{2,3},{3,2},{4,5},{5,4},{6,7},{7,6},{8,9},{9,8},{10,11... | collective-permute-start | bytes 98312 | tf_op jit(solution)/shard_map/ppermute | solution.py:316
  10.0 2.8 %shard_map.103 = (bf16[512,512]{1,0:T(8,128)(2,1)S(1)}, f32[8,512]{1,0:T(8,128)S(1)}, f32[27,128]{1,0:T(8,128)S(1)}, bf16[256,3456]{1,0:T(8,128)(2,1)S(1)}, bf16...) custom-call(bf16[8,64,512]{2,1,0:T(8,128)(2,1)} %bitcast.40, ...), custom_call_target="tpu_custom_call" | custom-call | flops 4000000000 | bytes 1048576 | tf_op jit(solution)/shard_map/pallas_call | solution.py:299
  12.8 0.0 collective-permute-done.1.far_slots
  12.8 0.0 collective-permute-done.3.across
  12.8 0.0 collective-permute-done.2.beside
  12.8 0.0 collective-permute-done.across.even
  12.8 0.1 collective-permute-start.5
  12.9 0.0 collective-permute-done.4.beside.odd
  12.9 0.1 shard_map.106
  13.0 1.4 %collective-permute-start.6 = (bf16[2,64,256]{2,1,0:T(8,128)(2,1)S(1)}, bf16[2,64,256]{2,1,0:T(8,128)(2,1)S(1)}, u32[]{:S(2)}, u32[]{:S(2)}) collective-permute-start(bf16[2,64,256]{2,1,0:T(8,128)(2,1)S(1)} %shard_map.106), channel_id=1, source_target_pairs={{0,4},{1,5},{2,6},{3,7},{4,0},{5,1},{6,2},{7,3},{8,12},{9,13},{10,... | collective-permute-start | bytes 196616 | tf_op jit(solution)/shard_map/ppermute | solution.py:316
  14.4 0.0 collective-permute-done.5.diagonal.odd
  14.4 0.1 shard_map.107
  14.6 1.7 %collective-permute-start.7 = (bf16[2,64,256]{2,1,0:T(8,128)(2,1)S(1)}, bf16[2,64,256]{2,1,0:T(8,128)(2,1)S(1)}, u32[]{:S(2)}, u32[]{:S(2)}) collective-permute-start(bf16[2,64,256]{2,1,0:T(8,128)(2,1)S(1)} %shard_map.107), channel_id=1, source_target_pairs={{0,4},{1,5},{2,6},{3,7},{4,0},{5,1},{6,2},{7,3},{8,12},{9,13},{10,... | collective-permute-start | bytes 196616 | tf_op jit(solution)/shard_map/ppermute | solution.py:316
  16.2 3.4 %shard_map.104 = (bf16[4,640,512]{2,1,0:T(8,128)(2,1)S(1)}, f32[512,512]{1,0:T(8,128)S(1)}, bf16[512,512]{1,0:T(8,128)(2,1)S(1)}, bf16[128,512]{1,0:T(8,128)(2,1...) custom-call(bf16[512,512]{1,0:T(8,128)(2,1)S(1)} %get-tuple-element.28.inner, ...), custom_call_target="tpu_custom_call" | custom-call | flops 4000000000 | bytes 1048576 | tf_op jit(solution)/shard_map/pallas_call | solution.py:299
  19.7 0.6 %shard_map.105 = (bf16[8,64,256]{2,1,0:T(8,128)(2,1)S(1)}, s32[8,256]{1,0:T(8,128)S(1)}) custom-call(s32[8]{0:T(128)S(1)} %get-tuple-element.42.slots, bf16[8,64,256]{2,1,0:T(8,128)(2,1)S(1)} %get-tuple-element.43.own.even, bf16[8,64,256]{2,1,0:T(8,128)(2,1)S(1)} %collective-permute-done.4.beside.odd, ...), custom_call_target="tpu_custom_call" | custom-call | bytes 1048576 | tf_op jit(solution)/shard_map/pallas_call | solution.py:299
  20.3 1.4 %collective-permute-done.6.far = bf16[2,64,256]{2,1,0:T(8,128)(2,1)S(1)} collective-permute-done((bf16[2,64,256]{2,1,0:T(8,128)(2,1)S(1)}, bf16[2,64,256]{2,1,0:T(8,128)(2,1)S(1)}, u32[]{:S(2)}, u32[]{:S(2)}) %collective-permute-start.6) | collective-permute-done | bytes 65568 | tf_op jit(solution)/shard_map/ppermute | solution.py:316
  21.7 1.0 %collective-permute-done.7.far_pair = bf16[2,64,256]{2,1,0:T(8,128)(2,1)S(1)} collective-permute-done((bf16[2,64,256]{2,1,0:T(8,128)(2,1)S(1)}, bf16[2,64,256]{2,1,0:T(8,128)(2,1)S(1)}, u32[]{:S(2)}, u32[]{:S(2)}) %collective-permute-start.7) | collective-permute-done | bytes 65568 | tf_op jit(solution)/shard_map/ppermute | solution.py:316
  22.7 2.8 %shard_map.108 = bf16[2,2,416,128]{3,2,1,0:T(8,128)(2,1)S(1)} custom-call(bf16[4,640,512]{2,1,0:T(8,128)(2,1)S(1)} %get-tuple-element.36.shifted, f32[512,512]{1,0:T(8,128)S(1)} %get-tuple-element.37.slope_pre, bf16[512,512]{1,0:T(8,128)(2,1)S(1)} %get-tuple-element.38.hid, bf16[128,512]{1,0:T(8,128)(2,1)S(1)} %get-tuple-element.39.coarse, ...), custom_call_target="tpu_custom_call" | custom-call | flops 4000000000 | bytes 1048576 | tf_op jit(solution)/shard_map/pallas_call | solution.py:299
  25.6 0.1 collective-permute-start.14
  25.6 0.5 collective-permute-start.8
  26.1 0.8 %collective-permute-done.14 = bf16[416,128]{1,0:T(8,128)(2,1)S(1)} collective-permute-done((bf16[416,128]{1,0:T(8,128)(2,1)S(1)}, bf16[416,128]{1,0:T(8,128)(2,1)S(1)}, u32[]{:S(2)}, u32[]{:S(2)}) %collective-permute-start.14) | collective-permute-done | bytes 106528 | tf_op jit(solution)/shard_map/ppermute | solution.py:316
  26.9 0.2 collective-permute-done.8
  27.1 1.6 %collective-permute-start.15 = (bf16[416,128]{1,0:T(8,128)(2,1)S(1)}, bf16[416,128]{1,0:T(8,128)(2,1)S(1)}, u32[]{:S(2)}, u32[]{:S(2)}) collective-permute-start(bf16[416,128]{1,0:T(8,128)(2,1)S(1)} %get-tuple-element.59), channel_id=1, source_target_pairs={{0,8},{8,0},{16,24},{24,16},{1,9},{9,1},{17,25},{25,17},{2,10},{10... | collective-permute-start | bytes 319496 | tf_op jit(solution)/shard_map/ppermute | solution.py:316
  28.7 0.0 collective-permute-start.9
  28.7 3.7 %collective-permute-done.15 = bf16[416,128]{1,0:T(8,128)(2,1)S(1)} collective-permute-done((bf16[416,128]{1,0:T(8,128)(2,1)S(1)}, bf16[416,128]{1,0:T(8,128)(2,1)S(1)}, u32[]{:S(2)}, u32[]{:S(2)}) %collective-permute-start.15) | collective-permute-done | bytes 106528 | tf_op jit(solution)/shard_map/ppermute | solution.py:316
  32.5 1.6 %collective-permute-start.16 = (bf16[416,128]{1,0:T(8,128)(2,1)S(1)}, bf16[416,128]{1,0:T(8,128)(2,1)S(1)}, u32[]{:S(2)}, u32[]{:S(2)}) collective-permute-start(bf16[416,128]{1,0:T(8,128)(2,1)S(1)} %add.36), channel_id=1, source_target_pairs={{0,16},{8,24},{16,0},{24,8},{1,17},{9,25},{17,1},{25,9},{2,18},{10... | collective-permute-start | bytes 319496 | tf_op jit(solution)/shard_map/ppermute | solution.py:316
  34.1 0.0 collective-permute-done.9
  34.1 1.6 %collective-permute-start.10 = (bf16[416,128]{1,0:T(8,128)(2,1)S(1)}, bf16[416,128]{1,0:T(8,128)(2,1)S(1)}, u32[]{:S(2)}, u32[]{:S(2)}) collective-permute-start(bf16[416,128]{1,0:T(8,128)(2,1)S(1)} %add.31), channel_id=1, source_target_pairs={{0,8},{8,0},{16,24},{24,16},{1,9},{9,1},{17,25},{25,17},{2,10},{10... | collective-permute-start | bytes 319496 | tf_op jit(solution)/shard_map/ppermute | solution.py:316
  35.7 1.6 %collective-permute-done.16 = bf16[416,128]{1,0:T(8,128)(2,1)S(1)} collective-permute-done((bf16[416,128]{1,0:T(8,128)(2,1)S(1)}, bf16[416,128]{1,0:T(8,128)(2,1)S(1)}, u32[]{:S(2)}, u32[]{:S(2)}) %collective-permute-start.16) | collective-permute-done | bytes 106528 | tf_op jit(solution)/shard_map/ppermute | solution.py:316
  37.3 0.1 collective-permute-start.17
  37.4 1.5 %collective-permute-done.10 = bf16[416,128]{1,0:T(8,128)(2,1)S(1)} collective-permute-done((bf16[416,128]{1,0:T(8,128)(2,1)S(1)}, bf16[416,128]{1,0:T(8,128)(2,1)S(1)}, u32[]{:S(2)}, u32[]{:S(2)}) %collective-permute-start.10) | collective-permute-done | bytes 106528 | tf_op jit(solution)/shard_map/ppermute | solution.py:316
  38.9 1.2 %collective-permute-start.11 = (bf16[416,128]{1,0:T(8,128)(2,1)S(1)}, bf16[416,128]{1,0:T(8,128)(2,1)S(1)}, u32[]{:S(2)}, u32[]{:S(2)}) collective-permute-start(bf16[416,128]{1,0:T(8,128)(2,1)S(1)} %add.32), channel_id=1, source_target_pairs={{0,16},{8,24},{16,0},{24,8},{1,17},{9,25},{17,1},{25,9},{2,18},{10... | collective-permute-start | bytes 319496 | tf_op jit(solution)/shard_map/ppermute | solution.py:316
  40.1 2.9 %collective-permute-done.17 = bf16[416,128]{1,0:T(8,128)(2,1)S(1)} collective-permute-done((bf16[416,128]{1,0:T(8,128)(2,1)S(1)}, bf16[416,128]{1,0:T(8,128)(2,1)S(1)}, u32[]{:S(2)}, u32[]{:S(2)}) %collective-permute-start.17) | collective-permute-done | bytes 106528 | tf_op jit(solution)/shard_map/ppermute | solution.py:316
  43.0 0.1 collective-permute-start.18
  43.1 0.6 %collective-permute-done.11 = bf16[416,128]{1,0:T(8,128)(2,1)S(1)} collective-permute-done((bf16[416,128]{1,0:T(8,128)(2,1)S(1)}, bf16[416,128]{1,0:T(8,128)(2,1)S(1)}, u32[]{:S(2)}, u32[]{:S(2)}) %collective-permute-start.11) | collective-permute-done | bytes 106528 | tf_op jit(solution)/shard_map/ppermute | solution.py:316
  43.7 2.1 %collective-permute-start.12 = (bf16[416,128]{1,0:T(8,128)(2,1)S(1)}, bf16[416,128]{1,0:T(8,128)(2,1)S(1)}, u32[]{:S(2)}, u32[]{:S(2)}) collective-permute-start(bf16[416,128]{1,0:T(8,128)(2,1)S(1)} %add.33), channel_id=1, source_target_pairs={{0,4},{1,5},{2,6},{3,7},{4,0},{5,1},{6,2},{7,3},{8,12},{9,13},{10,... | collective-permute-start | bytes 319496 | tf_op jit(solution)/shard_map/ppermute | solution.py:316
  45.8 2.2 %collective-permute-done.18 = bf16[416,128]{1,0:T(8,128)(2,1)S(1)} collective-permute-done((bf16[416,128]{1,0:T(8,128)(2,1)S(1)}, bf16[416,128]{1,0:T(8,128)(2,1)S(1)}, u32[]{:S(2)}, u32[]{:S(2)}) %collective-permute-start.18) | collective-permute-done | bytes 106528 | tf_op jit(solution)/shard_map/ppermute | solution.py:316
  48.0 0.1 collective-permute-start.19
  48.1 2.5 %collective-permute-done.12 = bf16[416,128]{1,0:T(8,128)(2,1)S(1)} collective-permute-done((bf16[416,128]{1,0:T(8,128)(2,1)S(1)}, bf16[416,128]{1,0:T(8,128)(2,1)S(1)}, u32[]{:S(2)}, u32[]{:S(2)}) %collective-permute-start.12) | collective-permute-done | bytes 106528 | tf_op jit(solution)/shard_map/ppermute | solution.py:316
  50.6 0.1 collective-permute-start.13
  50.6 0.0 collective-permute-done.19.other_b
  50.6 1.3 %collective-permute-done.13.other_a = bf16[416,128]{1,0:T(8,128)(2,1)S(1)} collective-permute-done((bf16[416,128]{1,0:T(8,128)(2,1)S(1)}, bf16[416,128]{1,0:T(8,128)(2,1)S(1)}, u32[]{:S(2)}, u32[]{:S(2)}) %collective-permute-start.13) | collective-permute-done | bytes 106528 | tf_op jit(solution)/shard_map/ppermute | solution.py:316
  51.9 1.2 %shard_map.109 = (f32[27,64,64]{2,1,0:T(8,128)}, f32[8,64,128]{2,1,0:T(8,128)}, f32[128,256]{1,0:T(8,128)}) custom-call(bf16[416,128]{1,0:T(8,128)(2,1)S(1)} %add.34.mine_a, bf16[416,128]{1,0:T(8,128)(2,1)S(1)} %collective-permute-done.13.other_a, bf16[416,128]{1,0:T(8,128)(2,1)S(1)} %add.39.mine_b, bf16[416,128]{1,0:T(8,128)(2,1)S(1)} %collective-permute-done.19.other_b), custom_call_target="tpu_custom_call" | custom-call | bytes 1048576 | tf_op jit(solution)/shard_map/pallas_call | solution.py:299
  (10 shorter events, 0.3 us)
Async XLA Ops:
  0.6 12.3 %collective-permute-start.4 = (bf16[8,64,256]{2,1,0:T(8,128)(2,1)}, bf16[8,64,256]{2,1,0:T(8,128)(2,1)S(1)}, u32[]{:S(2)}, u32[]{:S(2)}) collective-permute-start(bf16[8,64,256]{2,1,0:T(8,128)(2,1)} %bitcast.43), channel_id=1, source_target_pairs={{0,1},{1,0},{2,3},{3,2},{4,5},{5,4},{6,7},{7,6},{8,9},{9,8},{10,11... | collective-permute-start | bytes 786440 | tf_op jit(solution)/shard_map/ppermute | solution.py:316
  1.1 11.7 %collective-permute-start = (bf16[8,64,256]{2,1,0:T(8,128)(2,1)}, bf16[8,64,256]{2,1,0:T(8,128)(2,1)S(1)}, u32[]{:S(2)}, u32[]{:S(2)}) collective-permute-start(bf16[8,64,256]{2,1,0:T(8,128)(2,1)} %bitcast.44), channel_id=1, source_target_pairs={{0,2},{1,3},{2,0},{3,1},{4,6},{5,7},{6,4},{7,5},{8,10},{9,11},{10,... | collective-permute-start | bytes 786440 | tf_op jit(solution)/shard_map/ppermute | solution.py:316
  3.8 9.0 %collective-permute-start.1 = (s32[1,8]{1,0:T(1,128)}, s32[1,8]{1,0:T(1,128)S(1)}, u32[]{:S(2)}, u32[]{:S(2)}) collective-permute-start(s32[1,8]{1,0:T(1,128)} %param.11), channel_id=1, source_target_pairs={{0,4},{1,5},{2,6},{3,7},{4,0},{5,1},{6,2},{7,3},{8,12},{9,13},{10,... | collective-permute-start | bytes 104 | tf_op jit(solution)/shard_map/ppermute | solution.py:316
  7.4 5.3 %collective-permute-start.3 = (bf16[64,256]{1,0:T(8,128)(2,1)S(1)}, bf16[64,256]{1,0:T(8,128)(2,1)S(1)}, u32[]{:S(2)}, u32[]{:S(2)}) collective-permute-start(bf16[64,256]{1,0:T(8,128)(2,1)S(1)} %get-tuple-element.63), channel_id=1, source_target_pairs={{1,2},{3,4},{5,6},{2,1},{4,3},{6,5},{9,10},{11,12},{13,14},{10,9},... | collective-permute-start | bytes 98312 | tf_op jit(solution)/shard_map/ppermute | solution.py:338
  8.1 4.7 %collective-permute-start.2 = (bf16[64,256]{1,0:T(8,128)(2,1)S(1)}, bf16[64,256]{1,0:T(8,128)(2,1)S(1)}, u32[]{:S(2)}, u32[]{:S(2)}) collective-permute-start(bf16[64,256]{1,0:T(8,128)(2,1)S(1)} %get-tuple-element.64), channel_id=1, source_target_pairs={{0,1},{1,0},{2,3},{3,2},{4,5},{5,4},{6,7},{7,6},{8,9},{9,8},{10,11... | collective-permute-start | bytes 98312 | tf_op jit(solution)/shard_map/ppermute | solution.py:316
  12.8 1.6 %collective-permute-start.5 = (bf16[8,64,256]{2,1,0:T(8,128)(2,1)S(1)}, bf16[8,64,256]{2,1,0:T(8,128)(2,1)S(1)}, u32[]{:S(2)}, u32[]{:S(2)}) collective-permute-start(bf16[8,64,256]{2,1,0:T(8,128)(2,1)S(1)} %collective-permute-done.across.even), channel_id=1, source_target_pairs={{0,1},{1,0},{2,3},{3,2},{4,5},{5,4},{6,7},{7,6},{8,9},{9,8},{10,11... | collective-permute-start | bytes 786440 | tf_op jit(solution)/shard_map/ppermute | solution.py:316
  13.0 8.6 %collective-permute-start.6 = (bf16[2,64,256]{2,1,0:T(8,128)(2,1)S(1)}, bf16[2,64,256]{2,1,0:T(8,128)(2,1)S(1)}, u32[]{:S(2)}, u32[]{:S(2)}) collective-permute-start(bf16[2,64,256]{2,1,0:T(8,128)(2,1)S(1)} %shard_map.106), channel_id=1, source_target_pairs={{0,4},{1,5},{2,6},{3,7},{4,0},{5,1},{6,2},{7,3},{8,12},{9,13},{10,... | collective-permute-start | bytes 196616 | tf_op jit(solution)/shard_map/ppermute | solution.py:316
  14.6 8.1 %collective-permute-start.7 = (bf16[2,64,256]{2,1,0:T(8,128)(2,1)S(1)}, bf16[2,64,256]{2,1,0:T(8,128)(2,1)S(1)}, u32[]{:S(2)}, u32[]{:S(2)}) collective-permute-start(bf16[2,64,256]{2,1,0:T(8,128)(2,1)S(1)} %shard_map.107), channel_id=1, source_target_pairs={{0,4},{1,5},{2,6},{3,7},{4,0},{5,1},{6,2},{7,3},{8,12},{9,13},{10,... | collective-permute-start | bytes 196616 | tf_op jit(solution)/shard_map/ppermute | solution.py:316
  25.6 1.4 %collective-permute-start.14 = (bf16[416,128]{1,0:T(8,128)(2,1)S(1)}, bf16[416,128]{1,0:T(8,128)(2,1)S(1)}, u32[]{:S(2)}, u32[]{:S(2)}) collective-permute-start(bf16[416,128]{1,0:T(8,128)(2,1)S(1)} %get-tuple-element.61), channel_id=1, source_target_pairs={{0,1},{1,0},{2,3},{3,2},{4,5},{5,4},{6,7},{7,6},{8,9},{9,8},{10,11... | collective-permute-start | bytes 319496 | tf_op jit(solution)/shard_map/ppermute | solution.py:316
  25.6 1.5 %collective-permute-start.8 = (bf16[416,128]{1,0:T(8,128)(2,1)S(1)}, bf16[416,128]{1,0:T(8,128)(2,1)S(1)}, u32[]{:S(2)}, u32[]{:S(2)}) collective-permute-start(bf16[416,128]{1,0:T(8,128)(2,1)S(1)} %get-tuple-element.62), channel_id=1, source_target_pairs={{0,1},{1,0},{2,3},{3,2},{4,5},{5,4},{6,7},{7,6},{8,9},{9,8},{10,11... | collective-permute-start | bytes 319496 | tf_op jit(solution)/shard_map/ppermute | solution.py:316
  27.1 5.3 %collective-permute-start.15 = (bf16[416,128]{1,0:T(8,128)(2,1)S(1)}, bf16[416,128]{1,0:T(8,128)(2,1)S(1)}, u32[]{:S(2)}, u32[]{:S(2)}) collective-permute-start(bf16[416,128]{1,0:T(8,128)(2,1)S(1)} %get-tuple-element.59), channel_id=1, source_target_pairs={{0,8},{8,0},{16,24},{24,16},{1,9},{9,1},{17,25},{25,17},{2,10},{10... | collective-permute-start | bytes 319496 | tf_op jit(solution)/shard_map/ppermute | solution.py:316
  28.7 5.4 %collective-permute-start.9 = (bf16[416,128]{1,0:T(8,128)(2,1)S(1)}, bf16[416,128]{1,0:T(8,128)(2,1)S(1)}, u32[]{:S(2)}, u32[]{:S(2)}) collective-permute-start(bf16[416,128]{1,0:T(8,128)(2,1)S(1)} %get-tuple-element.60), channel_id=1, source_target_pairs={{0,2},{1,3},{2,0},{3,1},{4,6},{5,7},{6,4},{7,5},{8,10},{9,11},{10,... | collective-permute-start | bytes 319496 | tf_op jit(solution)/shard_map/ppermute | solution.py:316
  32.5 4.8 %collective-permute-start.16 = (bf16[416,128]{1,0:T(8,128)(2,1)S(1)}, bf16[416,128]{1,0:T(8,128)(2,1)S(1)}, u32[]{:S(2)}, u32[]{:S(2)}) collective-permute-start(bf16[416,128]{1,0:T(8,128)(2,1)S(1)} %add.36), channel_id=1, source_target_pairs={{0,16},{8,24},{16,0},{24,8},{1,17},{9,25},{17,1},{25,9},{2,18},{10... | collective-permute-start | bytes 319496 | tf_op jit(solution)/shard_map/ppermute | solution.py:316
  34.1 4.8 %collective-permute-start.10 = (bf16[416,128]{1,0:T(8,128)(2,1)S(1)}, bf16[416,128]{1,0:T(8,128)(2,1)S(1)}, u32[]{:S(2)}, u32[]{:S(2)}) collective-permute-start(bf16[416,128]{1,0:T(8,128)(2,1)S(1)} %add.31), channel_id=1, source_target_pairs={{0,8},{8,0},{16,24},{24,16},{1,9},{9,1},{17,25},{25,17},{2,10},{10... | collective-permute-start | bytes 319496 | tf_op jit(solution)/shard_map/ppermute | solution.py:316
  37.3 5.7 %collective-permute-start.17 = (bf16[416,128]{1,0:T(8,128)(2,1)S(1)}, bf16[416,128]{1,0:T(8,128)(2,1)S(1)}, u32[]{:S(2)}, u32[]{:S(2)}) collective-permute-start(bf16[416,128]{1,0:T(8,128)(2,1)S(1)} %add.37), channel_id=1, source_target_pairs={{0,4},{1,5},{2,6},{3,7},{4,0},{5,1},{6,2},{7,3},{8,12},{9,13},{10,... | collective-permute-start | bytes 319496 | tf_op jit(solution)/shard_map/ppermute | solution.py:316
  38.9 4.8 %collective-permute-start.11 = (bf16[416,128]{1,0:T(8,128)(2,1)S(1)}, bf16[416,128]{1,0:T(8,128)(2,1)S(1)}, u32[]{:S(2)}, u32[]{:S(2)}) collective-permute-start(bf16[416,128]{1,0:T(8,128)(2,1)S(1)} %add.32), channel_id=1, source_target_pairs={{0,16},{8,24},{16,0},{24,8},{1,17},{9,25},{17,1},{25,9},{2,18},{10... | collective-permute-start | bytes 319496 | tf_op jit(solution)/shard_map/ppermute | solution.py:316
  43.0 5.0 %collective-permute-start.18 = (bf16[416,128]{1,0:T(8,128)(2,1)S(1)}, bf16[416,128]{1,0:T(8,128)(2,1)S(1)}, u32[]{:S(2)}, u32[]{:S(2)}) collective-permute-start(bf16[416,128]{1,0:T(8,128)(2,1)S(1)} %add.38), channel_id=1, source_target_pairs={{0,2},{1,3},{2,0},{3,1},{4,6},{5,7},{6,4},{7,5},{8,10},{9,11},{10,... | collective-permute-start | bytes 319496 | tf_op jit(solution)/shard_map/ppermute | solution.py:316
  43.7 6.8 %collective-permute-start.12 = (bf16[416,128]{1,0:T(8,128)(2,1)S(1)}, bf16[416,128]{1,0:T(8,128)(2,1)S(1)}, u32[]{:S(2)}, u32[]{:S(2)}) collective-permute-start(bf16[416,128]{1,0:T(8,128)(2,1)S(1)} %add.33), channel_id=1, source_target_pairs={{0,4},{1,5},{2,6},{3,7},{4,0},{5,1},{6,2},{7,3},{8,12},{9,13},{10,... | collective-permute-start | bytes 319496 | tf_op jit(solution)/shard_map/ppermute | solution.py:316
  48.0 2.7 %collective-permute-start.19 = (bf16[416,128]{1,0:T(8,128)(2,1)S(1)}, bf16[416,128]{1,0:T(8,128)(2,1)S(1)}, u32[]{:S(2)}, u32[]{:S(2)}) collective-permute-start(bf16[416,128]{1,0:T(8,128)(2,1)S(1)} %add.39.mine_b), channel_id=1, source_target_pairs={{0,1},{1,0},{2,3},{3,2},{4,5},{5,4},{6,7},{7,6},{8,9},{9,8},{10,11... | collective-permute-start | bytes 319496 | tf_op jit(solution)/shard_map/ppermute | solution.py:316
  50.6 1.4 %collective-permute-start.13 = (bf16[416,128]{1,0:T(8,128)(2,1)S(1)}, bf16[416,128]{1,0:T(8,128)(2,1)S(1)}, u32[]{:S(2)}, u32[]{:S(2)}) collective-permute-start(bf16[416,128]{1,0:T(8,128)(2,1)S(1)} %add.34.mine_a), channel_id=1, source_target_pairs={{0,1},{1,0},{2,3},{3,2},{4,5},{5,4},{6,7},{7,6},{8,9},{9,8},{10,11... | collective-permute-start | bytes 319496 | tf_op jit(solution)/shard_map/ppermute | solution.py:316
